TPU v7x, 32 devices: a whole 2x2x4 slice. The times are simulated.
32 devices in a mesh: row: 4 (over y, x), col: 8 (over z, core).
Axes of the slice: x: 2, y: 2, z: 4, core: 2. Of those that a mesh axis runs over, the one named last changes fastest.
Arguments:
- matrix: float32 [4096, 4096], P('row', 'col'), may hold values from 0 to 9.5, as said below
Outputs:
- factored: float32 [4096, 4096], P('row', 'col')
Inputs may be any that keep to these rules, and one draw needn't show every extreme that they name: `matrix`: symmetric positive definite once the block order is reverted.
All inputs are finite; a program needn't handle non-finite values.
Results may differ from a plain program's by a relative error of at most 0.0003.
Values sent between devices are 32-bit elements; how exact they have to be, the bound alone decides.
No kernel may reach another device: no remote copies, remote signals or barrier semaphores. Data moves between devices by JAX's collectives and lax.ppermute only.
A program may use at most 128 MiB of HBM per device.

v0:
```python
import jax
import jax.numpy as jnp
from jax import lax
from jax.sharding import PartitionSpec as P

NB = 256
PANELS = 3


def from_root(shard, axis, root):
    mine = lax.axis_index(axis) == root
    return lax.psum(jnp.where(mine, shard, jnp.zeros_like(shard)), axis)


def solve_panel(factor, raw_rows):
    slots = raw_rows.shape[0]
    width = raw_rows.shape[1]
    flat = raw_rows.reshape(slots * width, width)
    solved = jax.scipy.linalg.solve_triangular(factor, flat.T, lower=True).T
    return solved.reshape(slots, width, width)


def subtract(part, panel_rows, column_rows):
    return part - jnp.einsum(
        "lan,mbn->lamb",
        panel_rows,
        column_rows,
        precision=lax.Precision.HIGHEST,
        preferred_element_type=jnp.float32,
    )


def body(matrix):
    grid_rows = lax.axis_size("row")
    grid_cols = lax.axis_size("col")
    row_slots = matrix.shape[0] // NB
    col_slots = matrix.shape[1] // NB
    stride = grid_cols // grid_rows
    my_row = lax.axis_index("row")
    my_col = lax.axis_index("col")
    blocks = matrix.reshape(row_slots, NB, col_slots, NB)
    row_ids = jnp.arange(row_slots, dtype=jnp.int32) * grid_rows + my_row
    col_ids = jnp.arange(col_slots, dtype=jnp.int32) * grid_cols + my_col
    carried = None
    for panel_at in range(PANELS):
        root_row = panel_at % grid_rows
        root_col = panel_at % grid_cols
        slot_row = panel_at // grid_rows
        slot_col = panel_at // grid_cols
        source = blocks[:, :, slot_col, :]
        below_mask = (row_ids > panel_at)[:, None, None]
        diag_block = from_root(source[slot_row], "row", root_row)
        factor = jnp.linalg.cholesky(diag_block)
        solved = jnp.where(below_mask, solve_panel(factor, source), 0.0)
        panel_rows = from_root(solved, "col", root_col)
        fetched = from_root(panel_rows, "row", my_col % grid_rows)
        column_rows = lax.dynamic_index_in_dim(
            fetched.reshape(col_slots, stride, NB, NB), my_col // grid_rows, 1, keepdims=False
        )
        owner_column = jnp.where((row_ids == panel_at)[:, None, None], factor[None], panel_rows)
        blocks = blocks.at[:, :, slot_col, :].set(
            jnp.where(my_col == root_col, owner_column, source)
        )
        blocks = subtract(blocks, panel_rows, column_rows)
        carried = None
    zero_mask = (row_ids[:, None] < col_ids[None, :]) & (row_ids[:, None] < PANELS)
    result = jnp.where(zero_mask[:, None, :, None], 0.0, blocks)
    return result.reshape(matrix.shape)


def solution(mesh):
    in_specs = (P("row", "col"),)
    out_specs = P("row", "col")
    return jax.shard_map(body, mesh=mesh, in_specs=in_specs, out_specs=out_specs, check_vma=False)
```

profile of v0, /device:TPU:0, one launch (start us, length us, event | category | flops | bytes accessed | tf_op | source)
XLA Modules:
  0.0 724.4 jit_solution(14478699010018959360)
XLA Ops:
  14.0 44.9 %all-reduce.11.cloned.1.call-done = f32[256,256]{0,1:T(8,128)} async-done(((f32[256,256]{0,1:T(8,128)}), f32[256,256]{0,1:T(8,128)}) %all-reduce.11.cloned.1.call-update) | async-done | bytes 262160 | tf_op jit(solution)/shard_map/psum | solution.py:12
  61.0 11.7 %cholesky.172 = f32[128,128]{1,0:T(8,128)S(1)} custom-call(f32[128,128]{1,0:T(8,128)S(1)} %cholesky.270), custom_call_target="Cholesky" | custom-call | tf_op jit(solution)/shard_map/jit(cholesky)/cholesky | solution.py:53
  72.8 9.8 %custom-call.15 = f32[1,128,128]{1,2,0:T(8,128)S(1)} custom-call(f32[1,128,128]{2,1,0:T(8,128)S(1)} %get-tuple-element.117), custom_call_target="InvertDiagBlocksLowerTriangular" | custom-call | tf_op jit(solution)/shard_map/jit(cholesky)/cholesky | solution.py:53
  83.1 11.7 %cholesky.189 = f32[128,128]{1,0:T(8,128)S(1)} custom-call(f32[128,128]{1,0:T(8,128)S(1)} %convolution_subtract_fusion.7), custom_call_target="Cholesky" | custom-call | tf_op jit(solution)/shard_map/jit(cholesky)/cholesky | solution.py:53
  96.9 4.3 while.9
  101.2 19.7 %custom-call.16 = f32[2,128,128]{1,2,0:T(8,128)S(1)} custom-call(f32[2,128,128]{2,1,0:T(8,128)S(1)} %get-tuple-element.63), custom_call_target="InvertDiagBlocksLowerTriangular" | custom-call | tf_op jit(solution)/shard_map/jit(_solve_triangular)/triangular_solve | solution.py:19
  125.3 58.9 %all-reduce.13.cloned.1.call-done = f32[4,256,256]{1,2,0:T(8,128)} async-done(((f32[4,256,256]{1,2,0:T(8,128)}), f32[4,256,256]{1,2,0:T(8,128)}) %all-reduce.13.cloned.1.call-update) | async-done | bytes 1048592 | tf_op jit(solution)/shard_map/psum | solution.py:12
  191.8 47.4 %all-reduce.15.cloned.1.call-done = f32[2,2,256,256]{2,3,1,0:T(8,128)} async-done(((f32[2,2,256,256]{2,3,1,0:T(8,128)}), f32[2,2,256,256]{2,3,1,0:T(8,128)}) %all-reduce.15.cloned.1.call-update) | async-done | bytes 1048592 | tf_op jit(solution)/shard_map/psum | solution.py:12
  246.8 40.1 %all-reduce.17.cloned.1.call-done = f32[256,256]{0,1:T(8,128)} async-done(((f32[256,256]{0,1:T(8,128)}), f32[256,256]{0,1:T(8,128)}) %all-reduce.17.cloned.1.call-update) | async-done | bytes 262160 | tf_op jit(solution)/shard_map/psum | solution.py:12
  289.7 11.7 %cholesky.206 = f32[128,128]{1,0:T(8,128)S(1)} custom-call(f32[128,128]{1,0:T(8,128)S(1)} %cholesky.273), custom_call_target="Cholesky" | custom-call | tf_op jit(solution)/shard_map/jit(cholesky)/cholesky | solution.py:53
  301.5 9.8 %custom-call.17 = f32[1,128,128]{1,2,0:T(8,128)S(1)} custom-call(f32[1,128,128]{2,1,0:T(8,128)S(1)} %get-tuple-element.113), custom_call_target="InvertDiagBlocksLowerTriangular" | custom-call | tf_op jit(solution)/shard_map/jit(cholesky)/cholesky | solution.py:53
  313.5 11.7 %cholesky.223 = f32[128,128]{1,0:T(8,128)S(1)} custom-call(f32[128,128]{1,0:T(8,128)S(1)} %convolution_subtract_fusion.6), custom_call_target="Cholesky" | custom-call | tf_op jit(solution)/shard_map/jit(cholesky)/cholesky | solution.py:53
  333.4 20.5 %custom-call.18 = f32[2,128,128]{1,2,0:T(8,128)S(1)} custom-call(f32[2,128,128]{2,1,0:T(8,128)} %copy-done.12), custom_call_target="InvertDiagBlocksLowerTriangular" | custom-call | tf_op jit(solution)/shard_map/jit(_solve_triangular)/triangular_solve | solution.py:19
  360.4 58.9 %all-reduce.19.cloned.1.call-done = f32[4,256,256]{1,2,0:T(8,128)} async-done(((f32[4,256,256]{1,2,0:T(8,128)}), f32[4,256,256]{1,2,0:T(8,128)}) %all-reduce.19.cloned.1.call-update) | async-done | bytes 1048592 | tf_op jit(solution)/shard_map/psum | solution.py:12
  425.7 48.1 %all-reduce.21.cloned.1.call-done = f32[2,2,256,256]{2,3,1,0:T(8,128)} async-done(((f32[2,2,256,256]{2,3,1,0:T(8,128)}), f32[2,2,256,256]{2,3,1,0:T(8,128)}) %all-reduce.21.cloned.1.call-update) | async-done | bytes 1048592 | tf_op jit(solution)/shard_map/psum | solution.py:12
  481.0 40.3 %all-reduce.23.cloned.1.call-done = f32[256,256]{0,1:T(8,128)} async-done(((f32[256,256]{0,1:T(8,128)}), f32[256,256]{0,1:T(8,128)}) %all-reduce.23.cloned.1.call-update) | async-done | bytes 262160 | tf_op jit(solution)/shard_map/psum | solution.py:12
  524.1 11.7 %cholesky.240 = f32[128,128]{1,0:T(8,128)S(1)} custom-call(f32[128,128]{1,0:T(8,128)S(1)} %cholesky.276), custom_call_target="Cholesky" | custom-call | tf_op jit(solution)/shard_map/jit(cholesky)/cholesky | solution.py:53
  535.9 9.8 %custom-call.19 = f32[1,128,128]{1,2,0:T(8,128)S(1)} custom-call(f32[1,128,128]{2,1,0:T(8,128)S(1)} %get-tuple-element.109), custom_call_target="InvertDiagBlocksLowerTriangular" | custom-call | tf_op jit(solution)/shard_map/jit(cholesky)/cholesky | solution.py:53
  547.9 11.7 %cholesky.257 = f32[128,128]{1,0:T(8,128)S(1)} custom-call(f32[128,128]{1,0:T(8,128)S(1)} %convolution_subtract_fusion.5), custom_call_target="Cholesky" | custom-call | tf_op jit(solution)/shard_map/jit(cholesky)/cholesky | solution.py:53
  563.0 4.2 while.11
  567.8 20.5 %custom-call.20 = f32[2,128,128]{1,2,0:T(8,128)S(1)} custom-call(f32[2,128,128]{2,1,0:T(8,128)} %copy-done.11), custom_call_target="InvertDiagBlocksLowerTriangular" | custom-call | tf_op jit(solution)/shard_map/jit(_solve_triangular)/triangular_solve | solution.py:19
  594.9 58.9 %all-reduce.25.cloned.1.call-done = f32[4,256,256]{1,2,0:T(8,128)} async-done(((f32[4,256,256]{1,2,0:T(8,128)}), f32[4,256,256]{1,2,0:T(8,128)}) %all-reduce.25.cloned.1.call-update) | async-done | bytes 1048592 | tf_op jit(solution)/shard_map/psum | solution.py:12
  658.9 49.8 %all-reduce.27.cloned.1.call-done = f32[2,2,256,256]{2,3,1,0:T(8,128)} async-done(((f32[2,2,256,256]{2,3,1,0:T(8,128)}), f32[2,2,256,256]{2,3,1,0:T(8,128)}) %all-reduce.27.cloned.1.call-update) | async-done | bytes 1048592 | tf_op jit(solution)/shard_map/psum | solution.py:12
  708.7 4.3 subtract_select_fusion
  (155 shorter events, 97.6 us)
Async XLA Ops:
  6.5 52.4 %all-reduce.11.cloned.1.call-start = ((), (), s32[]{:S(2)}) async-start(), calls=%async_computation | async-start | bytes 524288 | tf_op jit(solution)/shard_map/psum | solution.py:12
  13.1 171.1 %all-reduce.13.cloned.1.call-start = ((), (), s32[]{:S(2)}) async-start(), calls=%async_computation.1 | async-start | bytes 2097152 | tf_op jit(solution)/shard_map/psum | solution.py:12
  125.2 113.9 %all-reduce.15.cloned.1.call-start = ((), (), s32[]{:S(2)}) async-start(), calls=%async_computation.2 | async-start | bytes 2097152 | tf_op jit(solution)/shard_map/psum | solution.py:12
  186.5 2.1 copy-start.1
  186.6 100.4 %all-reduce.17.cloned.1.call-start = ((), (), s32[]{:S(2)}) async-start(), calls=%async_computation.3 | async-start | bytes 524288 | tf_op jit(solution)/shard_map/psum | solution.py:12
  190.4 1.3 copy-start.2
  243.9 175.5 %all-reduce.19.cloned.1.call-start = ((), (), s32[]{:S(2)}) async-start(), calls=%async_computation.4 | async-start | bytes 2097152 | tf_op jit(solution)/shard_map/psum | solution.py:12
  246.8 107.0 %copy-start.6 = (f32[4,256,1,256]{3,1,0,2:T(8,128)S(1)}, f32[4,256,1,256]{3,1,0,2:T(8,128)}, u32[]{:S(2)}) copy-start(f32[4,256,1,256]{3,1,0,2:T(8,128)} %copy.37) | copy-start | bytes 3145732
  289.0 0.7 copy-start.9
  325.2 2.6 copy-start.7
  332.7 0.6 copy-start.12
  360.4 113.4 %all-reduce.21.cloned.1.call-start = ((), (), s32[]{:S(2)}) async-start(), calls=%async_computation.5 | async-start | bytes 2097152 | tf_op jit(solution)/shard_map/psum | solution.py:12
  419.4 3.6 copy-start.4
  421.8 99.6 %all-reduce.23.cloned.1.call-start = ((), (), s32[]{:S(2)}) async-start(), calls=%async_computation.6 | async-start | bytes 524288 | tf_op jit(solution)/shard_map/psum | solution.py:12
  424.4 1.3 copy-start
  478.2 175.6 %all-reduce.25.cloned.1.call-start = ((), (), s32[]{:S(2)}) async-start(), calls=%async_computation.7 | async-start | bytes 2097152 | tf_op jit(solution)/shard_map/psum | solution.py:12
  481.0 107.3 %copy-start.5 = (f32[4,256,1,256]{3,1,0,2:T(8,128)S(1)}, f32[4,256,1,256]{3,1,0,2:T(8,128)}, u32[]{:S(2)}) copy-start(f32[4,256,1,256]{3,1,0,2:T(8,128)} %copy.47) | copy-start | bytes 3145732
  523.4 0.7 copy-start.10
  559.6 2.6 copy-start.8
  567.2 0.6 copy-start.11
  594.9 113.9 %all-reduce.27.cloned.1.call-start = ((), (), s32[]{:S(2)}) async-start(), calls=%async_computation.8 | async-start | bytes 2097152 | tf_op jit(solution)/shard_map/psum | solution.py:12
  653.8 3.6 copy-start.3
Sparse Core Ops, SparseCore 0:
  13.2 45.6 all-reduce.10
  125.4 58.8 all-reduce.12
  187.6 51.5 all-reduce.14
  244.0 42.8 all-reduce.16
  360.5 58.7 all-reduce.18
  422.3 51.4 all-reduce.20
  478.4 42.9 all-reduce.22
  595.0 58.7 all-reduce.24
  657.2 51.5 all-reduce.26
where the time goes:
time: 734 us; the launch traced here: 724 us
  waiting for transfers between devices  448 us (61%)
  other arithmetic  187 us (25%)
  local copies, waits for them, and re-layouts  46.1 us (6%)
  matrix products  23.5 us (3%)
  between operations  18 us (2%)
    psum x9, waiting for transfers between devices, from_root(): return lax.psum(jnp.where(mine, shard, jnp.zeros_like(shard)), axis)  447 us
    another operation x20, other arithmetic, body(): factor = jnp.linalg.cholesky(diag_block)  103 us
    another operation x7, other arithmetic, solve_panel(): solved = jax.scipy.linalg.solve_triangular(factor, flat.T, lower=True).T  62.2 us
  transfers between devices with their start and end apart: 9, of which 9 were waited for; matrix products, arithmetic and copies ran while one was open for 2% of the time, Pallas kernels for 0%

commit v1 on v0

v1 whole, which is shorter than its diff:
```python
import functools

import jax
import jax.numpy as jnp
from jax import lax
from jax.experimental import pallas as pl
from jax.experimental.pallas import tpu as pltpu
from jax.sharding import PartitionSpec as P

NB = 256
PANELS = 3
HALF = 128
TILE = 8
HEAD = PANELS * NB
VMEM = 56 * 1024 * 1024

CARRIED = (((0, 0), 0), ((0, 1), 1), ((1, 2), 0), ((1, 1), 1), ((2, 0), 0), ((2, 2), 1))


def sublane(x, k):
    return jnp.broadcast_to(x[k : k + 1, :], x.shape)


def lane(x, k):
    return jnp.broadcast_to(x[:, k : k + 1], x.shape)


def dot_nt(a, b):
    return lax.dot_general(
        a, b, (((1,), (1,)), ((), ())), precision=lax.Precision.HIGHEST, preferred_element_type=jnp.float32
    )


def dot_nn(a, b):
    return jnp.dot(a, b, precision=lax.Precision.HIGHEST, preferred_element_type=jnp.float32)


def invert_factor(tiles):
    count = len(tiles)
    rows = lax.broadcasted_iota(jnp.int32, (TILE, HALF), 0)
    lanes = lax.broadcasted_iota(jnp.int32, (TILE, HALF), 1)
    out = []
    for step in range(count):
        start = TILE * step
        own = (lanes >= start) & (lanes < start + TILE)
        pivot_rows = tiles[step]
        column = [lane(pivot_rows, start + k) for k in range(TILE)]
        pivot_rows = jnp.where(own, jnp.where(lanes - start == rows, 1.0, 0.0), pivot_rows)
        upper, inverse, pivot_row, pivots = {}, [], [], None
        for k in range(TILE):
            pivot = sublane(column[k], k)
            inverse.append(pl.reciprocal(pivot, approx=False))
            pivots = pivot if pivots is None else jnp.where(rows == k, pivot, pivots)
            pivot_row.append(sublane(pivot_rows, k))
            if k < TILE - 1:
                multiplier = jnp.where(rows > k, column[k], 0.0) * inverse[k]
                for j in range(k + 1, TILE):
                    upper[k, j] = sublane(column[j], k)
                    column[j] = column[j] - multiplier * upper[k, j]
                pivot_rows = pivot_rows - multiplier * pivot_row[k]
        out.append(pivot_rows * lax.rsqrt(pivots))
        for t in range(step + 1, count):
            tile = tiles[t]
            ahead = [lane(tile, start + k) for k in range(TILE)]
            tile = jnp.where(own, 0.0, tile)
            for k in range(TILE):
                multiplier = ahead[k] * inverse[k]
                for j in range(k + 1, TILE):
                    ahead[j] = ahead[j] - multiplier * upper[k, j]
                tile = tile - multiplier * pivot_row[k]
            tiles[t] = tile
    return out


def head_kernel(core_ref, mine_ref, other_ref, inverse_ref, lower_ref, work, inverses):
    core = core_ref[0]
    halves = HEAD // HALF
    held = {}
    for (i, j), carrier in CARRIED:
        held[i, j] = jnp.where(core == carrier, mine_ref[i], other_ref[i])
    for (i, j), block in held.items():
        if j > i:
            i, j, block = j, i, block.T
        work[i * NB : (i + 1) * NB, j * NB : (j + 1) * NB] = block
    low = lax.broadcasted_iota(jnp.int32, (HALF, HALF), 0) >= lax.broadcasted_iota(jnp.int32, (HALF, HALF), 1)

    @pl.loop(0, halves)
    def _(at):
        here = pl.ds(pl.multiple_of(at * HALF, HALF), HALF)
        tiles = [work[pl.ds(pl.multiple_of(at * HALF + TILE * i, TILE), TILE), here] for i in range(HALF // TILE)]
        inverse = jnp.where(low, jnp.concatenate(invert_factor(tiles), axis=0), 0.0)
        inverses[at] = inverse
        for step in range(halves - 1):

            @pl.when(at == step)
            def _():
                after = (step + 1) * HALF
                panel = dot_nt(work[after:, step * HALF : after], inverse)
                work[after:, step * HALF : after] = panel
                for begin in range(after, HEAD, HALF):
                    end = begin + HALF
                    part = panel[begin - after :]
                    work[begin:, begin:end] = work[begin:, begin:end] - dot_nt(part, part[:HALF])

    for k in range(PANELS):
        first, second = inverses[2 * k], inverses[2 * k + 1]
        below = work[k * NB + HALF : (k + 1) * NB, k * NB : k * NB + HALF]
        inverse_ref[k, :HALF, :HALF] = first
        inverse_ref[k, :HALF, HALF:] = jnp.zeros((HALF, HALF), jnp.float32)
        inverse_ref[k, HALF:, :HALF] = -dot_nn(second, dot_nn(below, first))
        inverse_ref[k, HALF:, HALF:] = second
    lower_ref[0] = work[NB : 2 * NB, :NB]
    lower_ref[1] = work[2 * NB :, :NB]
    lower_ref[2] = work[2 * NB :, NB : 2 * NB]


def factor_head(core, mine, other):
    return pl.pallas_call(
        head_kernel,
        out_shape=[jax.ShapeDtypeStruct((PANELS, NB, NB), jnp.float32)] * 2,
        in_specs=[pl.BlockSpec(memory_space=pltpu.SMEM)] + [pl.BlockSpec(memory_space=pltpu.VMEM)] * 2,
        out_specs=[pl.BlockSpec(memory_space=pltpu.VMEM)] * 2,
        scratch_shapes=[
            pltpu.VMEM((HEAD, HEAD), jnp.float32),
            pltpu.VMEM((HEAD // HALF, HALF, HALF), jnp.float32),
        ],
        cost_estimate=pl.CostEstimate(flops=40_000_000_000, bytes_accessed=3_000_000, transcendentals=0),
        compiler_params=pltpu.CompilerParams(vmem_limit_bytes=VMEM),
        name="factor_head",
    )(core, mine, other)


def update_kernel(grid_rows, grid_cols, place_ref, inverse_ref, lower_ref, matrix_ref, *refs):
    heads, (mine_ref, other_ref, last_ref, out_ref, across) = refs[:grid_rows], refs[grid_rows:]
    my_row, my_col = place_ref[0], place_ref[1]
    core = my_col % 2
    row_slots, col_slots = matrix_ref.shape[0] // NB, matrix_ref.shape[1] // NB
    for j in range(PANELS):
        raw = heads[0][...]
        for d in range(1, grid_rows):
            raw = jnp.where((my_row ^ j) == d, heads[d][...], raw)
        if j >= 1:
            raw = raw - dot_nn(lower_ref[j - 1], across[:NB])
        if j == 2:
            raw = raw - dot_nn(lower_ref[2], across[NB : 2 * NB])
        across[j * NB : (j + 1) * NB] = dot_nn(inverse_ref[j], raw)
    low = lax.broadcasted_iota(jnp.int32, (NB, NB), 0) >= lax.broadcasted_iota(jnp.int32, (NB, NB), 1)

    @pl.loop(0, row_slots)
    def _(slot):
        here = pl.ds(pl.multiple_of(slot * NB, NB), NB)
        row = my_row + grid_rows * slot
        mine, other, last = mine_ref[here], other_ref[here], last_ref[here]
        first = dot_nt(jnp.where(core == 0, mine, other), inverse_ref[0])
        second = dot_nt(jnp.where(core == 0, other, mine) - dot_nt(first, lower_ref[0]), inverse_ref[1])
        third = dot_nt(last - dot_nt(first, lower_ref[1]) - dot_nt(second, lower_ref[2]), inverse_ref[2])
        solved = jnp.concatenate([first, second, third], axis=1)
        for t in range(col_slots):
            there = slice(t * NB, (t + 1) * NB)
            updated = matrix_ref[here, there] - dot_nn(solved, across[:, there])
            updated = jnp.where(row < PANELS, 0.0, updated)
            if t == 0:
                panel = jnp.where(my_col == 0, first, jnp.where(my_col == 1, second, third))
                panel = jnp.where((row > my_col) | ((row == my_col) & low), panel, 0.0)
                updated = jnp.where(my_col < PANELS, panel, updated)
            out_ref[here, there] = updated


def update(place, inverse, lower, matrix, heads, mine, other, last):
    grid_rows, grid_cols = lax.axis_size("row"), lax.axis_size("col")
    return pl.pallas_call(
        functools.partial(update_kernel, grid_rows, grid_cols),
        out_shape=jax.ShapeDtypeStruct(matrix.shape, jnp.float32),
        in_specs=[pl.BlockSpec(memory_space=pltpu.SMEM)]
        + [pl.BlockSpec(memory_space=pltpu.VMEM)] * (6 + len(heads)),
        out_specs=pl.BlockSpec(memory_space=pltpu.VMEM),
        scratch_shapes=[pltpu.VMEM((HEAD, matrix.shape[1]), jnp.float32)],
        cost_estimate=pl.CostEstimate(flops=10_000_000_000, bytes_accessed=10_000_000, transcendentals=0),
        compiler_params=pltpu.CompilerParams(vmem_limit_bytes=VMEM),
        name="update",
    )(place, inverse, lower, matrix, *heads, mine, other, last)


def body(matrix):
    grid_rows, grid_cols = lax.axis_size("row"), lax.axis_size("col")
    planes = grid_cols // 2
    my_row, my_col = lax.axis_index("row"), lax.axis_index("col")
    plane, core = my_col // 2, my_col % 2

    def send(x, pairs):
        flat = [(a * grid_cols + b, c * grid_cols + d) for (a, b), (c, d) in pairs]
        return lax.ppermute(x, ("row", "col"), flat)

    def swap_cores(x):
        return send(x, [((r, c), (r, c ^ 1)) for r in range(grid_rows) for c in range(grid_cols)])

    def along_rows(x):
        out = [x]
        for d in range(1, grid_rows):
            out.append(
                send(x, [((i, c), (i ^ d, c)) for i in range(PANELS) if i ^ d < grid_rows for c in range(grid_cols)])
            )
        return out

    corner = matrix[:NB, :NB]
    carried = jnp.zeros_like(corner)
    for d in [*range(1, planes), 0]:
        pairs = []
        for (i, j), carrier in CARRIED:
            target = 2 * ((j // 2 + d) % planes) + carrier
            if target != j:
                pairs.append(((i, j), (i, target)))
        carried = carried + send(corner, pairs)
    native = jnp.zeros((), jnp.bool_)
    for (i, j), carrier in CARRIED:
        if j % 2 == carrier:
            native = native | ((my_row == i) & (my_col == j))
    carried = jnp.where(native, corner, carried)
    found = along_rows(carried)
    ordered = []
    for j in range(PANELS):
        block = found[0]
        for d in range(1, grid_rows):
            block = jnp.where((my_row ^ j) == d, found[d], block)
        ordered.append(block)
    ordered = jnp.stack(ordered)
    other_ordered = swap_cores(ordered)

    strip, matrix_after, _ = lax.optimization_barrier((matrix[:, :NB], matrix, carried))
    mine, last = strip, strip
    for d in range(1, planes):
        pairs = []
        for r in range(grid_rows):
            pairs += [((r, q), (r, 2 * d + q)) for q in range(2)]
            pairs.append(((r, 2), (r, 2 * ((1 + d) % planes))))
        got = send(strip, pairs)
        mine = jnp.where(plane == d, got, mine)
        last = jnp.where((plane - 1) % planes == d, got, last)
    heads = along_rows(matrix_after[:NB])
    other, other_last = swap_cores(mine), swap_cores(last)
    last = jnp.where(core == 0, last, other_last)

    inverse, lower = factor_head(jnp.full((1,), core, jnp.int32), ordered, other_ordered)
    place = jnp.stack([my_row, my_col]).astype(jnp.int32)
    return update(place, inverse, lower, matrix, heads, mine, other, last)


def solution(mesh):
    return jax.shard_map(body, mesh=mesh, in_specs=(P("row", "col"),), out_specs=P("row", "col"), check_vma=False)
```

time: 734 us -> 162 us (0.22); the launches traced: 724 us -> 162 us
  waiting for transfers between devices: 448 us -> 60.1 us
  other arithmetic: 187 us -> 7.11 us
  Pallas kernels: 0 us -> 54.5 us
  local copies, waits for them, and re-layouts: 46.1 us -> 3.41 us
  starting transfers between devices: 0.95 us -> 36.5 us
  matrix products: 23.5 us -> 0 us
  between operations: 18 us -> 0.21 us
    psum x9 -> x0, waiting for transfers between devices: 447 us -> none  [from_root(): return lax.psum(jnp.where(mine, shard, jnp.zeros_like(shard)), axis)]
    another operation x27 -> x3, other arithmetic: 165 us -> 2.75 us  [the longest x2 2.13 us: body(): ordered = jnp.stack(ordered)]
    ppermute x0 -> x16, waiting for transfers between devices: none -> 60.1 us  [send(): return lax.ppermute(x, ('row', 'col'), flat)]
    pallas_call x0 -> x2, Pallas kernels: none -> 54.5 us  [the longest x1 31.1 us: factor_head(): pl.pallas_call(head_kernel, out_shape=[jax.ShapeDtypeStruct((PANELS, NB,...]
    ppermute x0 -> x16, starting transfers between devices: none -> 36.5 us  [send(): return lax.ppermute(x, ('row', 'col'), flat)]
    dot_general x3 -> x0, matrix products: 12 us -> none  [subtract(): jnp.einsum('lan,mbn->lamb', panel_rows, column_rows, precision=lax.Precis...]
    another operation x28 -> x0, local copies, waits for them, and re-layouts: 11.9 us -> none  [the longest x22 11.9 us: solve_panel(): solved = jax.scipy.linalg.solve_triangular(factor, flat.T, lower=True).T]
    another operation x15 -> x0, matrix products: 11.6 us -> none  [the longest x9 6.82 us: solve_panel(): solved = jax.scipy.linalg.solve_triangular(factor, flat.T, lower=True).T]
  transfers between devices with their start and end apart: 9 -> 16, of which waited for: 9 -> 6; matrix products, arithmetic and copies ran while one was open for 2% -> 4% of each run, Pallas kernels for 0% -> 19%
where the time goes in v1:
time: 162 us
  waiting for transfers between devices  60.1 us (37%)
  Pallas kernels  54.5 us (34%)
  starting transfers between devices  36.5 us (23%)
  other arithmetic  7.11 us (4%)
  local copies, waits for them, and re-layouts  3.41 us (2%)
    ppermute x16, waiting for transfers between devices, send(): return lax.ppermute(x, ('row', 'col'), flat)  60.1 us
    ppermute x16, starting transfers between devices, send(): return lax.ppermute(x, ('row', 'col'), flat)  36.5 us
    pallas_call x1, Pallas kernels, factor_head(): pl.pallas_call(head_kernel, out_shape=[jax.ShapeDtypeStruct((PANELS, NB,...  31.1 us
    pallas_call x1, Pallas kernels, update(): pl.pallas_call(functools.partial(update_kernel, grid_rows, grid_cols), ou...  23.4 us
  transfers between devices with their start and end apart: 16, of which 6 were waited for; matrix products, arithmetic and copies ran while one was open for 4% of the time, Pallas kernels for 19%

profile of v1, /device:TPU:0, one launch (start us, length us, event | category | flops | bytes accessed | tf_op | source)
XLA Modules:
  0.0 161.8 jit_solution(13930647419084846441)
XLA Ops:
  1.1 4.9 %collective-permute-start = (f32[256,256]{1,0:T(8,128)S(1)}, f32[256,256]{1,0:T(8,128)S(1)}, u32[]{:S(2)}, u32[]{:S(2)}) collective-permute-start(f32[256,256]{1,0:T(8,128)S(1)} %slice.9), channel_id=1, source_target_pairs={{0,2},{1,3},{10,12},{9,11},{16,18},{18,21}} | collective-permute-start | bytes 786440 | tf_op jit(solution)/shard_map/ppermute | solution.py:192
  6.1 1.7 %collective-permute-start.1 = (f32[256,256]{1,0:T(8,128)S(1)}, f32[256,256]{1,0:T(8,128)S(1)}, u32[]{:S(2)}, u32[]{:S(2)}) collective-permute-start(f32[256,256]{1,0:T(8,128)S(1)} %slice.9), channel_id=1, source_target_pairs={{0,4},{1,5},{10,14},{9,13},{16,20},{18,23}} | collective-permute-start | bytes 786440 | tf_op jit(solution)/shard_map/ppermute | solution.py:192
  7.8 1.7 %collective-permute-start.2 = (f32[256,256]{1,0:T(8,128)S(1)}, f32[256,256]{1,0:T(8,128)S(1)}, u32[]{:S(2)}, u32[]{:S(2)}) collective-permute-start(f32[256,256]{1,0:T(8,128)S(1)} %slice.9), channel_id=1, source_target_pairs={{0,6},{1,7},{10,8},{9,15},{16,22},{18,17}} | collective-permute-start | bytes 786440 | tf_op jit(solution)/shard_map/ppermute | solution.py:192
  9.5 1.4 collective-permute-start.3
  10.8 1.9 %collective-permute-done = f32[256,256]{1,0:T(8,128)S(1)} collective-permute-done((f32[256,256]{1,0:T(8,128)S(1)}, f32[256,256]{1,0:T(8,128)S(1)}, u32[]{:S(2)}, u32[]{:S(2)}) %collective-permute-start) | collective-permute-done | bytes 262176 | tf_op jit(solution)/shard_map/ppermute | solution.py:192
  12.8 5.6 %collective-permute-done.1 = f32[256,256]{1,0:T(8,128)S(1)} collective-permute-done((f32[256,256]{1,0:T(8,128)S(1)}, f32[256,256]{1,0:T(8,128)S(1)}, u32[]{:S(2)}, u32[]{:S(2)}) %collective-permute-start.1) | collective-permute-done | bytes 262176 | tf_op jit(solution)/shard_map/ppermute | solution.py:192
  18.4 4.5 %collective-permute-done.2 = f32[256,256]{1,0:T(8,128)S(1)} collective-permute-done((f32[256,256]{1,0:T(8,128)S(1)}, f32[256,256]{1,0:T(8,128)S(1)}, u32[]{:S(2)}, u32[]{:S(2)}) %collective-permute-start.2) | collective-permute-done | bytes 262176 | tf_op jit(solution)/shard_map/ppermute | solution.py:192
  24.0 1.3 collective-permute-start.4
  25.3 1.9 %collective-permute-start.5 = (f32[256,256]{1,0:T(8,128)S(1)}, f32[256,256]{1,0:T(8,128)}, u32[]{:S(2)}, u32[]{:S(2)}) collective-permute-start(f32[256,256]{1,0:T(8,128)S(1)} %add_select_fusion), channel_id=1, source_target_pairs={{0,16},{1,17},{2,18},{3,19},{4,20},{5,21},{6,22},{7,23},{8,24},{9,... | collective-permute-start | bytes 786440 | tf_op jit(solution)/shard_map/ppermute | solution.py:192
  27.2 1.9 %collective-permute-start.6 = (f32[256,256]{1,0:T(8,128)S(1)}, f32[256,256]{1,0:T(8,128)}, u32[]{:S(2)}, u32[]{:S(2)}) collective-permute-start(f32[256,256]{1,0:T(8,128)S(1)} %add_select_fusion), channel_id=1, source_target_pairs={{0,8},{1,9},{2,10},{3,11},{4,12},{5,13},{6,14},{7,15},{8,0},{9,1},... | collective-permute-start | bytes 786440 | tf_op jit(solution)/shard_map/ppermute | solution.py:192
  29.3 6.2 %collective-permute-start.11 = (f32[1024,256]{1,0:T(8,128)S(1)}, f32[1024,256]{1,0:T(8,128)}, u32[]{:S(2)}, u32[]{:S(2)}) collective-permute-start(f32[1024,256]{1,0:T(8,128)S(1)} %slice.10), channel_id=1, source_target_pairs={{0,6},{1,7},{2,0},{8,14},{9,15},{10,8},{16,22},{17,23},{18,16},{24... | collective-permute-start | bytes 3145736 | tf_op jit(solution)/shard_map/ppermute | solution.py:192
  35.5 2.3 %collective-permute-start.12 = (f32[1024,256]{1,0:T(8,128)S(1)}, f32[1024,256]{1,0:T(8,128)}, u32[]{:S(2)}, u32[]{:S(2)}) collective-permute-start(f32[1024,256]{1,0:T(8,128)S(1)} %slice.10), channel_id=1, source_target_pairs={{0,4},{1,5},{2,6},{8,12},{9,13},{10,14},{16,20},{17,21},{18,22},{2... | collective-permute-start | bytes 3145736 | tf_op jit(solution)/shard_map/ppermute | solution.py:192
  38.4 3.4 %collective-permute-start.13 = (f32[1024,256]{1,0:T(8,128)S(1)}, f32[1024,256]{1,0:T(8,128)}, u32[]{:S(2)}, u32[]{:S(2)}) collective-permute-start(f32[1024,256]{1,0:T(8,128)S(1)} %slice.10), channel_id=1, source_target_pairs={{0,2},{1,3},{2,4},{8,10},{9,11},{10,12},{16,18},{17,19},{18,20},{2... | collective-permute-start | bytes 3145736 | tf_op jit(solution)/shard_map/ppermute | solution.py:192
  41.9 1.2 select_bitcast_fusion.2
  44.7 1.3 collective-permute-start.10
  46.0 13.1 %collective-permute-done.11 = f32[1024,256]{1,0:T(8,128)} collective-permute-done((f32[1024,256]{1,0:T(8,128)S(1)}, f32[1024,256]{1,0:T(8,128)}, u32[]{:S(2)}, u32[]{:S(2)}) %collective-permute-start.11) | collective-permute-done | bytes 1048608 | tf_op jit(solution)/shard_map/ppermute | solution.py:192
  59.1 3.9 %collective-permute-start.8 = (f32[256,512]{1,0:T(8,128)S(1)}, f32[256,512]{1,0:T(8,128)S(1)}, u32[]{:S(2)}, u32[]{:S(2)}) collective-permute-start(f32[256,512]{1,0:T(8,128)S(1)} %slice.11.refs_0_), channel_id=1, source_target_pairs={{0,8},{1,9},{2,10},{3,11},{4,12},{5,13},{6,14},{7,15},{8,0},{9,1},... | collective-permute-start | bytes 1572872 | tf_op jit(solution)/shard_map/ppermute | solution.py:192
  63.0 18.6 %collective-permute-done.12 = f32[1024,256]{1,0:T(8,128)} collective-permute-done((f32[1024,256]{1,0:T(8,128)S(1)}, f32[1024,256]{1,0:T(8,128)}, u32[]{:S(2)}, u32[]{:S(2)}) %collective-permute-start.12) | collective-permute-done | bytes 1048608 | tf_op jit(solution)/shard_map/ppermute | solution.py:192
  81.6 4.0 %collective-permute-start.9 = (f32[256,512]{1,0:T(8,128)S(1)}, f32[256,512]{1,0:T(8,128)S(1)}, u32[]{:S(2)}, u32[]{:S(2)}) collective-permute-start(f32[256,512]{1,0:T(8,128)S(1)} %slice.11.refs_0_), channel_id=1, source_target_pairs={{0,16},{1,17},{2,18},{3,19},{4,20},{5,21},{6,22},{7,23},{8,24},{9,... | collective-permute-start | bytes 1572872 | tf_op jit(solution)/shard_map/ppermute | solution.py:192
  85.5 16.4 %collective-permute-done.13 = f32[1024,256]{1,0:T(8,128)} collective-permute-done((f32[1024,256]{1,0:T(8,128)S(1)}, f32[1024,256]{1,0:T(8,128)}, u32[]{:S(2)}, u32[]{:S(2)}) %collective-permute-start.13) | collective-permute-done | bytes 1048608 | tf_op jit(solution)/shard_map/ppermute | solution.py:192
  102.0 2.1 %select_select_fusion = (f32[1024,256]{1,0:T(8,128)S(1)}, f32[1024,256]{1,0:T(8,128)S(1)}) fusion(f32[1024,256]{1,0:T(8,128)} %collective-permute-done.11, f32[1024,256]{1,0:T(8,128)} %collective-permute-done.12, f32[1024,256]{1,0:T(8,128)} %collective-permute-done.13, f32[1024,256]{1,0:T(8,128)S(1)} %slice.10, pred[]{:T(512)S(6)} %eq.90, pred[]{:T(512)S(6)} %eq.89, ...), kind=kLoop, calls=%fused_computation | loop fusion | flops 1572864 | bytes 6291462 | tf_op jit(solution)/shard_map/jit(_where)/select_n | solution.py:238
  104.7 31.1 %factor_head.1 = (f32[3,256,256]{2,1,0:T(8,128)}, f32[3,256,256]{2,1,0:T(8,128)}) custom-call(s32[1]{0:T(128)} %bitcast.2.core_ref, f32[3,256,256]{2,1,0:T(8,128)} %pad_maximum_fusion.mine_ref, f32[3,256,256]{2,1,0:T(8,128)} %collective-permute-done.7.other_ref), custom_call_target="tpu_custom_call" | custom-call | flops 40000000000 | bytes 3000000 | tf_op jit(solution)/shard_map/factor_head/pallas_call | solution.py:118
  135.8 1.1 broadcast_select_fusion.refs_6_
  138.4 23.4 %update.1 = f32[1024,512]{1,0:T(8,128)} custom-call(s32[2]{0:T(128)} %pad_add_fusion.place_ref, f32[3,256,256]{2,1,0:T(8,128)} %get-tuple-element.9.inverse_ref, f32[3,256,256]{2,1,0:T(8,128)} %get-tuple-element.10.lower_ref, f32[1024,512]{1,0:T(8,128)} %matrix_ref.1, f32[256,512]{1,0:T(8,128)} %copy-done.2, f32[256,512]{1,0:T(8,128)} %copy-done.6, ...), custom_call_target="tpu_custom_call" | custom-call | flops 10000000000 | bytes 10000000 | tf_op jit(solution)/shard_map/update/pallas_call | solution.py:171
  (35 shorter events, 6.7 us)
Async XLA Ops:
  0.0 29.1 %copy-start = (f32[1024,512]{1,0:T(8,128)S(1)}, f32[1024,512]{1,0:T(8,128)}, u32[]{:S(2)}) copy-start(f32[1024,512]{1,0:T(8,128)} %matrix_ref.1) | copy-start | bytes 6291460
  1.1 11.6 %collective-permute-start = (f32[256,256]{1,0:T(8,128)S(1)}, f32[256,256]{1,0:T(8,128)S(1)}, u32[]{:S(2)}, u32[]{:S(2)}) collective-permute-start(f32[256,256]{1,0:T(8,128)S(1)} %slice.9), channel_id=1, source_target_pairs={{0,2},{1,3},{10,12},{9,11},{16,18},{18,21}} | collective-permute-start | bytes 786440 | tf_op jit(solution)/shard_map/ppermute | solution.py:192
  6.1 12.3 %collective-permute-start.1 = (f32[256,256]{1,0:T(8,128)S(1)}, f32[256,256]{1,0:T(8,128)S(1)}, u32[]{:S(2)}, u32[]{:S(2)}) collective-permute-start(f32[256,256]{1,0:T(8,128)S(1)} %slice.9), channel_id=1, source_target_pairs={{0,4},{1,5},{10,14},{9,13},{16,20},{18,23}} | collective-permute-start | bytes 786440 | tf_op jit(solution)/shard_map/ppermute | solution.py:192
  7.8 15.1 %collective-permute-start.2 = (f32[256,256]{1,0:T(8,128)S(1)}, f32[256,256]{1,0:T(8,128)S(1)}, u32[]{:S(2)}, u32[]{:S(2)}) collective-permute-start(f32[256,256]{1,0:T(8,128)S(1)} %slice.9), channel_id=1, source_target_pairs={{0,6},{1,7},{10,8},{9,15},{16,22},{18,17}} | collective-permute-start | bytes 786440 | tf_op jit(solution)/shard_map/ppermute | solution.py:192
  9.5 13.4 %collective-permute-start.3 = (f32[256,256]{1,0:T(8,128)S(1)}, f32[256,256]{1,0:T(8,128)}, u32[]{:S(2)}, u32[]{:S(2)}) collective-permute-start(f32[256,256]{1,0:T(8,128)S(1)} %slice.9), channel_id=1, source_target_pairs={{18,19}} | collective-permute-start | bytes 786440 | tf_op jit(solution)/shard_map/ppermute | solution.py:192
  24.0 13.8 %collective-permute-start.4 = (f32[256,256]{1,0:T(8,128)S(1)}, f32[256,256]{1,0:T(8,128)S(1)}, u32[]{:S(2)}, u32[]{:S(2)}) collective-permute-start(f32[256,256]{1,0:T(8,128)S(1)} %add_select_fusion), channel_id=1, source_target_pairs={{0,24},{1,25},{2,26},{3,27},{4,28},{5,29},{6,30},{7,31},{8,16},{9,... | collective-permute-start | bytes 786440 | tf_op jit(solution)/shard_map/ppermute | solution.py:192
  25.3 16.6 %collective-permute-start.5 = (f32[256,256]{1,0:T(8,128)S(1)}, f32[256,256]{1,0:T(8,128)}, u32[]{:S(2)}, u32[]{:S(2)}) collective-permute-start(f32[256,256]{1,0:T(8,128)S(1)} %add_select_fusion), channel_id=1, source_target_pairs={{0,16},{1,17},{2,18},{3,19},{4,20},{5,21},{6,22},{7,23},{8,24},{9,... | collective-permute-start | bytes 786440 | tf_op jit(solution)/shard_map/ppermute | solution.py:192
  27.2 14.7 %collective-permute-start.6 = (f32[256,256]{1,0:T(8,128)S(1)}, f32[256,256]{1,0:T(8,128)}, u32[]{:S(2)}, u32[]{:S(2)}) collective-permute-start(f32[256,256]{1,0:T(8,128)S(1)} %add_select_fusion), channel_id=1, source_target_pairs={{0,8},{1,9},{2,10},{3,11},{4,12},{5,13},{6,14},{7,15},{8,0},{9,1},... | collective-permute-start | bytes 786440 | tf_op jit(solution)/shard_map/ppermute | solution.py:192
  29.3 29.8 %collective-permute-start.11 = (f32[1024,256]{1,0:T(8,128)S(1)}, f32[1024,256]{1,0:T(8,128)}, u32[]{:S(2)}, u32[]{:S(2)}) collective-permute-start(f32[1024,256]{1,0:T(8,128)S(1)} %slice.10), channel_id=1, source_target_pairs={{0,6},{1,7},{2,0},{8,14},{9,15},{10,8},{16,22},{17,23},{18,16},{24... | collective-permute-start | bytes 3145736 | tf_op jit(solution)/shard_map/ppermute | solution.py:192
  35.5 46.1 %collective-permute-start.12 = (f32[1024,256]{1,0:T(8,128)S(1)}, f32[1024,256]{1,0:T(8,128)}, u32[]{:S(2)}, u32[]{:S(2)}) collective-permute-start(f32[1024,256]{1,0:T(8,128)S(1)} %slice.10), channel_id=1, source_target_pairs={{0,4},{1,5},{2,6},{8,12},{9,13},{10,14},{16,20},{17,21},{18,22},{2... | collective-permute-start | bytes 3145736 | tf_op jit(solution)/shard_map/ppermute | solution.py:192
  37.7 0.7 copy-start.3
  38.4 63.5 %collective-permute-start.13 = (f32[1024,256]{1,0:T(8,128)S(1)}, f32[1024,256]{1,0:T(8,128)}, u32[]{:S(2)}, u32[]{:S(2)}) collective-permute-start(f32[1024,256]{1,0:T(8,128)S(1)} %slice.10), channel_id=1, source_target_pairs={{0,2},{1,3},{2,4},{8,10},{9,11},{10,12},{16,18},{17,19},{18,20},{2... | collective-permute-start | bytes 3145736 | tf_op jit(solution)/shard_map/ppermute | solution.py:192
  44.0 60.2 %collective-permute-start.7 = (f32[3,256,256]{2,1,0:T(8,128)}, f32[3,256,256]{2,1,0:T(8,128)}, u32[]{:S(2)}, u32[]{:S(2)}) collective-permute-start(f32[3,256,256]{2,1,0:T(8,128)} %pad_maximum_fusion.mine_ref), channel_id=1, source_target_pairs={{0,1},{1,0},{2,3},{3,2},{4,5},{5,4},{6,7},{7,6},{8,9},{9,8},{10,11... | collective-permute-start | bytes 2359304 | tf_op jit(solution)/shard_map/ppermute | solution.py:192
  44.7 59.4 %copy-start.2 = (f32[256,512]{1,0:T(8,128)}, f32[256,512]{1,0:T(8,128)S(1)}, u32[]{:S(2)}) copy-start(f32[256,512]{1,0:T(8,128)S(1)} %slice.11.refs_0_) | copy-start | bytes 1572868
  44.7 92.2 %collective-permute-start.10 = (f32[256,512]{1,0:T(8,128)S(1)}, f32[256,512]{1,0:T(8,128)S(1)}, u32[]{:S(2)}, u32[]{:S(2)}) collective-permute-start(f32[256,512]{1,0:T(8,128)S(1)} %slice.11.refs_0_), channel_id=1, source_target_pairs={{0,24},{1,25},{2,26},{3,27},{4,28},{5,29},{6,30},{7,31},{8,16},{9,... | collective-permute-start | bytes 1572872 | tf_op jit(solution)/shard_map/ppermute | solution.py:192
  59.1 77.8 %collective-permute-start.8 = (f32[256,512]{1,0:T(8,128)S(1)}, f32[256,512]{1,0:T(8,128)S(1)}, u32[]{:S(2)}, u32[]{:S(2)}) collective-permute-start(f32[256,512]{1,0:T(8,128)S(1)} %slice.11.refs_0_), channel_id=1, source_target_pairs={{0,8},{1,9},{2,10},{3,11},{4,12},{5,13},{6,14},{7,15},{8,0},{9,1},... | collective-permute-start | bytes 1572872 | tf_op jit(solution)/shard_map/ppermute | solution.py:192
  81.6 55.3 %collective-permute-start.9 = (f32[256,512]{1,0:T(8,128)S(1)}, f32[256,512]{1,0:T(8,128)S(1)}, u32[]{:S(2)}, u32[]{:S(2)}) collective-permute-start(f32[256,512]{1,0:T(8,128)S(1)} %slice.11.refs_0_), channel_id=1, source_target_pairs={{0,16},{1,17},{2,18},{3,19},{4,20},{5,21},{6,22},{7,23},{8,24},{9,... | collective-permute-start | bytes 1572872 | tf_op jit(solution)/shard_map/ppermute | solution.py:192
  104.1 31.6 %copy-start.1 = (f32[1024,256]{1,0:T(8,128)}, f32[1024,256]{1,0:T(8,128)S(1)}, u32[]{:S(2)}) copy-start(f32[1024,256]{1,0:T(8,128)S(1)} %get-tuple-element.14.refs_4_) | copy-start | bytes 3145732
  104.1 31.6 %collective-permute-start.15 = (f32[1024,256]{1,0:T(8,128)S(1)}, f32[1024,256]{1,0:T(8,128)S(1)}, u32[]{:S(2)}, u32[]{:S(2)}) collective-permute-start(f32[1024,256]{1,0:T(8,128)S(1)} %get-tuple-element.13), channel_id=1, source_target_pairs={{0,1},{1,0},{2,3},{3,2},{4,5},{5,4},{6,7},{7,6},{8,9},{9,8},{10,11... | collective-permute-start | bytes 3145736 | tf_op jit(solution)/shard_map/ppermute | solution.py:192
  104.2 32.7 %collective-permute-start.14 = (f32[1024,256]{1,0:T(8,128)S(1)}, f32[1024,256]{1,0:T(8,128)S(1)}, u32[]{:S(2)}, u32[]{:S(2)}) collective-permute-start(f32[1024,256]{1,0:T(8,128)S(1)} %get-tuple-element.14.refs_4_), channel_id=1, source_target_pairs={{0,1},{1,0},{2,3},{3,2},{4,5},{5,4},{6,7},{7,6},{8,9},{9,8},{10,11... | collective-permute-start | bytes 3145736 | tf_op jit(solution)/shard_map/ppermute | solution.py:192
  136.9 0.8 copy-start.5
  136.9 1.0 copy-start.6
  136.9 1.2 copy-start.7
  136.9 1.4 copy-start.4

commit v2 on v0

v2 whole, which is shorter than its diff:
```python
import functools

import jax
import jax.numpy as jnp
from jax import lax
from jax.experimental import pallas as pl
from jax.experimental.pallas import tpu as pltpu
from jax.sharding import PartitionSpec as P

NB = 256
PANELS = 3
HALF = 128
TILE = 8
STEP = 16
HEAD = PANELS * NB
MIB = 1024 * 1024

CARRIED = (((0, 0), 0), ((0, 1), 1), ((1, 2), 0), ((1, 1), 1), ((2, 0), 0), ((2, 2), 1))


def sublane(x, k):
    return jnp.broadcast_to(x[k : k + 1, :], x.shape)


def lane(x, k):
    return jnp.broadcast_to(x[:, k : k + 1], x.shape)


def dot_nt(a, b):
    return lax.dot_general(
        a, b, (((1,), (1,)), ((), ())), precision=lax.Precision.HIGHEST, preferred_element_type=jnp.float32
    )


def dot_nn(a, b):
    return jnp.dot(a, b, precision=lax.Precision.HIGHEST, preferred_element_type=jnp.float32)


def opaque(x):
    return jnp.maximum(x, -3.0e38)


def total(terms):
    while len(terms) > 1:
        terms = [sum(terms[i : i + 2][1:], terms[i]) for i in range(0, len(terms), 2)]
    return terms[0]


def invert_factor(tiles):
    count, wide = len(tiles), STEP // TILE
    rows = lax.broadcasted_iota(jnp.int32, (TILE, HALF), 0)
    lanes = lax.broadcasted_iota(jnp.int32, (TILE, HALF), 1)
    out = []
    for step in range(0, count, wide):
        start, after = TILE * step, step + wide
        own = (lanes >= start) & (lanes < start + STEP)
        column = [[opaque(lane(tiles[step + e], start + k)) for e in range(wide)] for k in range(STEP)]
        forward = [
            jnp.where(own, jnp.where(lanes - start == rows + TILE * e, 1.0, 0.0), tiles[step + e]) for e in range(wide)
        ]
        solved, pivots, below = list(forward), [], {}
        for k in range(0, STEP, 2):
            o, i = k // TILE, k % TILE
            a, b, c = sublane(column[k][o], i), sublane(column[k + 1][o], i), sublane(column[k + 1][o], i + 1)
            det = a * c - b * b
            inverse = pl.reciprocal(det, approx=False)
            pivots.append((a, b, c, det, inverse))
            if k == 0:
                zero = jnp.minimum(jnp.abs(inverse), 0.0)
                for t in range(after, count):
                    below[t] = [lane(tiles[t] + zero, start + j) for j in range(STEP)]
            one = [column[k][e] * c - column[k + 1][e] * b for e in range(wide)]
            two = [column[k + 1][e] * a - column[k][e] * b for e in range(wide)]
            pair = (rows == i) | (rows == i + 1)
            one[o], two[o] = jnp.where(pair, 0.0, one[o]), jnp.where(pair, 0.0, two[o])
            first, second = [x * inverse for x in one], [x * inverse for x in two]
            for j in range(k + 2, STEP):
                u, v = sublane(column[j][o], i), sublane(column[j][o], i + 1)
                for e in range(wide):
                    if j < k + 4:
                        column[j][e] = column[j][e] - (one[e] * u + two[e] * v) * inverse
                    else:
                        column[j][e] = column[j][e] - (first[e] * u + second[e] * v)
            u, v = sublane(forward[o], i), sublane(forward[o], i + 1)
            x, y = sublane(solved[o], i), sublane(solved[o], i + 1)
            for e in range(wide):
                if after < count:
                    solved[e] = solved[e] - (first[e] * x + second[e] * y)
                if e > o:
                    forward[e] = forward[e] - (first[e] * u + second[e] * v)
                elif e == o and i + 2 < TILE:
                    forward[e] = forward[e] - jnp.where(rows > i, first[e] * u + second[e] * v, 0.0)
        if after < count:
            right = []
            for k in range(0, STEP, 2):
                o, i = k // TILE, k % TILE
                a, b, c, _, inverse = pivots[k // 2]
                x, y = sublane(solved[o], i), sublane(solved[o], i + 1)
                right += [(x * c - y * b) * inverse, (y * a - x * b) * inverse]
            for t in range(after, count):
                tiles[t] = jnp.where(own, 0.0, tiles[t]) - total([below[t][k] * right[k] for k in range(STEP)])
        for e in range(wide):
            diagonal, within = jnp.ones_like(forward[e]), jnp.zeros_like(forward[e])
            for i in range(0, TILE, 2):
                a, b, _, det, _ = pivots[(TILE * e + i) // 2]
                inverse = pl.reciprocal(a, approx=False)
                diagonal = jnp.where(rows == i, a, jnp.where(rows == i + 1, det * inverse, diagonal))
                within = jnp.where(rows == i + 1, b * inverse * sublane(forward[e], i), within)
            out.append((forward[e] - within) * lax.rsqrt(diagonal))
    return out


def assemble(my_row, core, found, mirrored, work):
    for (i, j), carrier in CARRIED:
        for d in range(len(found)):

            @pl.when((my_row ^ i) == d)
            def _():
                block = jnp.where(core == carrier, found[d][...], mirrored[d][...])
                if j > i:
                    work[j * NB : (j + 1) * NB, i * NB : (i + 1) * NB] = block.T
                else:
                    work[i * NB : (i + 1) * NB, j * NB : (j + 1) * NB] = block


def head_kernel(begin, end, place_ref, *refs):
    inverse_ref, work = refs[-2:]
    if begin == 0:
        count = (len(refs) - 2) // 2
        assemble(place_ref[0], place_ref[1] % 2, refs[:count], refs[count : 2 * count], work)
    else:
        work[...] = refs[0][...]
    low = lax.broadcasted_iota(jnp.int32, (HALF, HALF), 0) >= lax.broadcasted_iota(jnp.int32, (HALF, HALF), 1)

    @pl.loop(2 * begin, 2 * end)
    def _(at):
        here = pl.ds(pl.multiple_of(at * HALF, HALF), HALF)
        tiles = [work[pl.ds(pl.multiple_of(at * HALF + TILE * i, TILE), TILE), here] for i in range(HALF // TILE)]
        inverse = jnp.where(low, jnp.concatenate(invert_factor(tiles), axis=0), 0.0)
        diagonal = pl.ds(pl.multiple_of((at % 2) * HALF, HALF), HALF)
        inverse_ref[at // 2 - begin, diagonal, diagonal] = inverse
        work[here, here] = jnp.where(low, dot_nt(work[here, here], inverse), 0.0)
        for step in range(2 * begin, min(2 * end, HEAD // HALF - 1)):

            @pl.when(at == step)
            def _():
                after = (step + 1) * HALF
                solved = dot_nt(work[after:, step * HALF : after], inverse)
                work[after:, step * HALF : after] = solved
                for left in range(after, HEAD, HALF):
                    right = left + HALF
                    part = solved[left - after :]
                    work[left:, left:right] = work[left:, left:right] - dot_nt(part, part[:HALF])

    for k in range(begin, end):
        first, second = inverse_ref[k - begin, :HALF, :HALF], inverse_ref[k - begin, HALF:, HALF:]
        below = work[k * NB + HALF : (k + 1) * NB, k * NB : k * NB + HALF]
        inverse_ref[k - begin, HALF:, :HALF] = -dot_nn(second, dot_nn(below, first))
        inverse_ref[k - begin, :HALF, HALF:] = jnp.zeros((HALF, HALF), jnp.float32)
        work[k * NB : k * NB + HALF, k * NB + HALF : (k + 1) * NB] = jnp.zeros((HALF, HALF), jnp.float32)


def factor_panels(begin, end, place, *blocks):
    return pl.pallas_call(
        functools.partial(head_kernel, begin, end),
        out_shape=[
            jax.ShapeDtypeStruct((end - begin, NB, NB), jnp.float32),
            jax.ShapeDtypeStruct((HEAD, HEAD), jnp.float32),
        ],
        in_specs=[pl.BlockSpec(memory_space=pltpu.SMEM)] + [pl.BlockSpec(memory_space=pltpu.VMEM)] * len(blocks),
        out_specs=[pl.BlockSpec(memory_space=pltpu.VMEM)] * 2,
        cost_estimate=pl.CostEstimate(flops=1_000, bytes_accessed=1_000, transcendentals=0),
        compiler_params=pltpu.CompilerParams(vmem_limit_bytes=(14 if begin else 56) * MIB),
        name="factor_panels",
    )(place, *blocks)


def update_kernel(grid_rows, place_ref, early_ref, late_ref, head_ref, top_ref, top_other_ref, *refs):
    (held_ref, held_other_ref, swapped_ref, swapped_other_ref), heads = refs[:4], refs[4:-4]
    matrix_ref, out_ref, across, solved = refs[-4:]
    my_row, my_col = place_ref[0], place_ref[1]
    plane, core = my_col // 2, my_col % 2
    slot = pl.program_id(0)
    row = my_row + grid_rows * slot
    col_slots = out_ref.shape[1] // NB
    inverse = (early_ref.at[0], late_ref.at[0], late_ref.at[1])
    lower = {
        (i, j): head_ref.at[i * NB : (i + 1) * NB, j * NB : (j + 1) * NB] for i, j in ((1, 0), (2, 0), (2, 1))
    }

    @pl.when(slot == 0)
    def _():
        for j in range(PANELS):
            raw = heads[0][...]
            for d in range(1, grid_rows):
                raw = jnp.where((my_row ^ j) == d, heads[d][...], raw)
            for i in range(j):
                raw = raw - dot_nn(lower[j, i][...], across[i * NB : (i + 1) * NB])
            across[j * NB : (j + 1) * NB] = dot_nn(inverse[j][...], raw)

        def by_core(mine, other):
            return jnp.where(core == 0, mine, other)

        held, held_other = held_ref[...], held_other_ref[...]
        swapped, swapped_other = swapped_ref[...], swapped_other_ref[...]
        even = plane % 2 == 0
        own, across_core = jnp.where(even, held, swapped), jnp.where(even, held_other, swapped_other)
        last = jnp.where(even, by_core(swapped, swapped_other), by_core(held, held_other))
        first, second, third = top_ref[0], top_other_ref[0], by_core(top_ref[1], top_other_ref[1])
        raw = [
            jnp.concatenate([by_core(first, second), by_core(own, across_core)], axis=0),
            jnp.concatenate([by_core(second, first), by_core(across_core, own)], axis=0),
            jnp.concatenate([third, last], axis=0),
        ]
        for j in range(PANELS):
            rest = raw[j]
            for i in range(j):
                rest = rest - dot_nt(solved[:, i * NB : (i + 1) * NB], lower[j, i][...])
            solved[:, j * NB : (j + 1) * NB] = dot_nt(rest, inverse[j][...])

    mine = solved[pl.ds(pl.multiple_of(slot * NB, NB), NB), :]
    head_row = pl.ds(pl.multiple_of(jnp.minimum(my_row, PANELS - 1) * NB, NB), NB)
    head_col = pl.ds(pl.multiple_of(jnp.minimum(my_col, PANELS - 1) * NB, NB), NB)
    for t in range(col_slots):
        there = slice(t * NB, (t + 1) * NB)
        updated = matrix_ref[:, there] - dot_nn(mine, across[:, there])
        updated = jnp.where(row < PANELS, 0.0, updated)
        if t == 0:
            panel = mine[:, :NB]
            for j in range(1, PANELS):
                panel = jnp.where(my_col == j, mine[:, j * NB : (j + 1) * NB], panel)
            factor = jnp.where(my_col <= row, head_ref[head_row, head_col], 0.0)
            panel = jnp.where(row < PANELS, factor, panel)
            updated = jnp.where(my_col < PANELS, panel, updated)
        out_ref[:, there] = updated


def update(place, early, late, head, top, top_other, sent, heads, matrix):
    whole = pl.BlockSpec(memory_space=pltpu.VMEM)
    strip = pl.BlockSpec((NB, matrix.shape[1]), lambda slot: (slot, 0))
    return pl.pallas_call(
        functools.partial(update_kernel, len(heads)),
        out_shape=jax.ShapeDtypeStruct(matrix.shape, jnp.float32),
        grid=(matrix.shape[0] // NB,),
        in_specs=[pl.BlockSpec(memory_space=pltpu.SMEM)] + [whole] * (5 + len(sent) + len(heads)) + [strip],
        out_specs=strip,
        scratch_shapes=[
            pltpu.VMEM((HEAD, matrix.shape[1]), jnp.float32),
            pltpu.VMEM((matrix.shape[0], HEAD), jnp.float32),
        ],
        cost_estimate=pl.CostEstimate(flops=10_000_000_000, bytes_accessed=10_000_000, transcendentals=0),
        compiler_params=pltpu.CompilerParams(vmem_limit_bytes=(30 if len(heads) <= 4 else 56) * MIB),
        name="update",
    )(place, early, late, head, top, top_other, *sent, *heads, matrix)


def body(matrix):
    grid_rows, grid_cols = lax.axis_size("row"), lax.axis_size("col")
    planes = grid_cols // 2
    my_row, my_col = lax.axis_index("row"), lax.axis_index("col")
    plane, core = my_col // 2, my_col % 2

    def send(x, pairs):
        flat = [(a * grid_cols + b, c * grid_cols + d) for (a, b), (c, d) in pairs]
        return lax.ppermute(x, ("row", "col"), flat)

    def swap_cores(x):
        return send(x, [((r, c), (r, c ^ 1)) for r in range(grid_rows) for c in range(grid_cols)])

    def along_rows(x):
        out = [x]
        for d in range(1, grid_rows):
            out.append(
                send(x, [((i, c), (i ^ d, c)) for i in range(PANELS) if i ^ d < grid_rows for c in range(grid_cols)])
            )
        return out

    place = jnp.stack([my_row, my_col]).astype(jnp.int32)
    corner = matrix[:NB, :NB]
    carried = jnp.zeros_like(corner)
    passed = []
    for d in [*range(1, planes), 0]:
        pairs = []
        for (i, j), carrier in CARRIED:
            target = 2 * ((j // 2 + d) % planes) + carrier
            if target != j:
                pairs.append(((i, j), (i, target)))
        if d:
            for r in range(PANELS, grid_rows):
                pairs += [((r, q), (r, 2 * d + q)) for q in range(2)]
                pairs.append(((r, 2), (r, 2 * ((1 + d) % planes))))
        passed.append(send(corner, pairs))
        carried = carried + passed[-1]
    native = jnp.zeros((), jnp.bool_)
    for (i, j), carrier in CARRIED:
        if j % 2 == carrier:
            native = native | ((my_row == i) & (my_col == j))
    carried = jnp.where(native, corner, carried)
    heads = along_rows(matrix[:NB])
    found = along_rows(carried)
    top_mine, top_last = corner, corner
    for d in range(1, planes):
        top_mine = jnp.where(plane == d, passed[d - 1], top_mine)
        top_last = jnp.where((plane - 1) % planes == d, passed[d - 1], top_last)
    found, top = lax.optimization_barrier((found, jnp.stack([top_mine, top_last])))
    mirrored = [swap_cores(x) for x in found]
    strip, _ = lax.optimization_barrier((matrix[NB:, :NB], carried))

    held = strip
    distance = planes // 2
    while distance > 1:
        pairs = []
        for z in range(0, planes, 2 * distance):
            for r in range(grid_rows):
                pairs += [((r, 2 * z + q), (r, 2 * (z + distance) + q)) for q in range(2)]
                pairs.append(((r, 2 * z + 2), (r, 2 * (z + distance) + 2)))
        got = send(held, pairs)
        if distance == 2:
            early, head = factor_panels(0, 1, place, *found, *mirrored)
            got, head, heads = lax.optimization_barrier((got, head, heads))
        held = jnp.where((plane // distance) % 2 == 1, got, held)
        distance //= 2
    held, head, top = lax.optimization_barrier((held, head, top))
    pairs = []
    for z in range(0, planes, 2):
        for r in range(grid_rows):
            pairs += [((r, 2 * z + q), (r, 2 * z + 2 + q)) for q in range(2)]
            pairs.append(((r, 2 * z + 2), (r, 2 * z)))
    swapped = send(held, pairs)
    held_other, top_other = swap_cores(held), swap_cores(top)
    late, head = factor_panels(1, PANELS, place, head)
    swapped, late, head = lax.optimization_barrier((swapped, late, head))
    sent = [held, held_other, swapped, swap_cores(swapped)]
    return update(place, early, late, head, top, top_other, sent, heads, matrix)


def solution(mesh):
    return jax.shard_map(body, mesh=mesh, in_specs=(P("row", "col"),), out_specs=P("row", "col"), check_vma=False)
```

time: 734 us -> 119 us (0.16); the launches traced: 724 us -> 118 us
  waiting for transfers between devices: 448 us -> 25.8 us
  other arithmetic: 187 us -> 3.17 us
  Pallas kernels: 0 us -> 48.3 us
  local copies, waits for them, and re-layouts: 46.1 us -> 3.56 us
  starting transfers between devices: 0.95 us -> 36.8 us
  matrix products: 23.5 us -> 0 us
  between operations: 18 us -> 0.22 us
    psum x9 -> x0, waiting for transfers between devices: 447 us -> none  [from_root(): return lax.psum(jnp.where(mine, shard, jnp.zeros_like(shard)), axis)]
    another operation x27 -> x3, other arithmetic: 165 us -> 1.88 us  [the longest x2 1.24 us: body(): jnp.stack([top_mine, top_last])]
    pallas_call x0 -> x3, Pallas kernels: none -> 48.3 us  [the longest x2 28.8 us: factor_panels(): pl.pallas_call(functools.partial(head_kernel, begin, end), out_shape=[jax...]
    ppermute x0 -> x19, starting transfers between devices: none -> 36.8 us  [send(): return lax.ppermute(x, ('row', 'col'), flat)]
    ppermute x0 -> x19, waiting for transfers between devices: none -> 25.8 us  [send(): return lax.ppermute(x, ('row', 'col'), flat)]
    select_n x9 -> x1, other arithmetic: 13.9 us -> 1.28 us  [body(): held = jnp.where(plane // distance % 2 == 1, got, held)]
    dot_general x3 -> x0, matrix products: 12 us -> none  [subtract(): jnp.einsum('lan,mbn->lamb', panel_rows, column_rows, precision=lax.Precis...]
    another operation x28 -> x0, local copies, waits for them, and re-layouts: 11.9 us -> none  [the longest x22 11.9 us: solve_panel(): solved = jax.scipy.linalg.solve_triangular(factor, flat.T, lower=True).T]
  transfers between devices with their start and end apart: 9 -> 19, of which waited for: 9 -> 11; matrix products, arithmetic and copies ran while one was open for 2% -> 1% of each run, Pallas kernels for 0% -> 24%
where the time goes in v2:
time: 119 us; the launch traced here: 118 us
  Pallas kernels  48.3 us (41%)
  starting transfers between devices  36.8 us (31%)
  waiting for transfers between devices  25.8 us (22%)
  local copies, waits for them, and re-layouts  3.56 us (3%)
  other arithmetic  3.17 us (3%)
    ppermute x19, starting transfers between devices, send(): return lax.ppermute(x, ('row', 'col'), flat)  36.8 us
    pallas_call x2, Pallas kernels, factor_panels(): pl.pallas_call(functools.partial(head_kernel, begin, end), out_shape=[jax...  28.8 us
    ppermute x19, waiting for transfers between devices, send(): return lax.ppermute(x, ('row', 'col'), flat)  25.8 us
    pallas_call x1, Pallas kernels, update(): pl.pallas_call(functools.partial(update_kernel, len(heads)), out_shape=ja...  19.5 us
  transfers between devices with their start and end apart: 19, of which 11 were waited for; matrix products, arithmetic and copies ran while one was open for 1% of the time, Pallas kernels for 24%

profile of v2, /device:TPU:0, one launch (start us, length us, event | category | flops | bytes accessed | tf_op | source)
XLA Modules:
  0.0 117.8 jit_solution(17906852140997559239)
XLA Ops:
  1.8 7.0 %collective-permute-start.2 = (f32[256,256]{1,0:T(8,128)S(1)}, f32[256,256]{1,0:T(8,128)S(1)}, u32[]{:S(2)}, u32[]{:S(2)}) collective-permute-start(f32[256,256]{1,0:T(8,128)S(1)} %slice.9), channel_id=1, source_target_pairs={{0,6},{1,7},{10,8},{9,15},{16,22},{18,17},{24,30},{25,31},{26,24}} | collective-permute-start | bytes 786440 | tf_op jit(solution)/shard_map/ppermute | solution.py:265
  8.8 1.3 %collective-permute-start.1 = (f32[256,256]{1,0:T(8,128)S(1)}, f32[256,256]{1,0:T(8,128)S(1)}, u32[]{:S(2)}, u32[]{:S(2)}) collective-permute-start(f32[256,256]{1,0:T(8,128)S(1)} %slice.9), channel_id=1, source_target_pairs={{0,4},{1,5},{10,14},{9,13},{16,20},{18,23},{24,28},{25,29},{26,30}} | collective-permute-start | bytes 786440 | tf_op jit(solution)/shard_map/ppermute | solution.py:265
  10.1 2.0 %collective-permute-start = (f32[256,256]{1,0:T(8,128)S(1)}, f32[256,256]{1,0:T(8,128)}, u32[]{:S(2)}, u32[]{:S(2)}) collective-permute-start(f32[256,256]{1,0:T(8,128)S(1)} %slice.9), channel_id=1, source_target_pairs={{0,2},{1,3},{10,12},{9,11},{16,18},{18,21},{24,26},{25,27},{26,28}} | collective-permute-start | bytes 786440 | tf_op jit(solution)/shard_map/ppermute | solution.py:265
  12.1 3.4 %collective-permute-done.2 = f32[256,256]{1,0:T(8,128)S(1)} collective-permute-done((f32[256,256]{1,0:T(8,128)S(1)}, f32[256,256]{1,0:T(8,128)S(1)}, u32[]{:S(2)}, u32[]{:S(2)}) %collective-permute-start.2) | collective-permute-done | bytes 262176 | tf_op jit(solution)/shard_map/ppermute | solution.py:265
  15.5 5.6 %collective-permute-done.1 = f32[256,256]{1,0:T(8,128)S(1)} collective-permute-done((f32[256,256]{1,0:T(8,128)S(1)}, f32[256,256]{1,0:T(8,128)S(1)}, u32[]{:S(2)}, u32[]{:S(2)}) %collective-permute-start.1) | collective-permute-done | bytes 262176 | tf_op jit(solution)/shard_map/ppermute | solution.py:265
  21.8 3.8 %collective-permute-done = f32[256,256]{1,0:T(8,128)} collective-permute-done((f32[256,256]{1,0:T(8,128)S(1)}, f32[256,256]{1,0:T(8,128)}, u32[]{:S(2)}, u32[]{:S(2)}) %collective-permute-start) | collective-permute-done | bytes 262176 | tf_op jit(solution)/shard_map/ppermute | solution.py:265
  25.6 1.2 %select_bitcast_fusion.1 = (f32[1,256,256]{2,1,0:T(8,128)S(1)}, f32[1,256,256]{2,1,0:T(8,128)S(1)}, f32[256,256]{1,0:T(8,128)S(1)}) fusion(f32[256,256]{1,0:T(8,128)S(1)} %collective-permute-done.2, f32[256,256]{1,0:T(8,128)} %copy-done.7, f32[256,256]{1,0:T(8,128)} %collective-permute-done, pred[]{:T(512)S(6)} %eq.56, pred[]{:T(512)S(6)} %eq.55, ...), kind=kLoop, calls=%fused_computation.3 | loop fusion | flops 655360 | bytes 2097159 | tf_op jit(solution)/shard_map/stack | solution.py:305
  26.8 5.1 %collective-permute-start.6 = (f32[256,256]{1,0:T(8,128)S(1)}, f32[256,256]{1,0:T(8,128)}, u32[]{:S(2)}, u32[]{:S(2)}) collective-permute-start(f32[256,256]{1,0:T(8,128)S(1)} %get-tuple-element.27.refs_0_), channel_id=1, source_target_pairs={{0,24},{1,25},{2,26},{3,27},{4,28},{5,29},{6,30},{7,31},{8,16},{9,... | collective-permute-start | bytes 786440 | tf_op jit(solution)/shard_map/ppermute | solution.py:265
  31.9 1.9 %collective-permute-start.5 = (f32[256,256]{1,0:T(8,128)S(1)}, f32[256,256]{1,0:T(8,128)S(1)}, u32[]{:S(2)}, u32[]{:S(2)}) collective-permute-start(f32[256,256]{1,0:T(8,128)S(1)} %get-tuple-element.27.refs_0_), channel_id=1, source_target_pairs={{0,16},{1,17},{2,18},{3,19},{4,20},{5,21},{6,22},{7,23},{8,24},{9,... | collective-permute-start | bytes 786440 | tf_op jit(solution)/shard_map/ppermute | solution.py:265
  33.8 1.9 %collective-permute-start.4 = (f32[256,256]{1,0:T(8,128)S(1)}, f32[256,256]{1,0:T(8,128)S(1)}, u32[]{:S(2)}, u32[]{:S(2)}) collective-permute-start(f32[256,256]{1,0:T(8,128)S(1)} %get-tuple-element.27.refs_0_), channel_id=1, source_target_pairs={{0,8},{1,9},{2,10},{3,11},{4,12},{5,13},{6,14},{7,15},{8,0},{9,1},... | collective-permute-start | bytes 786440 | tf_op jit(solution)/shard_map/ppermute | solution.py:265
  36.9 3.8 %collective-permute-done.5.refs_2_ = f32[256,256]{1,0:T(8,128)S(1)} collective-permute-done((f32[256,256]{1,0:T(8,128)S(1)}, f32[256,256]{1,0:T(8,128)S(1)}, u32[]{:S(2)}, u32[]{:S(2)}) %collective-permute-start.5) | collective-permute-done | bytes 262176 | tf_op jit(solution)/shard_map/ppermute | solution.py:265
  40.7 1.9 %collective-permute-done.4.refs_1_ = f32[256,256]{1,0:T(8,128)S(1)} collective-permute-done((f32[256,256]{1,0:T(8,128)S(1)}, f32[256,256]{1,0:T(8,128)S(1)}, u32[]{:S(2)}, u32[]{:S(2)}) %collective-permute-start.4) | collective-permute-done | bytes 262176 | tf_op jit(solution)/shard_map/ppermute | solution.py:265
  43.1 5.7 %collective-permute-start.11 = (f32[768,256]{1,0:T(8,128)}, f32[768,256]{1,0:T(8,128)}, u32[]{:S(2)}, u32[]{:S(2)}) collective-permute-start(f32[768,256]{1,0:T(8,128)} %slice.10), channel_id=1, source_target_pairs={{0,4},{1,5},{2,6},{8,12},{9,13},{10,14},{16,20},{17,21},{18,22},{2... | collective-permute-start | bytes 2359304 | tf_op jit(solution)/shard_map/ppermute | solution.py:265
  48.9 3.6 %collective-permute-start.14 = (f32[256,512]{1,0:T(8,128)S(1)}, f32[256,512]{1,0:T(8,128)}, u32[]{:S(2)}, u32[]{:S(2)}) collective-permute-start(f32[256,512]{1,0:T(8,128)S(1)} %slice.11.refs_4_), channel_id=1, source_target_pairs={{0,24},{1,25},{2,26},{3,27},{4,28},{5,29},{6,30},{7,31},{8,16},{9,... | collective-permute-start | bytes 1572872 | tf_op jit(solution)/shard_map/ppermute | solution.py:265
  52.4 1.9 %collective-permute-start.13 = (f32[256,512]{1,0:T(8,128)S(1)}, f32[256,512]{1,0:T(8,128)}, u32[]{:S(2)}, u32[]{:S(2)}) collective-permute-start(f32[256,512]{1,0:T(8,128)S(1)} %slice.11.refs_4_), channel_id=1, source_target_pairs={{0,16},{1,17},{2,18},{3,19},{4,20},{5,21},{6,22},{7,23},{8,24},{9,... | collective-permute-start | bytes 1572872 | tf_op jit(solution)/shard_map/ppermute | solution.py:265
  54.4 1.9 %collective-permute-start.12 = (f32[256,512]{1,0:T(8,128)S(1)}, f32[256,512]{1,0:T(8,128)}, u32[]{:S(2)}, u32[]{:S(2)}) collective-permute-start(f32[256,512]{1,0:T(8,128)S(1)} %slice.11.refs_4_), channel_id=1, source_target_pairs={{0,8},{1,9},{2,10},{3,11},{4,12},{5,13},{6,14},{7,15},{8,0},{9,1},... | collective-permute-start | bytes 1572872 | tf_op jit(solution)/shard_map/ppermute | solution.py:265
  59.0 13.0 %factor_panels.2 = (f32[1,256,256]{2,1,0:T(8,128)}, f32[768,768]{1,0:T(8,128)}) custom-call(s32[2]{0:T(128)} %pad_add_fusion.place_ref, f32[256,256]{1,0:T(8,128)} %copy-done.4, f32[256,256]{1,0:T(8,128)} %copy-done.6, f32[256,256]{1,0:T(8,128)} %copy-done.5, f32[256,256]{1,0:T(8,128)} %collective-permute-done.6.refs_3_, f32[256,256]{1,0:T(8,128)} %copy-done.8, ...), custom_call_target="tpu_custom_call" | custom-call | flops 1000 | bytes 1000 | tf_op jit(solution)/shard_map/factor_panels/pallas_call | solution.py:164
  72.0 1.7 %collective-permute-done.13.refs_6_ = f32[256,512]{1,0:T(8,128)} collective-permute-done((f32[256,512]{1,0:T(8,128)S(1)}, f32[256,512]{1,0:T(8,128)}, u32[]{:S(2)}, u32[]{:S(2)}) %collective-permute-start.13) | collective-permute-done | bytes 524320 | tf_op jit(solution)/shard_map/ppermute | solution.py:265
  73.7 1.1 collective-permute-done.12.refs_5_
  74.8 1.3 %broadcast_select_fusion.refs_0_ = f32[768,256]{1,0:T(8,128)S(1)} fusion(f32[768,256]{1,0:T(8,128)} %collective-permute-done.11, f32[768,256]{1,0:T(8,128)} %slice.10, pred[]{:T(512)S(6)} %eq.60), kind=kLoop, calls=%fused_computation.1 | loop fusion | flops 196608 | bytes 2359297 | tf_op jit(solution)/shard_map/jit(_where)/select_n | solution.py:321
  76.1 2.5 %collective-permute-start.15 = (f32[768,256]{1,0:T(8,128)S(1)}, f32[768,256]{1,0:T(8,128)S(1)}, u32[]{:S(2)}, u32[]{:S(2)}) collective-permute-start(f32[768,256]{1,0:T(8,128)S(1)} %broadcast_select_fusion.refs_0_), channel_id=1, source_target_pairs={{0,2},{1,3},{2,0},{8,10},{9,11},{10,8},{16,18},{17,19},{18,16},{24... | collective-permute-start | bytes 2359304 | tf_op jit(solution)/shard_map/ppermute | solution.py:265
  78.7 15.8 %factor_panels.3 = (f32[2,256,256]{2,1,0:T(8,128)S(1)}, f32[768,768]{1,0:T(8,128)S(1)}) custom-call(s32[2]{0:T(128)S(1)} %copy-done.2, f32[768,768]{1,0:T(8,128)S(1)} %copy-done), custom_call_target="tpu_custom_call" | custom-call | flops 1000 | bytes 1000 | tf_op jit(solution)/shard_map/factor_panels/pallas_call | solution.py:164
  95.8 2.5 %collective-permute-done.16.top_other_ref = f32[2,256,256]{2,1,0:T(8,128)S(1)} collective-permute-done((f32[2,256,256]{2,1,0:T(8,128)S(1)}, f32[2,256,256]{2,1,0:T(8,128)S(1)}, u32[]{:S(2)}, u32[]{:S(2)}) %collective-permute-start.16) | collective-permute-done | bytes 524320 | tf_op jit(solution)/shard_map/ppermute | solution.py:265
  98.3 19.5 %update.1 = f32[1024,512]{1,0:T(8,128)} custom-call(s32[2]{0:T(128)S(1)} %copy-done.2, f32[1,256,256]{2,1,0:T(8,128)S(1)} %copy-done.3, f32[2,256,256]{2,1,0:T(8,128)S(1)} %get-tuple-element.41.late_ref, f32[768,768]{1,0:T(8,128)S(1)} %get-tuple-element.42.head_ref, f32[2,256,256]{2,1,0:T(8,128)S(1)} %pad_maximum_fusion.top_ref, ...), custom_call_target="tpu_custom_call" | custom-call | flops 10000000000 | bytes 10000000 | tf_op jit(solution)/shard_map/update/pallas_call | solution.py:241
  (46 shorter events, 8.2 us)
Async XLA Ops:
  0.0 35.8 %copy-start.1 = (f32[1024,512]{1,0:T(8,128)S(1)}, f32[1024,512]{1,0:T(8,128)}, u32[]{:S(2)}) copy-start(f32[1024,512]{1,0:T(8,128)} %refs_8_.1) | copy-start | bytes 6291460
  1.1 11.0 %collective-permute-start.3 = (f32[256,256]{1,0:T(8,128)S(1)}, f32[256,256]{1,0:T(8,128)S(1)}, u32[]{:S(2)}, u32[]{:S(2)}) collective-permute-start(f32[256,256]{1,0:T(8,128)S(1)} %slice.9), channel_id=1, source_target_pairs={{18,19}} | collective-permute-start | bytes 786440 | tf_op jit(solution)/shard_map/ppermute | solution.py:265
  1.8 13.7 %collective-permute-start.2 = (f32[256,256]{1,0:T(8,128)S(1)}, f32[256,256]{1,0:T(8,128)S(1)}, u32[]{:S(2)}, u32[]{:S(2)}) collective-permute-start(f32[256,256]{1,0:T(8,128)S(1)} %slice.9), channel_id=1, source_target_pairs={{0,6},{1,7},{10,8},{9,15},{16,22},{18,17},{24,30},{25,31},{26,24}} | collective-permute-start | bytes 786440 | tf_op jit(solution)/shard_map/ppermute | solution.py:265
  8.8 12.3 %collective-permute-start.1 = (f32[256,256]{1,0:T(8,128)S(1)}, f32[256,256]{1,0:T(8,128)S(1)}, u32[]{:S(2)}, u32[]{:S(2)}) collective-permute-start(f32[256,256]{1,0:T(8,128)S(1)} %slice.9), channel_id=1, source_target_pairs={{0,4},{1,5},{10,14},{9,13},{16,20},{18,23},{24,28},{25,29},{26,30}} | collective-permute-start | bytes 786440 | tf_op jit(solution)/shard_map/ppermute | solution.py:265
  10.1 15.5 %collective-permute-start = (f32[256,256]{1,0:T(8,128)S(1)}, f32[256,256]{1,0:T(8,128)}, u32[]{:S(2)}, u32[]{:S(2)}) collective-permute-start(f32[256,256]{1,0:T(8,128)S(1)} %slice.9), channel_id=1, source_target_pairs={{0,2},{1,3},{10,12},{9,11},{16,18},{18,21},{24,26},{25,27},{26,28}} | collective-permute-start | bytes 786440 | tf_op jit(solution)/shard_map/ppermute | solution.py:265
  26.8 32.2 %copy-start.4 = (f32[256,256]{1,0:T(8,128)}, f32[256,256]{1,0:T(8,128)S(1)}, u32[]{:S(2)}) copy-start(f32[256,256]{1,0:T(8,128)S(1)} %get-tuple-element.27.refs_0_) | copy-start | bytes 786436
  26.8 10.1 %collective-permute-start.6 = (f32[256,256]{1,0:T(8,128)S(1)}, f32[256,256]{1,0:T(8,128)}, u32[]{:S(2)}, u32[]{:S(2)}) collective-permute-start(f32[256,256]{1,0:T(8,128)S(1)} %get-tuple-element.27.refs_0_), channel_id=1, source_target_pairs={{0,24},{1,25},{2,26},{3,27},{4,28},{5,29},{6,30},{7,31},{8,16},{9,... | collective-permute-start | bytes 786440 | tf_op jit(solution)/shard_map/ppermute | solution.py:265
  31.9 8.8 %collective-permute-start.5 = (f32[256,256]{1,0:T(8,128)S(1)}, f32[256,256]{1,0:T(8,128)S(1)}, u32[]{:S(2)}, u32[]{:S(2)}) collective-permute-start(f32[256,256]{1,0:T(8,128)S(1)} %get-tuple-element.27.refs_0_), channel_id=1, source_target_pairs={{0,16},{1,17},{2,18},{3,19},{4,20},{5,21},{6,22},{7,23},{8,24},{9,... | collective-permute-start | bytes 786440 | tf_op jit(solution)/shard_map/ppermute | solution.py:265
  33.8 8.8 %collective-permute-start.4 = (f32[256,256]{1,0:T(8,128)S(1)}, f32[256,256]{1,0:T(8,128)S(1)}, u32[]{:S(2)}, u32[]{:S(2)}) collective-permute-start(f32[256,256]{1,0:T(8,128)S(1)} %get-tuple-element.27.refs_0_), channel_id=1, source_target_pairs={{0,8},{1,9},{2,10},{3,11},{4,12},{5,13},{6,14},{7,15},{8,0},{9,1},... | collective-permute-start | bytes 786440 | tf_op jit(solution)/shard_map/ppermute | solution.py:265
  42.6 13.7 %copy-start.6 = (f32[256,256]{1,0:T(8,128)}, f32[256,256]{1,0:T(8,128)S(1)}, u32[]{:S(2)}) copy-start(f32[256,256]{1,0:T(8,128)S(1)} %collective-permute-done.4.refs_1_) | copy-start | bytes 786436
  42.6 9.8 %collective-permute-start.7 = (f32[256,256]{1,0:T(8,128)S(1)}, f32[256,256]{1,0:T(8,128)S(1)}, u32[]{:S(2)}, u32[]{:S(2)}) collective-permute-start(f32[256,256]{1,0:T(8,128)S(1)} %get-tuple-element.27.refs_0_), channel_id=1, source_target_pairs={{0,1},{1,0},{2,3},{3,2},{4,5},{5,4},{6,7},{7,6},{8,9},{9,8},{10,11... | collective-permute-start | bytes 786440 | tf_op jit(solution)/shard_map/ppermute | solution.py:265
  42.6 11.7 %collective-permute-start.8 = (f32[256,256]{1,0:T(8,128)S(1)}, f32[256,256]{1,0:T(8,128)S(1)}, u32[]{:S(2)}, u32[]{:S(2)}) collective-permute-start(f32[256,256]{1,0:T(8,128)S(1)} %collective-permute-done.4.refs_1_), channel_id=1, source_target_pairs={{0,1},{1,0},{2,3},{3,2},{4,5},{5,4},{6,7},{7,6},{8,9},{9,8},{10,11... | collective-permute-start | bytes 786440 | tf_op jit(solution)/shard_map/ppermute | solution.py:265
  43.1 31.7 %collective-permute-start.11 = (f32[768,256]{1,0:T(8,128)}, f32[768,256]{1,0:T(8,128)}, u32[]{:S(2)}, u32[]{:S(2)}) collective-permute-start(f32[768,256]{1,0:T(8,128)} %slice.10), channel_id=1, source_target_pairs={{0,4},{1,5},{2,6},{8,12},{9,13},{10,14},{16,20},{17,21},{18,22},{2... | collective-permute-start | bytes 2359304 | tf_op jit(solution)/shard_map/ppermute | solution.py:265
  48.8 7.5 %collective-permute-start.9 = (f32[256,256]{1,0:T(8,128)S(1)}, f32[256,256]{1,0:T(8,128)S(1)}, u32[]{:S(2)}, u32[]{:S(2)}) collective-permute-start(f32[256,256]{1,0:T(8,128)S(1)} %collective-permute-done.5.refs_2_), channel_id=1, source_target_pairs={{0,1},{1,0},{2,3},{3,2},{4,5},{5,4},{6,7},{7,6},{8,9},{9,8},{10,11... | collective-permute-start | bytes 786440 | tf_op jit(solution)/shard_map/ppermute | solution.py:265
  48.9 23.1 %collective-permute-start.14 = (f32[256,512]{1,0:T(8,128)S(1)}, f32[256,512]{1,0:T(8,128)}, u32[]{:S(2)}, u32[]{:S(2)}) collective-permute-start(f32[256,512]{1,0:T(8,128)S(1)} %slice.11.refs_4_), channel_id=1, source_target_pairs={{0,24},{1,25},{2,26},{3,27},{4,28},{5,29},{6,30},{7,31},{8,16},{9,... | collective-permute-start | bytes 1572872 | tf_op jit(solution)/shard_map/ppermute | solution.py:265
  52.4 21.3 %collective-permute-start.13 = (f32[256,512]{1,0:T(8,128)S(1)}, f32[256,512]{1,0:T(8,128)}, u32[]{:S(2)}, u32[]{:S(2)}) collective-permute-start(f32[256,512]{1,0:T(8,128)S(1)} %slice.11.refs_4_), channel_id=1, source_target_pairs={{0,16},{1,17},{2,18},{3,19},{4,20},{5,21},{6,22},{7,23},{8,24},{9,... | collective-permute-start | bytes 1572872 | tf_op jit(solution)/shard_map/ppermute | solution.py:265
  54.4 20.5 %collective-permute-start.12 = (f32[256,512]{1,0:T(8,128)S(1)}, f32[256,512]{1,0:T(8,128)}, u32[]{:S(2)}, u32[]{:S(2)}) collective-permute-start(f32[256,512]{1,0:T(8,128)S(1)} %slice.11.refs_4_), channel_id=1, source_target_pairs={{0,8},{1,9},{2,10},{3,11},{4,12},{5,13},{6,14},{7,15},{8,0},{9,1},... | collective-permute-start | bytes 1572872 | tf_op jit(solution)/shard_map/ppermute | solution.py:265
  57.1 1.9 %collective-permute-start.10 = (f32[256,256]{1,0:T(8,128)}, f32[256,256]{1,0:T(8,128)}, u32[]{:S(2)}, u32[]{:S(2)}) collective-permute-start(f32[256,256]{1,0:T(8,128)} %collective-permute-done.6.refs_3_), channel_id=1, source_target_pairs={{0,1},{1,0},{2,3},{3,2},{4,5},{5,4},{6,7},{7,6},{8,9},{9,8},{10,11... | collective-permute-start | bytes 786440 | tf_op jit(solution)/shard_map/ppermute | solution.py:265
  58.0 20.8 %copy-start.2 = (s32[2]{0:T(128)S(1)}, s32[2]{0:T(128)}, u32[]{:S(2)}) copy-start(s32[2]{0:T(128)} %pad_add_fusion.place_ref) | copy-start | bytes 28
  74.8 23.5 %copy-start.3 = (f32[1,256,256]{2,1,0:T(8,128)S(1)}, f32[1,256,256]{2,1,0:T(8,128)}, u32[]{:S(2)}) copy-start(f32[1,256,256]{2,1,0:T(8,128)} %get-tuple-element.31.early_ref) | copy-start | bytes 786436
  76.1 19.1 %collective-permute-start.15 = (f32[768,256]{1,0:T(8,128)S(1)}, f32[768,256]{1,0:T(8,128)S(1)}, u32[]{:S(2)}, u32[]{:S(2)}) collective-permute-start(f32[768,256]{1,0:T(8,128)S(1)} %broadcast_select_fusion.refs_0_), channel_id=1, source_target_pairs={{0,2},{1,3},{2,0},{8,10},{9,11},{10,8},{16,18},{17,19},{18,16},{24... | collective-permute-start | bytes 2359304 | tf_op jit(solution)/shard_map/ppermute | solution.py:265
  78.6 19.7 %collective-permute-start.17 = (f32[768,256]{1,0:T(8,128)S(1)}, f32[768,256]{1,0:T(8,128)S(1)}, u32[]{:S(2)}, u32[]{:S(2)}) collective-permute-start(f32[768,256]{1,0:T(8,128)S(1)} %broadcast_select_fusion.refs_0_), channel_id=1, source_target_pairs={{0,1},{1,0},{2,3},{3,2},{4,5},{5,4},{6,7},{7,6},{8,9},{9,8},{10,11... | collective-permute-start | bytes 2359304 | tf_op jit(solution)/shard_map/ppermute | solution.py:265
  95.3 3.0 %collective-permute-start.18 = (f32[768,256]{1,0:T(8,128)S(1)}, f32[768,256]{1,0:T(8,128)S(1)}, u32[]{:S(2)}, u32[]{:S(2)}) collective-permute-start(f32[768,256]{1,0:T(8,128)S(1)} %collective-permute-done.15.refs_2_), channel_id=1, source_target_pairs={{0,1},{1,0},{2,3},{3,2},{4,5},{5,4},{6,7},{7,6},{8,9},{9,8},{10,11... | collective-permute-start | bytes 2359304 | tf_op jit(solution)/shard_map/ppermute | solution.py:265
  95.3 3.0 %collective-permute-start.16 = (f32[2,256,256]{2,1,0:T(8,128)S(1)}, f32[2,256,256]{2,1,0:T(8,128)S(1)}, u32[]{:S(2)}, u32[]{:S(2)}) collective-permute-start(f32[2,256,256]{2,1,0:T(8,128)S(1)} %pad_maximum_fusion.top_ref), channel_id=1, source_target_pairs={{0,1},{1,0},{2,3},{3,2},{4,5},{5,4},{6,7},{7,6},{8,9},{9,8},{10,11... | collective-permute-start | bytes 1572872 | tf_op jit(solution)/shard_map/ppermute | solution.py:265
  (6 other events, 27.8 us)

commit v3 on v2

--- a/solution.py
+++ b/solution.py
@@ -12,6 +12,7 @@
 HALF = 128
 TILE = 8
 STEP = 16
+EARLY = 3
 HEAD = PANELS * NB
 MIB = 1024 * 1024
 
@@ -67,7 +68,7 @@
             pivots.append((a, b, c, det, inverse))
             if k == 0:
                 zero = jnp.minimum(jnp.abs(inverse), 0.0)
-                for t in range(after, count):
+                for t in range(after, min(after + wide, count)):
                     below[t] = [lane(tiles[t] + zero, start + j) for j in range(STEP)]
             one = [column[k][e] * c - column[k + 1][e] * b for e in range(wide)]
             two = [column[k + 1][e] * a - column[k][e] * b for e in range(wide)]
@@ -97,8 +98,18 @@
                 a, b, c, _, inverse = pivots[k // 2]
                 x, y = sublane(solved[o], i), sublane(solved[o], i + 1)
                 right += [(x * c - y * b) * inverse, (y * a - x * b) * inverse]
-            for t in range(after, count):
+            for t in below:
                 tiles[t] = jnp.where(own, 0.0, tiles[t]) - total([below[t][k] * right[k] for k in range(STEP)])
+            far = after + wide
+            if far < count:
+                packed = [jnp.zeros_like(tiles[0])] * count
+                for e in range(wide):
+                    packed[step + e] = right[TILE * e]
+                    for i in range(1, TILE):
+                        packed[step + e] = jnp.where(rows == i, right[TILE * e + i], packed[step + e])
+                product = dot_nn(jnp.concatenate(tiles[far:], axis=0), jnp.concatenate(packed, axis=0))
+                for t in range(far, count):
+                    tiles[t] = jnp.where(own, 0.0, tiles[t]) - product[TILE * (t - far) : TILE * (t - far + 1)]
         for e in range(wide):
             diagonal, within = jnp.ones_like(forward[e]), jnp.zeros_like(forward[e])
             for i in range(0, TILE, 2):
@@ -132,25 +143,21 @@
         work[...] = refs[0][...]
     low = lax.broadcasted_iota(jnp.int32, (HALF, HALF), 0) >= lax.broadcasted_iota(jnp.int32, (HALF, HALF), 1)
 
-    @pl.loop(2 * begin, 2 * end)
-    def _(at):
-        here = pl.ds(pl.multiple_of(at * HALF, HALF), HALF)
-        tiles = [work[pl.ds(pl.multiple_of(at * HALF + TILE * i, TILE), TILE), here] for i in range(HALF // TILE)]
+    for at in range(2 * begin, 2 * end):
+        left, right = at * HALF, (at + 1) * HALF
+        block = work[left:right, left:right]
+        tiles = [block[TILE * i : TILE * (i + 1)] for i in range(HALF // TILE)]
         inverse = jnp.where(low, jnp.concatenate(invert_factor(tiles), axis=0), 0.0)
-        diagonal = pl.ds(pl.multiple_of((at % 2) * HALF, HALF), HALF)
+        diagonal = slice((at % 2) * HALF, (at % 2 + 1) * HALF)
         inverse_ref[at // 2 - begin, diagonal, diagonal] = inverse
-        work[here, here] = jnp.where(low, dot_nt(work[here, here], inverse), 0.0)
-        for step in range(2 * begin, min(2 * end, HEAD // HALF - 1)):
-
-            @pl.when(at == step)
-            def _():
-                after = (step + 1) * HALF
-                solved = dot_nt(work[after:, step * HALF : after], inverse)
-                work[after:, step * HALF : after] = solved
-                for left in range(after, HEAD, HALF):
-                    right = left + HALF
-                    part = solved[left - after :]
-                    work[left:, left:right] = work[left:, left:right] - dot_nt(part, part[:HALF])
+        work[left:right, left:right] = jnp.where(low, dot_nt(block, inverse), 0.0)
+        if right < HEAD:
+            solved = dot_nt(work[right:, left:right], inverse)
+            work[right:, left:right] = solved
+            for column in range(right, HEAD, HALF):
+                part = solved[column - right :]
+                part = work[column:, column : column + HALF] - dot_nt(part, part[:HALF])
+                work[column:, column : column + HALF] = part
 
     for k in range(begin, end):
         first, second = inverse_ref[k - begin, :HALF, :HALF], inverse_ref[k - begin, HALF:, HALF:]
@@ -175,29 +182,48 @@
     )(place, *blocks)
 
 
-def update_kernel(grid_rows, place_ref, early_ref, late_ref, head_ref, top_ref, top_other_ref, *refs):
-    (held_ref, held_other_ref, swapped_ref, swapped_other_ref), heads = refs[:4], refs[4:-4]
-    matrix_ref, out_ref, across, solved = refs[-4:]
-    my_row, my_col = place_ref[0], place_ref[1]
-    plane, core = my_col // 2, my_col % 2
-    slot = pl.program_id(0)
-    row = my_row + grid_rows * slot
-    col_slots = out_ref.shape[1] // NB
+def across_kernel(place_ref, early_ref, late_ref, head_ref, *refs):
+    heads, across = refs[:-1], refs[-1]
+    inverse, lower = head_blocks(early_ref, late_ref, head_ref)
+    for j in range(PANELS):
+        raw = heads[0][...]
+        for d in range(1, len(heads)):
+            raw = jnp.where((place_ref[0] ^ j) == d, heads[d][...], raw)
+        for i in range(j):
+            raw = raw - dot_nn(lower[j, i][...], across[i * NB : (i + 1) * NB])
+        across[j * NB : (j + 1) * NB] = dot_nn(inverse[j][...], raw)
+
+
+def head_blocks(early_ref, late_ref, head_ref):
     inverse = (early_ref.at[0], late_ref.at[0], late_ref.at[1])
     lower = {
         (i, j): head_ref.at[i * NB : (i + 1) * NB, j * NB : (j + 1) * NB] for i, j in ((1, 0), (2, 0), (2, 1))
     }
-
-    @pl.when(slot == 0)
+    return inverse, lower
+
+
+def solve_across(place, early, late, head, heads):
+    whole = pl.BlockSpec(memory_space=pltpu.VMEM)
+    return pl.pallas_call(
+        across_kernel,
+        out_shape=jax.ShapeDtypeStruct((HEAD, heads[0].shape[1]), jnp.float32),
+        in_specs=[pl.BlockSpec(memory_space=pltpu.SMEM)] + [whole] * (3 + len(heads)),
+        out_specs=whole,
+        cost_estimate=pl.CostEstimate(flops=4_000_000_000, bytes_accessed=5_000_000, transcendentals=0),
+        compiler_params=pltpu.CompilerParams(vmem_limit_bytes=(20 if len(heads) <= 4 else 56) * MIB),
+        name="solve_across",
+    )(place, early, late, head, *heads)
+
+
+def update_kernel(grid_rows, place_ref, early_ref, late_ref, head_ref, top_ref, top_other_ref, *refs):
+    held_ref, held_other_ref, swapped_ref, swapped_other_ref, across, matrix_ref, out_ref, solved = refs
+    my_row, my_col = place_ref[0], place_ref[1]
+    plane, core = my_col // 2, my_col % 2
+    step = pl.program_id(0)
+    inverse, lower = head_blocks(early_ref, late_ref, head_ref)
+
+    @pl.when(step == 0)
     def _():
-        for j in range(PANELS):
-            raw = heads[0][...]
-            for d in range(1, grid_rows):
-                raw = jnp.where((my_row ^ j) == d, heads[d][...], raw)
-            for i in range(j):
-                raw = raw - dot_nn(lower[j, i][...], across[i * NB : (i + 1) * NB])
-            across[j * NB : (j + 1) * NB] = dot_nn(inverse[j][...], raw)
-
         def by_core(mine, other):
             return jnp.where(core == 0, mine, other)
 
@@ -212,46 +238,53 @@
             jnp.concatenate([by_core(second, first), by_core(across_core, own)], axis=0),
             jnp.concatenate([third, last], axis=0),
         ]
+        depth = solved.shape[0] // 2
         for j in range(PANELS):
-            rest = raw[j]
-            for i in range(j):
-                rest = rest - dot_nt(solved[:, i * NB : (i + 1) * NB], lower[j, i][...])
-            solved[:, j * NB : (j + 1) * NB] = dot_nt(rest, inverse[j][...])
-
-    mine = solved[pl.ds(pl.multiple_of(slot * NB, NB), NB), :]
+            there = slice(j * NB, (j + 1) * NB)
+            for here in (slice(0, depth), slice(depth, 2 * depth)):
+                rest = raw[j][here]
+                for i in range(j):
+                    rest = rest - dot_nt(solved[here, i * NB : (i + 1) * NB], lower[j, i][...])
+                solved[here, there] = dot_nt(rest, inverse[j][...])
+
+    depth = out_ref.shape[0]
+    product = dot_nn(solved[pl.ds(pl.multiple_of(step * depth, depth), depth), :], across[...])
     head_row = pl.ds(pl.multiple_of(jnp.minimum(my_row, PANELS - 1) * NB, NB), NB)
     head_col = pl.ds(pl.multiple_of(jnp.minimum(my_col, PANELS - 1) * NB, NB), NB)
-    for t in range(col_slots):
-        there = slice(t * NB, (t + 1) * NB)
-        updated = matrix_ref[:, there] - dot_nn(mine, across[:, there])
-        updated = jnp.where(row < PANELS, 0.0, updated)
-        if t == 0:
-            panel = mine[:, :NB]
-            for j in range(1, PANELS):
-                panel = jnp.where(my_col == j, mine[:, j * NB : (j + 1) * NB], panel)
-            factor = jnp.where(my_col <= row, head_ref[head_row, head_col], 0.0)
-            panel = jnp.where(row < PANELS, factor, panel)
-            updated = jnp.where(my_col < PANELS, panel, updated)
-        out_ref[:, there] = updated
-
-
-def update(place, early, late, head, top, top_other, sent, heads, matrix):
+    for block in range(depth // NB):
+        slot = step * (depth // NB) + block
+        row = my_row + grid_rows * slot
+        here = slice(block * NB, (block + 1) * NB)
+        mine = solved[pl.ds(pl.multiple_of(slot * NB, NB), NB), :]
+        for t in range(out_ref.shape[1] // NB):
+            there = slice(t * NB, (t + 1) * NB)
+            updated = matrix_ref[here, there] - product[here, there]
+            updated = jnp.where(row < PANELS, 0.0, updated)
+            if t == 0:
+                panel = mine[:, :NB]
+                for j in range(1, PANELS):
+                    panel = jnp.where(my_col == j, mine[:, j * NB : (j + 1) * NB], panel)
+                factor = jnp.where(my_col <= row, head_ref[head_row, head_col], 0.0)
+                panel = jnp.where(row < PANELS, factor, panel)
+                updated = jnp.where(my_col < PANELS, panel, updated)
+            out_ref[here, there] = updated
+
+
+def update(grid_rows, place, early, late, head, top, top_other, sent, across, matrix):
     whole = pl.BlockSpec(memory_space=pltpu.VMEM)
-    strip = pl.BlockSpec((NB, matrix.shape[1]), lambda slot: (slot, 0))
+    depth = 2 * NB if matrix.shape[0] % (2 * NB) == 0 else NB
+    strip = pl.BlockSpec((depth, matrix.shape[1]), lambda step: (step, 0))
     return pl.pallas_call(
-        functools.partial(update_kernel, len(heads)),
+        functools.partial(update_kernel, grid_rows),
         out_shape=jax.ShapeDtypeStruct(matrix.shape, jnp.float32),
-        grid=(matrix.shape[0] // NB,),
-        in_specs=[pl.BlockSpec(memory_space=pltpu.SMEM)] + [whole] * (5 + len(sent) + len(heads)) + [strip],
+        grid=(matrix.shape[0] // depth,),
+        in_specs=[pl.BlockSpec(memory_space=pltpu.SMEM)] + [whole] * (6 + len(sent)) + [strip],
         out_specs=strip,
-        scratch_shapes=[
-            pltpu.VMEM((HEAD, matrix.shape[1]), jnp.float32),
-            pltpu.VMEM((matrix.shape[0], HEAD), jnp.float32),
-        ],
+        scratch_shapes=[pltpu.VMEM((matrix.shape[0], HEAD), jnp.float32)],
         cost_estimate=pl.CostEstimate(flops=10_000_000_000, bytes_accessed=10_000_000, transcendentals=0),
-        compiler_params=pltpu.CompilerParams(vmem_limit_bytes=(30 if len(heads) <= 4 else 56) * MIB),
+        compiler_params=pltpu.CompilerParams(vmem_limit_bytes=30 * MIB),
         name="update",
-    )(place, early, late, head, top, top_other, *sent, *heads, matrix)
+    )(place, early, late, head, top, top_other, *sent, across, matrix)
 
 
 def body(matrix):
@@ -298,6 +331,8 @@
     carried = jnp.where(native, corner, carried)
     heads = along_rows(matrix[:NB])
     found = along_rows(carried)
+    found, early_heads = lax.optimization_barrier((found, heads[:EARLY]))
+    heads = [*early_heads, *heads[EARLY:]]
     top_mine, top_last = corner, corner
     for d in range(1, planes):
         top_mine = jnp.where(plane == d, passed[d - 1], top_mine)
@@ -329,9 +364,11 @@
     swapped = send(held, pairs)
     held_other, top_other = swap_cores(held), swap_cores(top)
     late, head = factor_panels(1, PANELS, place, head)
-    swapped, late, head = lax.optimization_barrier((swapped, late, head))
-    sent = [held, held_other, swapped, swap_cores(swapped)]
-    return update(place, early, late, head, top, top_other, sent, heads, matrix)
+    across = solve_across(place, early, late, head, heads)
+    swapped, across = lax.optimization_barrier((swapped, across))
+    swapped_other = swap_cores(swapped)
+    sent = [held, held_other, swapped, swapped_other]
+    return update(grid_rows, place, early, late, head, top, top_other, sent, across, matrix)
 
 
 def solution(mesh):

time: 119 us -> 105 us (0.88)
  waiting for transfers between devices: 25.8 us -> 8.48 us
  starting transfers between devices: 36.8 us -> 43.9 us
  Pallas kernels: 48.3 us -> 41.4 us
  local copies, waits for them, and re-layouts: 3.56 us -> 6.11 us
    ppermute x19, waiting for transfers between devices: 25.8 us -> 8.48 us  [send(): return lax.ppermute(x, ('row', 'col'), flat)]
    ppermute x19, starting transfers between devices: 36.8 us -> 43.9 us  [send(): return lax.ppermute(x, ('row', 'col'), flat)]
    pallas_call x2, Pallas kernels: 28.8 us -> 22.5 us  [factor_panels(): pl.pallas_call(functools.partial(head_kernel, begin, end), out_shape=[jax...]
    pallas_call x1 -> x2, Pallas kernels: 19.5 us -> 19 us  [the longest x1 14.1 us: update(): pl.pallas_call(functools.partial(update_kernel, grid_rows), out_shape=jax...]
  transfers between devices with their start and end apart: 19 -> 19, of which waited for: 11 -> 6; matrix products, arithmetic and copies ran while one was open for 1% -> 4% of each run, Pallas kernels for 24% -> 26%
where the time goes in v3:
time: 105 us; the launch traced here: 103 us
  starting transfers between devices  43.9 us (42%)
  Pallas kernels  41.4 us (39%)
  waiting for transfers between devices  8.48 us (8%)
  local copies, waits for them, and re-layouts  6.11 us (6%)
  other arithmetic  3.2 us (3%)
    ppermute x19, starting transfers between devices, send(): return lax.ppermute(x, ('row', 'col'), flat)  43.9 us
    pallas_call x2, Pallas kernels, factor_panels(): pl.pallas_call(functools.partial(head_kernel, begin, end), out_shape=[jax...  22.5 us
    pallas_call x1, Pallas kernels, update(): pl.pallas_call(functools.partial(update_kernel, grid_rows), out_shape=jax...  14.1 us
    ppermute x19, waiting for transfers between devices, send(): return lax.ppermute(x, ('row', 'col'), flat)  8.48 us
    pallas_call x1, Pallas kernels, solve_across(): pl.pallas_call(across_kernel, out_shape=jax.ShapeDtypeStruct((HEAD, heads...  4.89 us
    unnamed x18, local copies, waits for them, and re-layouts  2.27 us
  transfers between devices with their start and end apart: 19, of which 6 were waited for; matrix products, arithmetic and copies ran while one was open for 4% of the time, Pallas kernels for 26%

profile of v3, /device:TPU:0, one launch (start us, length us, event | category | flops | bytes accessed | tf_op | source)
XLA Modules:
  0.0 103.5 jit_solution(1611754969802133625)
XLA Ops:
  0.0 1.8 %slice.9 = f32[256,256]{1,0:T(8,128)} slice(f32[1024,512]{1,0:T(8,128)} %refs_5_.1), slice={[0:256], [0:256]} | slice | bytes 524288 | tf_op jit(solution)/shard_map/slice | solution.py:312
  2.5 7.0 %collective-permute-start.2 = (f32[256,256]{1,0:T(8,128)}, f32[256,256]{1,0:T(8,128)S(1)}, u32[]{:S(2)}, u32[]{:S(2)}) collective-permute-start(f32[256,256]{1,0:T(8,128)} %slice.9), channel_id=1, source_target_pairs={{0,6},{1,7},{10,8},{9,15},{16,22},{18,17},{24,30},{25,31},{26,24}} | collective-permute-start | bytes 786440 | tf_op jit(solution)/shard_map/ppermute | solution.py:298
  9.5 1.3 %collective-permute-start.1 = (f32[256,256]{1,0:T(8,128)}, f32[256,256]{1,0:T(8,128)S(1)}, u32[]{:S(2)}, u32[]{:S(2)}) collective-permute-start(f32[256,256]{1,0:T(8,128)} %slice.9), channel_id=1, source_target_pairs={{0,4},{1,5},{10,14},{9,13},{16,20},{18,23},{24,28},{25,29},{26,30}} | collective-permute-start | bytes 786440 | tf_op jit(solution)/shard_map/ppermute | solution.py:298
  10.8 2.0 %collective-permute-start = (f32[256,256]{1,0:T(8,128)}, f32[256,256]{1,0:T(8,128)}, u32[]{:S(2)}, u32[]{:S(2)}) collective-permute-start(f32[256,256]{1,0:T(8,128)} %slice.9), channel_id=1, source_target_pairs={{0,2},{1,3},{10,12},{9,11},{16,18},{18,21},{24,26},{25,27},{26,28}} | collective-permute-start | bytes 786440 | tf_op jit(solution)/shard_map/ppermute | solution.py:298
  12.8 1.1 %slice.10.refs_0_ = f32[256,512]{1,0:T(8,128)S(1)} slice(f32[1024,512]{1,0:T(8,128)} %refs_5_.1), slice={[0:256], [0:512]} | slice | bytes 1048576 | tf_op jit(solution)/shard_map/slice | solution.py:332
  13.9 3.4 %collective-permute-start.8 = (f32[256,512]{1,0:T(8,128)S(1)}, f32[256,512]{1,0:T(8,128)}, u32[]{:S(2)}, u32[]{:S(2)}) collective-permute-start(f32[256,512]{1,0:T(8,128)S(1)} %slice.10.refs_0_), channel_id=1, source_target_pairs={{0,16},{1,17},{2,18},{3,19},{4,20},{5,21},{6,22},{7,23},{8,24},{9,... | collective-permute-start | bytes 1572872 | tf_op jit(solution)/shard_map/ppermute | solution.py:298
  17.4 5.3 %collective-permute-start.7 = (f32[256,512]{1,0:T(8,128)S(1)}, f32[256,512]{1,0:T(8,128)S(1)}, u32[]{:S(2)}, u32[]{:S(2)}) collective-permute-start(f32[256,512]{1,0:T(8,128)S(1)} %slice.10.refs_0_), channel_id=1, source_target_pairs={{0,8},{1,9},{2,10},{3,11},{4,12},{5,13},{6,14},{7,15},{8,0},{9,1},... | collective-permute-start | bytes 1572872 | tf_op jit(solution)/shard_map/ppermute | solution.py:298
  23.4 3.1 %collective-permute-done = f32[256,256]{1,0:T(8,128)} collective-permute-done((f32[256,256]{1,0:T(8,128)}, f32[256,256]{1,0:T(8,128)}, u32[]{:S(2)}, u32[]{:S(2)}) %collective-permute-start) | collective-permute-done | bytes 262176 | tf_op jit(solution)/shard_map/ppermute | solution.py:298
  26.6 1.2 %select_bitcast_fusion.1 = (f32[1,256,256]{2,1,0:T(8,128)S(1)}, f32[1,256,256]{2,1,0:T(8,128)S(1)}, f32[256,256]{1,0:T(8,128)S(1)}) fusion(f32[256,256]{1,0:T(8,128)S(1)} %collective-permute-done.2, f32[256,256]{1,0:T(8,128)} %copy-done.7, f32[256,256]{1,0:T(8,128)} %collective-permute-done, pred[]{:T(512)S(6)} %eq.56, pred[]{:T(512)S(6)} %eq.55, ...), kind=kLoop, calls=%fused_computation.3 | loop fusion | flops 655360 | bytes 2097159 | tf_op jit(solution)/shard_map/stack | solution.py:340
  27.8 5.1 %collective-permute-start.6 = (f32[256,256]{1,0:T(8,128)S(1)}, f32[256,256]{1,0:T(8,128)}, u32[]{:S(2)}, u32[]{:S(2)}) collective-permute-start(f32[256,256]{1,0:T(8,128)S(1)} %get-tuple-element.37.refs_0_), channel_id=1, source_target_pairs={{0,24},{1,25},{2,26},{3,27},{4,28},{5,29},{6,30},{7,31},{8,16},{9,... | collective-permute-start | bytes 786440 | tf_op jit(solution)/shard_map/ppermute | solution.py:298
  32.9 1.9 %collective-permute-start.5 = (f32[256,256]{1,0:T(8,128)S(1)}, f32[256,256]{1,0:T(8,128)}, u32[]{:S(2)}, u32[]{:S(2)}) collective-permute-start(f32[256,256]{1,0:T(8,128)S(1)} %get-tuple-element.37.refs_0_), channel_id=1, source_target_pairs={{0,16},{1,17},{2,18},{3,19},{4,20},{5,21},{6,22},{7,23},{8,24},{9,... | collective-permute-start | bytes 786440 | tf_op jit(solution)/shard_map/ppermute | solution.py:298
  34.8 1.9 %collective-permute-start.4 = (f32[256,256]{1,0:T(8,128)S(1)}, f32[256,256]{1,0:T(8,128)}, u32[]{:S(2)}, u32[]{:S(2)}) collective-permute-start(f32[256,256]{1,0:T(8,128)S(1)} %get-tuple-element.37.refs_0_), channel_id=1, source_target_pairs={{0,8},{1,9},{2,10},{3,11},{4,12},{5,13},{6,14},{7,15},{8,0},{9,1},... | collective-permute-start | bytes 786440 | tf_op jit(solution)/shard_map/ppermute | solution.py:298
  36.8 1.0 slice.11
  37.7 1.3 %collective-permute-done.6.refs_3_ = f32[256,256]{1,0:T(8,128)} collective-permute-done((f32[256,256]{1,0:T(8,128)S(1)}, f32[256,256]{1,0:T(8,128)}, u32[]{:S(2)}, u32[]{:S(2)}) %collective-permute-start.6) | collective-permute-done | bytes 262176 | tf_op jit(solution)/shard_map/ppermute | solution.py:298
  39.0 4.9 %collective-permute-start.13 = (f32[768,256]{1,0:T(8,128)}, f32[768,256]{1,0:T(8,128)}, u32[]{:S(2)}, u32[]{:S(2)}) collective-permute-start(f32[768,256]{1,0:T(8,128)} %slice.11), channel_id=1, source_target_pairs={{0,4},{1,5},{2,6},{8,12},{9,13},{10,14},{16,20},{17,21},{18,22},{2... | collective-permute-start | bytes 2359304 | tf_op jit(solution)/shard_map/ppermute | solution.py:298
  45.1 5.2 %collective-permute-start.14 = (f32[256,512]{1,0:T(8,128)S(1)}, f32[256,512]{1,0:T(8,128)}, u32[]{:S(2)}, u32[]{:S(2)}) collective-permute-start(f32[256,512]{1,0:T(8,128)S(1)} %slice.10.refs_0_), channel_id=1, source_target_pairs={{0,24},{1,25},{2,26},{3,27},{4,28},{5,29},{6,30},{7,31},{8,16},{9,... | collective-permute-start | bytes 1572872 | tf_op jit(solution)/shard_map/ppermute | solution.py:298
  52.5 0.9 collective-permute-done.12.refs_7_
  53.4 10.4 %factor_panels.2 = (f32[1,256,256]{2,1,0:T(8,128)}, f32[768,768]{1,0:T(8,128)}) custom-call(s32[2]{0:T(128)} %pad_add_fusion.place_ref, f32[256,256]{1,0:T(8,128)} %copy-done.6, f32[256,256]{1,0:T(8,128)} %collective-permute-done.4.refs_1_, f32[256,256]{1,0:T(8,128)} %collective-permute-done.5.refs_2_, f32[256,256]{1,0:T(8,128)} %collective-permute-done.6.refs_3_, ...), custom_call_target="tpu_custom_call" | custom-call | flops 1000 | bytes 1000 | tf_op jit(solution)/shard_map/factor_panels/pallas_call | solution.py:171
  63.8 1.4 %broadcast_select_fusion.refs_0_ = f32[768,256]{1,0:T(8,128)S(1)} fusion(f32[768,256]{1,0:T(8,128)} %collective-permute-done.13, f32[768,256]{1,0:T(8,128)} %slice.11, pred[]{:T(512)S(6)} %eq.60), kind=kLoop, calls=%fused_computation.1 | loop fusion | flops 196608 | bytes 2359297 | tf_op jit(solution)/shard_map/jit(_where)/select_n | solution.py:356
  65.2 3.9 %collective-permute-start.17 = (f32[768,256]{1,0:T(8,128)S(1)}, f32[768,256]{1,0:T(8,128)S(1)}, u32[]{:S(2)}, u32[]{:S(2)}) collective-permute-start(f32[768,256]{1,0:T(8,128)S(1)} %broadcast_select_fusion.refs_0_), channel_id=1, source_target_pairs={{0,2},{1,3},{2,0},{8,10},{9,11},{10,8},{16,18},{17,19},{18,16},{24... | collective-permute-start | bytes 2359304 | tf_op jit(solution)/shard_map/ppermute | solution.py:298
  69.1 12.1 %factor_panels.3 = (f32[2,256,256]{2,1,0:T(8,128)S(1)}, f32[768,768]{1,0:T(8,128)S(1)}) custom-call(s32[2]{0:T(128)S(1)} %copy-done.2, f32[768,768]{1,0:T(8,128)S(1)} %copy-done), custom_call_target="tpu_custom_call" | custom-call | flops 1000 | bytes 1000 | tf_op jit(solution)/shard_map/factor_panels/pallas_call | solution.py:171
  81.3 4.9 %solve_across.1.refs_4_ = f32[768,512]{1,0:T(8,128)S(1)} custom-call(s32[2]{0:T(128)S(1)} %copy-done.2, f32[1,256,256]{2,1,0:T(8,128)S(1)} %copy-done.5, f32[2,256,256]{2,1,0:T(8,128)S(1)} %get-tuple-element.51.late_ref, f32[768,768]{1,0:T(8,128)S(1)} %get-tuple-element.52.head_ref, f32[256,512]{1,0:T(8,128)S(1)} %slice.10.refs_0_, ...), custom_call_target="tpu_custom_call" | custom-call | flops 4000000000 | bytes 5000000 | tf_op jit(solution)/shard_map/solve_across/pallas_call | solution.py:207
  86.8 2.6 %collective-permute-done.15.top_other_ref = f32[2,256,256]{2,1,0:T(8,128)S(1)} collective-permute-done((f32[2,256,256]{2,1,0:T(8,128)S(1)}, f32[2,256,256]{2,1,0:T(8,128)S(1)}, u32[]{:S(2)}, u32[]{:S(2)}) %collective-permute-start.15) | collective-permute-done | bytes 524320 | tf_op jit(solution)/shard_map/ppermute | solution.py:298
  89.4 14.1 %update.1 = f32[1024,512]{1,0:T(8,128)} custom-call(s32[2]{0:T(128)S(1)} %copy-done.2, f32[1,256,256]{2,1,0:T(8,128)S(1)} %copy-done.5, f32[2,256,256]{2,1,0:T(8,128)S(1)} %get-tuple-element.51.late_ref, f32[768,768]{1,0:T(8,128)S(1)} %get-tuple-element.52.head_ref, f32[2,256,256]{2,1,0:T(8,128)S(1)} %pad_maximum_fusion.top_ref, ...), custom_call_target="tpu_custom_call" | custom-call | flops 10000000000 | bytes 10000000 | tf_op jit(solution)/shard_map/update/pallas_call | solution.py:277
  (43 shorter events, 5.6 us)
Async XLA Ops:
  0.0 36.7 %copy-start.1 = (f32[1024,512]{1,0:T(8,128)S(1)}, f32[1024,512]{1,0:T(8,128)}, u32[]{:S(2)}) copy-start(f32[1024,512]{1,0:T(8,128)} %refs_5_.1) | copy-start | bytes 6291460
  1.8 15.6 %collective-permute-start.3 = (f32[256,256]{1,0:T(8,128)}, f32[256,256]{1,0:T(8,128)S(1)}, u32[]{:S(2)}, u32[]{:S(2)}) collective-permute-start(f32[256,256]{1,0:T(8,128)} %slice.9), channel_id=1, source_target_pairs={{18,19}} | collective-permute-start | bytes 786440 | tf_op jit(solution)/shard_map/ppermute | solution.py:298
  2.5 20.2 %collective-permute-start.2 = (f32[256,256]{1,0:T(8,128)}, f32[256,256]{1,0:T(8,128)S(1)}, u32[]{:S(2)}, u32[]{:S(2)}) collective-permute-start(f32[256,256]{1,0:T(8,128)} %slice.9), channel_id=1, source_target_pairs={{0,6},{1,7},{10,8},{9,15},{16,22},{18,17},{24,30},{25,31},{26,24}} | collective-permute-start | bytes 786440 | tf_op jit(solution)/shard_map/ppermute | solution.py:298
  9.5 13.2 %collective-permute-start.1 = (f32[256,256]{1,0:T(8,128)}, f32[256,256]{1,0:T(8,128)S(1)}, u32[]{:S(2)}, u32[]{:S(2)}) collective-permute-start(f32[256,256]{1,0:T(8,128)} %slice.9), channel_id=1, source_target_pairs={{0,4},{1,5},{10,14},{9,13},{16,20},{18,23},{24,28},{25,29},{26,30}} | collective-permute-start | bytes 786440 | tf_op jit(solution)/shard_map/ppermute | solution.py:298
  10.8 15.8 %collective-permute-start = (f32[256,256]{1,0:T(8,128)}, f32[256,256]{1,0:T(8,128)}, u32[]{:S(2)}, u32[]{:S(2)}) collective-permute-start(f32[256,256]{1,0:T(8,128)} %slice.9), channel_id=1, source_target_pairs={{0,2},{1,3},{10,12},{9,11},{16,18},{18,21},{24,26},{25,27},{26,28}} | collective-permute-start | bytes 786440 | tf_op jit(solution)/shard_map/ppermute | solution.py:298
  13.9 30.4 %collective-permute-start.8 = (f32[256,512]{1,0:T(8,128)S(1)}, f32[256,512]{1,0:T(8,128)}, u32[]{:S(2)}, u32[]{:S(2)}) collective-permute-start(f32[256,512]{1,0:T(8,128)S(1)} %slice.10.refs_0_), channel_id=1, source_target_pairs={{0,16},{1,17},{2,18},{3,19},{4,20},{5,21},{6,22},{7,23},{8,24},{9,... | collective-permute-start | bytes 1572872 | tf_op jit(solution)/shard_map/ppermute | solution.py:298
  17.4 26.9 %collective-permute-start.7 = (f32[256,512]{1,0:T(8,128)S(1)}, f32[256,512]{1,0:T(8,128)S(1)}, u32[]{:S(2)}, u32[]{:S(2)}) collective-permute-start(f32[256,512]{1,0:T(8,128)S(1)} %slice.10.refs_0_), channel_id=1, source_target_pairs={{0,8},{1,9},{2,10},{3,11},{4,12},{5,13},{6,14},{7,15},{8,0},{9,1},... | collective-permute-start | bytes 1572872 | tf_op jit(solution)/shard_map/ppermute | solution.py:298
  27.8 25.6 %copy-start.6 = (f32[256,256]{1,0:T(8,128)}, f32[256,256]{1,0:T(8,128)S(1)}, u32[]{:S(2)}) copy-start(f32[256,256]{1,0:T(8,128)S(1)} %get-tuple-element.37.refs_0_) | copy-start | bytes 786436
  27.8 11.2 %collective-permute-start.6 = (f32[256,256]{1,0:T(8,128)S(1)}, f32[256,256]{1,0:T(8,128)}, u32[]{:S(2)}, u32[]{:S(2)}) collective-permute-start(f32[256,256]{1,0:T(8,128)S(1)} %get-tuple-element.37.refs_0_), channel_id=1, source_target_pairs={{0,24},{1,25},{2,26},{3,27},{4,28},{5,29},{6,30},{7,31},{8,16},{9,... | collective-permute-start | bytes 786440 | tf_op jit(solution)/shard_map/ppermute | solution.py:298
  32.9 11.0 %collective-permute-start.5 = (f32[256,256]{1,0:T(8,128)S(1)}, f32[256,256]{1,0:T(8,128)}, u32[]{:S(2)}, u32[]{:S(2)}) collective-permute-start(f32[256,256]{1,0:T(8,128)S(1)} %get-tuple-element.37.refs_0_), channel_id=1, source_target_pairs={{0,16},{1,17},{2,18},{3,19},{4,20},{5,21},{6,22},{7,23},{8,24},{9,... | collective-permute-start | bytes 786440 | tf_op jit(solution)/shard_map/ppermute | solution.py:298
  34.8 9.4 %collective-permute-start.4 = (f32[256,256]{1,0:T(8,128)S(1)}, f32[256,256]{1,0:T(8,128)}, u32[]{:S(2)}, u32[]{:S(2)}) collective-permute-start(f32[256,256]{1,0:T(8,128)S(1)} %get-tuple-element.37.refs_0_), channel_id=1, source_target_pairs={{0,8},{1,9},{2,10},{3,11},{4,12},{5,13},{6,14},{7,15},{8,0},{9,1},... | collective-permute-start | bytes 786440 | tf_op jit(solution)/shard_map/ppermute | solution.py:298
  39.0 24.8 %collective-permute-start.13 = (f32[768,256]{1,0:T(8,128)}, f32[768,256]{1,0:T(8,128)}, u32[]{:S(2)}, u32[]{:S(2)}) collective-permute-start(f32[768,256]{1,0:T(8,128)} %slice.11), channel_id=1, source_target_pairs={{0,4},{1,5},{2,6},{8,12},{9,13},{10,14},{16,20},{17,21},{18,22},{2... | collective-permute-start | bytes 2359304 | tf_op jit(solution)/shard_map/ppermute | solution.py:298
  45.1 5.7 %collective-permute-start.9 = (f32[256,256]{1,0:T(8,128)S(1)}, f32[256,256]{1,0:T(8,128)S(1)}, u32[]{:S(2)}, u32[]{:S(2)}) collective-permute-start(f32[256,256]{1,0:T(8,128)S(1)} %get-tuple-element.37.refs_0_), channel_id=1, source_target_pairs={{0,1},{1,0},{2,3},{3,2},{4,5},{5,4},{6,7},{7,6},{8,9},{9,8},{10,11... | collective-permute-start | bytes 786440 | tf_op jit(solution)/shard_map/ppermute | solution.py:298
  45.1 18.6 %collective-permute-start.14 = (f32[256,512]{1,0:T(8,128)S(1)}, f32[256,512]{1,0:T(8,128)}, u32[]{:S(2)}, u32[]{:S(2)}) collective-permute-start(f32[256,512]{1,0:T(8,128)S(1)} %slice.10.refs_0_), channel_id=1, source_target_pairs={{0,24},{1,25},{2,26},{3,27},{4,28},{5,29},{6,30},{7,31},{8,16},{9,... | collective-permute-start | bytes 1572872 | tf_op jit(solution)/shard_map/ppermute | solution.py:298
  50.2 2.0 %collective-permute-start.10 = (f32[256,256]{1,0:T(8,128)}, f32[256,256]{1,0:T(8,128)}, u32[]{:S(2)}, u32[]{:S(2)}) collective-permute-start(f32[256,256]{1,0:T(8,128)} %collective-permute-done.4.refs_1_), channel_id=1, source_target_pairs={{0,1},{1,0},{2,3},{3,2},{4,5},{5,4},{6,7},{7,6},{8,9},{9,8},{10,11... | collective-permute-start | bytes 786440 | tf_op jit(solution)/shard_map/ppermute | solution.py:298
  50.5 2.0 %collective-permute-start.11 = (f32[256,256]{1,0:T(8,128)}, f32[256,256]{1,0:T(8,128)}, u32[]{:S(2)}, u32[]{:S(2)}) collective-permute-start(f32[256,256]{1,0:T(8,128)} %collective-permute-done.5.refs_2_), channel_id=1, source_target_pairs={{0,1},{1,0},{2,3},{3,2},{4,5},{5,4},{6,7},{7,6},{8,9},{9,8},{10,11... | collective-permute-start | bytes 786440 | tf_op jit(solution)/shard_map/ppermute | solution.py:298
  51.5 1.9 %collective-permute-start.12 = (f32[256,256]{1,0:T(8,128)}, f32[256,256]{1,0:T(8,128)}, u32[]{:S(2)}, u32[]{:S(2)}) collective-permute-start(f32[256,256]{1,0:T(8,128)} %collective-permute-done.6.refs_3_), channel_id=1, source_target_pairs={{0,1},{1,0},{2,3},{3,2},{4,5},{5,4},{6,7},{7,6},{8,9},{9,8},{10,11... | collective-permute-start | bytes 786440 | tf_op jit(solution)/shard_map/ppermute | solution.py:298
  52.3 16.9 %copy-start.2 = (s32[2]{0:T(128)S(1)}, s32[2]{0:T(128)}, u32[]{:S(2)}) copy-start(s32[2]{0:T(128)} %pad_add_fusion.place_ref) | copy-start | bytes 28
  63.7 17.5 %copy-start.4 = (f32[256,512]{1,0:T(8,128)S(1)}, f32[256,512]{1,0:T(8,128)}, u32[]{:S(2)}) copy-start(f32[256,512]{1,0:T(8,128)} %copy-done.3) | copy-start | bytes 1572868
  63.8 17.5 %copy-start.5 = (f32[1,256,256]{2,1,0:T(8,128)S(1)}, f32[1,256,256]{2,1,0:T(8,128)}, u32[]{:S(2)}) copy-start(f32[1,256,256]{2,1,0:T(8,128)} %get-tuple-element.41.early_ref) | copy-start | bytes 786436
  65.2 21.0 %collective-permute-start.17 = (f32[768,256]{1,0:T(8,128)S(1)}, f32[768,256]{1,0:T(8,128)S(1)}, u32[]{:S(2)}, u32[]{:S(2)}) collective-permute-start(f32[768,256]{1,0:T(8,128)S(1)} %broadcast_select_fusion.refs_0_), channel_id=1, source_target_pairs={{0,2},{1,3},{2,0},{8,10},{9,11},{10,8},{16,18},{17,19},{18,16},{24... | collective-permute-start | bytes 2359304 | tf_op jit(solution)/shard_map/ppermute | solution.py:298
  69.0 20.4 %collective-permute-start.16 = (f32[768,256]{1,0:T(8,128)S(1)}, f32[768,256]{1,0:T(8,128)S(1)}, u32[]{:S(2)}, u32[]{:S(2)}) collective-permute-start(f32[768,256]{1,0:T(8,128)S(1)} %broadcast_select_fusion.refs_0_), channel_id=1, source_target_pairs={{0,1},{1,0},{2,3},{3,2},{4,5},{5,4},{6,7},{7,6},{8,9},{9,8},{10,11... | collective-permute-start | bytes 2359304 | tf_op jit(solution)/shard_map/ppermute | solution.py:298
  86.2 3.2 %collective-permute-start.18 = (f32[768,256]{1,0:T(8,128)S(1)}, f32[768,256]{1,0:T(8,128)S(1)}, u32[]{:S(2)}, u32[]{:S(2)}) collective-permute-start(f32[768,256]{1,0:T(8,128)S(1)} %collective-permute-done.17.refs_2_), channel_id=1, source_target_pairs={{0,1},{1,0},{2,3},{3,2},{4,5},{5,4},{6,7},{7,6},{8,9},{9,8},{10,11... | collective-permute-start | bytes 2359304 | tf_op jit(solution)/shard_map/ppermute | solution.py:298
  86.7 2.7 %collective-permute-start.15 = (f32[2,256,256]{2,1,0:T(8,128)S(1)}, f32[2,256,256]{2,1,0:T(8,128)S(1)}, u32[]{:S(2)}, u32[]{:S(2)}) collective-permute-start(f32[2,256,256]{2,1,0:T(8,128)S(1)} %pad_maximum_fusion.top_ref), channel_id=1, source_target_pairs={{0,1},{1,0},{2,3},{3,2},{4,5},{5,4},{6,7},{7,6},{8,9},{9,8},{10,11... | collective-permute-start | bytes 1572872 | tf_op jit(solution)/shard_map/ppermute | solution.py:298
  (4 other events, 7.6 us)

commit v4 on v3

--- a/solution.py
+++ b/solution.py
@@ -140,16 +140,19 @@
         count = (len(refs) - 2) // 2
         assemble(place_ref[0], place_ref[1] % 2, refs[:count], refs[count : 2 * count], work)
     else:
-        work[...] = refs[0][...]
+        inverse_ref[0, :HALF, :HALF] = refs[0][...]
+        work[...] = refs[1][...]
     low = lax.broadcasted_iota(jnp.int32, (HALF, HALF), 0) >= lax.broadcasted_iota(jnp.int32, (HALF, HALF), 1)
-
-    for at in range(2 * begin, 2 * end):
+    for at in range(begin, end):
         left, right = at * HALF, (at + 1) * HALF
         block = work[left:right, left:right]
         tiles = [block[TILE * i : TILE * (i + 1)] for i in range(HALF // TILE)]
         inverse = jnp.where(low, jnp.concatenate(invert_factor(tiles), axis=0), 0.0)
-        diagonal = slice((at % 2) * HALF, (at % 2 + 1) * HALF)
-        inverse_ref[at // 2 - begin, diagonal, diagonal] = inverse
+        if begin == 0:
+            inverse_ref[...] = inverse
+        else:
+            diagonal = slice((at % 2) * HALF, (at % 2 + 1) * HALF)
+            inverse_ref[at // 2, diagonal, diagonal] = inverse
         work[left:right, left:right] = jnp.where(low, dot_nt(block, inverse), 0.0)
         if right < HEAD:
             solved = dot_nt(work[right:, left:right], inverse)
@@ -158,33 +161,33 @@
                 part = solved[column - right :]
                 part = work[column:, column : column + HALF] - dot_nt(part, part[:HALF])
                 work[column:, column : column + HALF] = part
-
-    for k in range(begin, end):
-        first, second = inverse_ref[k - begin, :HALF, :HALF], inverse_ref[k - begin, HALF:, HALF:]
-        below = work[k * NB + HALF : (k + 1) * NB, k * NB : k * NB + HALF]
-        inverse_ref[k - begin, HALF:, :HALF] = -dot_nn(second, dot_nn(below, first))
-        inverse_ref[k - begin, :HALF, HALF:] = jnp.zeros((HALF, HALF), jnp.float32)
-        work[k * NB : k * NB + HALF, k * NB + HALF : (k + 1) * NB] = jnp.zeros((HALF, HALF), jnp.float32)
-
-
-def factor_panels(begin, end, place, *blocks):
+        if begin and at % 2:
+            k = at // 2
+            first, second = inverse_ref[k, :HALF, :HALF], inverse_ref[k, HALF:, HALF:]
+            below = work[left:right, left - HALF : left]
+            inverse_ref[k, HALF:, :HALF] = -dot_nn(second, dot_nn(below, first))
+            inverse_ref[k, :HALF, HALF:] = jnp.zeros((HALF, HALF), jnp.float32)
+            work[left - HALF : left, left:right] = jnp.zeros((HALF, HALF), jnp.float32)
+
+
+def factor_head(begin, end, place, *blocks):
     return pl.pallas_call(
         functools.partial(head_kernel, begin, end),
         out_shape=[
-            jax.ShapeDtypeStruct((end - begin, NB, NB), jnp.float32),
+            jax.ShapeDtypeStruct((PANELS, NB, NB) if begin else (HALF, HALF), jnp.float32),
             jax.ShapeDtypeStruct((HEAD, HEAD), jnp.float32),
         ],
         in_specs=[pl.BlockSpec(memory_space=pltpu.SMEM)] + [pl.BlockSpec(memory_space=pltpu.VMEM)] * len(blocks),
         out_specs=[pl.BlockSpec(memory_space=pltpu.VMEM)] * 2,
         cost_estimate=pl.CostEstimate(flops=1_000, bytes_accessed=1_000, transcendentals=0),
         compiler_params=pltpu.CompilerParams(vmem_limit_bytes=(14 if begin else 56) * MIB),
-        name="factor_panels",
+        name="factor_head",
     )(place, *blocks)
 
 
-def across_kernel(place_ref, early_ref, late_ref, head_ref, *refs):
+def across_kernel(place_ref, inverse_ref, head_ref, *refs):
     heads, across = refs[:-1], refs[-1]
-    inverse, lower = head_blocks(early_ref, late_ref, head_ref)
+    inverse, lower = head_blocks(inverse_ref, head_ref)
     for j in range(PANELS):
         raw = heads[0][...]
         for d in range(1, len(heads)):
@@ -194,33 +197,33 @@
         across[j * NB : (j + 1) * NB] = dot_nn(inverse[j][...], raw)
 
 
-def head_blocks(early_ref, late_ref, head_ref):
-    inverse = (early_ref.at[0], late_ref.at[0], late_ref.at[1])
+def head_blocks(inverse_ref, head_ref):
+    inverse = [inverse_ref.at[j] for j in range(PANELS)]
     lower = {
         (i, j): head_ref.at[i * NB : (i + 1) * NB, j * NB : (j + 1) * NB] for i, j in ((1, 0), (2, 0), (2, 1))
     }
     return inverse, lower
 
 
-def solve_across(place, early, late, head, heads):
+def solve_across(place, inverse, head, heads):
     whole = pl.BlockSpec(memory_space=pltpu.VMEM)
     return pl.pallas_call(
         across_kernel,
         out_shape=jax.ShapeDtypeStruct((HEAD, heads[0].shape[1]), jnp.float32),
-        in_specs=[pl.BlockSpec(memory_space=pltpu.SMEM)] + [whole] * (3 + len(heads)),
+        in_specs=[pl.BlockSpec(memory_space=pltpu.SMEM)] + [whole] * (2 + len(heads)),
         out_specs=whole,
         cost_estimate=pl.CostEstimate(flops=4_000_000_000, bytes_accessed=5_000_000, transcendentals=0),
         compiler_params=pltpu.CompilerParams(vmem_limit_bytes=(20 if len(heads) <= 4 else 56) * MIB),
         name="solve_across",
-    )(place, early, late, head, *heads)
-
-
-def update_kernel(grid_rows, place_ref, early_ref, late_ref, head_ref, top_ref, top_other_ref, *refs):
+    )(place, inverse, head, *heads)
+
+
+def update_kernel(grid_rows, place_ref, inverse_ref, head_ref, top_ref, top_other_ref, *refs):
     held_ref, held_other_ref, swapped_ref, swapped_other_ref, across, matrix_ref, out_ref, solved = refs
     my_row, my_col = place_ref[0], place_ref[1]
     plane, core = my_col // 2, my_col % 2
     step = pl.program_id(0)
-    inverse, lower = head_blocks(early_ref, late_ref, head_ref)
+    inverse, lower = head_blocks(inverse_ref, head_ref)
 
     @pl.when(step == 0)
     def _():
@@ -270,7 +273,7 @@
             out_ref[here, there] = updated
 
 
-def update(grid_rows, place, early, late, head, top, top_other, sent, across, matrix):
+def update(grid_rows, place, inverse, head, top, top_other, sent, across, matrix):
     whole = pl.BlockSpec(memory_space=pltpu.VMEM)
     depth = 2 * NB if matrix.shape[0] % (2 * NB) == 0 else NB
     strip = pl.BlockSpec((depth, matrix.shape[1]), lambda step: (step, 0))
@@ -278,13 +281,13 @@
         functools.partial(update_kernel, grid_rows),
         out_shape=jax.ShapeDtypeStruct(matrix.shape, jnp.float32),
         grid=(matrix.shape[0] // depth,),
-        in_specs=[pl.BlockSpec(memory_space=pltpu.SMEM)] + [whole] * (6 + len(sent)) + [strip],
+        in_specs=[pl.BlockSpec(memory_space=pltpu.SMEM)] + [whole] * (5 + len(sent)) + [strip],
         out_specs=strip,
         scratch_shapes=[pltpu.VMEM((matrix.shape[0], HEAD), jnp.float32)],
         cost_estimate=pl.CostEstimate(flops=10_000_000_000, bytes_accessed=10_000_000, transcendentals=0),
         compiler_params=pltpu.CompilerParams(vmem_limit_bytes=30 * MIB),
         name="update",
-    )(place, early, late, head, top, top_other, *sent, across, matrix)
+    )(place, inverse, head, top, top_other, *sent, across, matrix)
 
 
 def body(matrix):
@@ -300,16 +303,15 @@
     def swap_cores(x):
         return send(x, [((r, c), (r, c ^ 1)) for r in range(grid_rows) for c in range(grid_cols)])
 
-    def along_rows(x):
-        out = [x]
-        for d in range(1, grid_rows):
-            out.append(
-                send(x, [((i, c), (i ^ d, c)) for i in range(PANELS) if i ^ d < grid_rows for c in range(grid_cols)])
-            )
+    def along_rows(x, begin, end):
+        out = []
+        for d in range(begin, end):
+            pairs = [((i, c), (i ^ d, c)) for i in range(PANELS) if i ^ d < grid_rows for c in range(grid_cols)]
+            out.append(send(x, pairs) if d else x)
         return out
 
     place = jnp.stack([my_row, my_col]).astype(jnp.int32)
-    corner = matrix[:NB, :NB]
+    corner, matrix = lax.optimization_barrier((matrix[:NB, :NB], matrix))
     carried = jnp.zeros_like(corner)
     passed = []
     for d in [*range(1, planes), 0]:
@@ -329,10 +331,9 @@
         if j % 2 == carrier:
             native = native | ((my_row == i) & (my_col == j))
     carried = jnp.where(native, corner, carried)
-    heads = along_rows(matrix[:NB])
-    found = along_rows(carried)
-    found, early_heads = lax.optimization_barrier((found, heads[:EARLY]))
-    heads = [*early_heads, *heads[EARLY:]]
+    heads = along_rows(matrix[:NB], 0, EARLY)
+    carried, heads, place = lax.optimization_barrier((carried, heads, place))
+    found = along_rows(carried, 0, grid_rows)
     top_mine, top_last = corner, corner
     for d in range(1, planes):
         top_mine = jnp.where(plane == d, passed[d - 1], top_mine)
@@ -351,8 +352,9 @@
                 pairs.append(((r, 2 * z + 2), (r, 2 * (z + distance) + 2)))
         got = send(held, pairs)
         if distance == 2:
-            early, head = factor_panels(0, 1, place, *found, *mirrored)
-            got, head, heads = lax.optimization_barrier((got, head, heads))
+            early, head = factor_head(0, 1, place, *found, *mirrored)
+            got, head, late_matrix = lax.optimization_barrier((got, head, matrix))
+            heads += along_rows(late_matrix[:NB], EARLY, grid_rows)
         held = jnp.where((plane // distance) % 2 == 1, got, held)
         distance //= 2
     held, head, top = lax.optimization_barrier((held, head, top))
@@ -363,12 +365,12 @@
             pairs.append(((r, 2 * z + 2), (r, 2 * z)))
     swapped = send(held, pairs)
     held_other, top_other = swap_cores(held), swap_cores(top)
-    late, head = factor_panels(1, PANELS, place, head)
-    across = solve_across(place, early, late, head, heads)
+    inverse, head = factor_head(1, HEAD // HALF, place, early, head)
+    across = solve_across(place, inverse, head, heads)
     swapped, across = lax.optimization_barrier((swapped, across))
     swapped_other = swap_cores(swapped)
     sent = [held, held_other, swapped, swapped_other]
-    return update(grid_rows, place, early, late, head, top, top_other, sent, across, matrix)
+    return update(grid_rows, place, inverse, head, top, top_other, sent, across, matrix)
 
 
 def solution(mesh):

time: 105 us -> 103 us (0.981)
  waiting for transfers between devices: 8.48 us -> 17.6 us
  starting transfers between devices: 43.9 us -> 36.4 us
  other arithmetic: 3.2 us -> 1.97 us
  local copies, waits for them, and re-layouts: 6.11 us -> 4.96 us
    ppermute x19, waiting for transfers between devices: 8.48 us -> 17.6 us  [send(): return lax.ppermute(x, ('row', 'col'), flat)]
    ppermute x19, starting transfers between devices: 43.9 us -> 36.4 us  [send(): return lax.ppermute(x, ('row', 'col'), flat)]
    unnamed x18 -> x14, local copies, waits for them, and re-layouts: 2.27 us -> 0.81 us
    slice x1, local copies, waits for them, and re-layouts: 0.95 us -> 2.07 us  [body(): strip, _ = lax.optimization_barrier((matrix[NB:, :NB], carried))]
    another operation x2, other arithmetic: 1.24 us -> 0.13 us  [body(): jnp.stack([top_mine, top_last])]
    slice x2 -> x3, local copies, waits for them, and re-layouts: 2.89 us -> 2.08 us  [the longest x1 1.08 us: body(): heads = along_rows(matrix[:NB], 0, EARLY)]
  transfers between devices with their start and end apart: 19 -> 19, of which waited for: 6 -> 11; matrix products, arithmetic and copies ran while one was open for 4% -> 5% of each run, Pallas kernels for 26% -> 26%
where the time goes in v4:
time: 103 us; the launch traced here: 102 us
  Pallas kernels  40.9 us (40%)
  starting transfers between devices  36.4 us (35%)
  waiting for transfers between devices  17.6 us (17%)
  local copies, waits for them, and re-layouts  4.96 us (5%)
  other arithmetic  1.97 us (2%)
    ppermute x19, starting transfers between devices, send(): return lax.ppermute(x, ('row', 'col'), flat)  36.4 us
    pallas_call x2, Pallas kernels, factor_head(): pl.pallas_call(functools.partial(head_kernel, begin, end), out_shape=[jax...  22.6 us
    ppermute x19, waiting for transfers between devices, send(): return lax.ppermute(x, ('row', 'col'), flat)  17.6 us
    pallas_call x1, Pallas kernels, update(): pl.pallas_call(functools.partial(update_kernel, grid_rows), out_shape=jax...  13.9 us
    pallas_call x1, Pallas kernels, solve_across(): pl.pallas_call(across_kernel, out_shape=jax.ShapeDtypeStruct((HEAD, heads...  4.47 us
    slice x1, local copies, waits for them, and re-layouts, body(): strip, _ = lax.optimization_barrier((matrix[NB:, :NB], carried))  2.07 us
  transfers between devices with their start and end apart: 19, of which 11 were waited for; matrix products, arithmetic and copies ran while one was open for 5% of the time, Pallas kernels for 26%

profile of v4, /device:TPU:0, one launch (start us, length us, event | category | flops | bytes accessed | tf_op | source)
XLA Modules:
  0.0 102.2 jit_solution(8230554509217833763)
XLA Ops:
  1.7 7.0 %collective-permute-start.2 = (f32[256,256]{1,0:T(8,128)S(1)}, f32[256,256]{1,0:T(8,128)S(1)}, u32[]{:S(2)}, u32[]{:S(2)}) collective-permute-start(f32[256,256]{1,0:T(8,128)S(1)} %slice.12), channel_id=1, source_target_pairs={{0,6},{1,7},{10,8},{9,15},{16,22},{18,17},{24,30},{25,31},{26,24}} | collective-permute-start | bytes 786440 | tf_op jit(solution)/shard_map/ppermute | solution.py:301
  8.6 1.3 %collective-permute-start.1 = (f32[256,256]{1,0:T(8,128)S(1)}, f32[256,256]{1,0:T(8,128)S(1)}, u32[]{:S(2)}, u32[]{:S(2)}) collective-permute-start(f32[256,256]{1,0:T(8,128)S(1)} %slice.12), channel_id=1, source_target_pairs={{0,4},{1,5},{10,14},{9,13},{16,20},{18,23},{24,28},{25,29},{26,30}} | collective-permute-start | bytes 786440 | tf_op jit(solution)/shard_map/ppermute | solution.py:301
  9.9 1.3 %collective-permute-start = (f32[256,256]{1,0:T(8,128)S(1)}, f32[256,256]{1,0:T(8,128)S(1)}, u32[]{:S(2)}, u32[]{:S(2)}) collective-permute-start(f32[256,256]{1,0:T(8,128)S(1)} %slice.12), channel_id=1, source_target_pairs={{0,2},{1,3},{10,12},{9,11},{16,18},{18,21},{24,26},{25,27},{26,28}} | collective-permute-start | bytes 786440 | tf_op jit(solution)/shard_map/ppermute | solution.py:301
  11.3 1.1 %slice.13.refs_0_ = f32[256,512]{1,0:T(8,128)S(1)} slice(f32[1024,512]{1,0:T(8,128)} %refs_5_), slice={[0:256], [0:512]} | slice | bytes 1048576 | tf_op jit(solution)/shard_map/slice | solution.py:334
  12.3 3.4 %collective-permute-start.5 = (f32[256,512]{1,0:T(8,128)S(1)}, f32[256,512]{1,0:T(8,128)S(1)}, u32[]{:S(2)}, u32[]{:S(2)}) collective-permute-start(f32[256,512]{1,0:T(8,128)S(1)} %slice.13.refs_0_), channel_id=1, source_target_pairs={{0,16},{1,17},{2,18},{3,19},{4,20},{5,21},{6,22},{7,23},{8,24},{9,... | collective-permute-start | bytes 1572872 | tf_op jit(solution)/shard_map/ppermute | solution.py:301
  15.8 4.6 %collective-permute-start.4 = (f32[256,512]{1,0:T(8,128)S(1)}, f32[256,512]{1,0:T(8,128)}, u32[]{:S(2)}, u32[]{:S(2)}) collective-permute-start(f32[256,512]{1,0:T(8,128)S(1)} %slice.13.refs_0_), channel_id=1, source_target_pairs={{0,8},{1,9},{2,10},{3,11},{4,12},{5,13},{6,14},{7,15},{8,0},{9,1},... | collective-permute-start | bytes 1572872 | tf_op jit(solution)/shard_map/ppermute | solution.py:301
  20.4 2.1 %slice.14 = f32[768,256]{1,0:T(8,128)} slice(f32[1024,512]{1,0:T(8,128)} %refs_5_), slice={[256:1024], [0:256]} | slice | bytes 1572864 | tf_op jit(solution)/shard_map/slice | solution.py:343
  23.1 2.3 %collective-permute-done = f32[256,256]{1,0:T(8,128)S(1)} collective-permute-done((f32[256,256]{1,0:T(8,128)S(1)}, f32[256,256]{1,0:T(8,128)S(1)}, u32[]{:S(2)}, u32[]{:S(2)}) %collective-permute-start) | collective-permute-done | bytes 262176 | tf_op jit(solution)/shard_map/ppermute | solution.py:301
  25.5 2.1 %collective-permute-done.5.refs_2_ = f32[256,512]{1,0:T(8,128)S(1)} collective-permute-done((f32[256,512]{1,0:T(8,128)S(1)}, f32[256,512]{1,0:T(8,128)S(1)}, u32[]{:S(2)}, u32[]{:S(2)}) %collective-permute-start.5) | collective-permute-done | bytes 524320 | tf_op jit(solution)/shard_map/ppermute | solution.py:301
  28.4 2.3 %collective-permute-done.4.refs_1_ = f32[256,512]{1,0:T(8,128)} collective-permute-done((f32[256,512]{1,0:T(8,128)S(1)}, f32[256,512]{1,0:T(8,128)}, u32[]{:S(2)}, u32[]{:S(2)}) %collective-permute-start.4) | collective-permute-done | bytes 524320 | tf_op jit(solution)/shard_map/ppermute | solution.py:301
  30.7 2.2 %collective-permute-start.13 = (f32[768,256]{1,0:T(8,128)}, f32[768,256]{1,0:T(8,128)}, u32[]{:S(2)}, u32[]{:S(2)}) collective-permute-start(f32[768,256]{1,0:T(8,128)} %slice.14), channel_id=1, source_target_pairs={{0,4},{1,5},{2,6},{8,12},{9,13},{10,14},{16,20},{17,21},{18,22},{2... | collective-permute-start | bytes 2359304 | tf_op jit(solution)/shard_map/ppermute | solution.py:301
  32.9 4.8 %collective-permute-start.8 = (f32[256,256]{1,0:T(8,128)S(1)}, f32[256,256]{1,0:T(8,128)}, u32[]{:S(2)}, u32[]{:S(2)}) collective-permute-start(f32[256,256]{1,0:T(8,128)S(1)} %get-tuple-element.34.refs_0_), channel_id=1, source_target_pairs={{0,24},{1,25},{2,26},{3,27},{4,28},{5,29},{6,30},{7,31},{8,16},{9,... | collective-permute-start | bytes 786440 | tf_op jit(solution)/shard_map/ppermute | solution.py:301
  37.7 2.2 %collective-permute-start.7 = (f32[256,256]{1,0:T(8,128)S(1)}, f32[256,256]{1,0:T(8,128)}, u32[]{:S(2)}, u32[]{:S(2)}) collective-permute-start(f32[256,256]{1,0:T(8,128)S(1)} %get-tuple-element.34.refs_0_), channel_id=1, source_target_pairs={{0,16},{1,17},{2,18},{3,19},{4,20},{5,21},{6,22},{7,23},{8,24},{9,... | collective-permute-start | bytes 786440 | tf_op jit(solution)/shard_map/ppermute | solution.py:301
  39.9 1.9 %collective-permute-start.6 = (f32[256,256]{1,0:T(8,128)S(1)}, f32[256,256]{1,0:T(8,128)}, u32[]{:S(2)}, u32[]{:S(2)}) collective-permute-start(f32[256,256]{1,0:T(8,128)S(1)} %get-tuple-element.34.refs_0_), channel_id=1, source_target_pairs={{0,8},{1,9},{2,10},{3,11},{4,12},{5,13},{6,14},{7,15},{8,0},{9,1},... | collective-permute-start | bytes 786440 | tf_op jit(solution)/shard_map/ppermute | solution.py:301
  42.9 3.1 %collective-permute-done.7.refs_2_ = f32[256,256]{1,0:T(8,128)} collective-permute-done((f32[256,256]{1,0:T(8,128)S(1)}, f32[256,256]{1,0:T(8,128)}, u32[]{:S(2)}, u32[]{:S(2)}) %collective-permute-start.7) | collective-permute-done | bytes 262176 | tf_op jit(solution)/shard_map/ppermute | solution.py:301
  46.1 2.2 %collective-permute-done.6.refs_1_ = f32[256,256]{1,0:T(8,128)} collective-permute-done((f32[256,256]{1,0:T(8,128)S(1)}, f32[256,256]{1,0:T(8,128)}, u32[]{:S(2)}, u32[]{:S(2)}) %collective-permute-start.6) | collective-permute-done | bytes 262176 | tf_op jit(solution)/shard_map/ppermute | solution.py:301
  51.3 7.3 %factor_head.2 = (f32[128,128]{1,0:T(8,128)}, f32[768,768]{1,0:T(8,128)}) custom-call(s32[2]{0:T(128)} %pad_add_fusion.place_ref, f32[256,256]{1,0:T(8,128)} %copy-done.6, f32[256,256]{1,0:T(8,128)} %collective-permute-done.6.refs_1_, f32[256,256]{1,0:T(8,128)} %collective-permute-done.7.refs_2_, f32[256,256]{1,0:T(8,128)} %collective-permute-done.8.refs_3_, ...), custom_call_target="tpu_custom_call" | custom-call | flops 1000 | bytes 1000 | tf_op jit(solution)/shard_map/factor_head/pallas_call | solution.py:174
  58.7 3.2 %collective-permute-start.17 = (f32[256,512]{1,0:T(8,128)S(1)}, f32[256,512]{1,0:T(8,128)S(1)}, u32[]{:S(2)}, u32[]{:S(2)}) collective-permute-start(f32[256,512]{1,0:T(8,128)S(1)} %slice.15), channel_id=1, source_target_pairs={{0,24},{1,25},{2,26},{3,27},{4,28},{5,29},{6,30},{7,31},{8,16},{9,... | collective-permute-start | bytes 1572872 | tf_op jit(solution)/shard_map/ppermute | solution.py:301
  61.9 1.2 %broadcast_select_fusion.refs_0_ = f32[768,256]{1,0:T(8,128)S(1)} fusion(f32[768,256]{1,0:T(8,128)} %collective-permute-done.13, f32[768,256]{1,0:T(8,128)} %slice.14, pred[]{:T(512)S(6)} %eq.60), kind=kLoop, calls=%fused_computation.1 | loop fusion | flops 196608 | bytes 2359297 | tf_op jit(solution)/shard_map/jit(_where)/select_n | solution.py:358
  63.1 2.1 %collective-permute-start.16 = (f32[768,256]{1,0:T(8,128)S(1)}, f32[768,256]{1,0:T(8,128)S(1)}, u32[]{:S(2)}, u32[]{:S(2)}) collective-permute-start(f32[768,256]{1,0:T(8,128)S(1)} %broadcast_select_fusion.refs_0_), channel_id=1, source_target_pairs={{0,2},{1,3},{2,0},{8,10},{9,11},{10,8},{16,18},{17,19},{18,16},{24... | collective-permute-start | bytes 2359304 | tf_op jit(solution)/shard_map/ppermute | solution.py:301
  65.3 15.2 %factor_head.3 = (f32[3,256,256]{2,1,0:T(8,128)S(1)}, f32[768,768]{1,0:T(8,128)S(1)}) custom-call(s32[2]{0:T(128)S(1)} %copy-done.3, f32[128,128]{1,0:T(8,128)S(1)} %copy-done.2, f32[768,768]{1,0:T(8,128)S(1)} %copy-done), custom_call_target="tpu_custom_call" | custom-call | flops 1000 | bytes 1000 | tf_op jit(solution)/shard_map/factor_head/pallas_call | solution.py:174
  80.6 4.5 %solve_across.1.refs_4_ = f32[768,512]{1,0:T(8,128)S(1)} custom-call(s32[2]{0:T(128)S(1)} %copy-done.3, f32[3,256,256]{2,1,0:T(8,128)S(1)} %get-tuple-element.45.inverse_ref, f32[768,768]{1,0:T(8,128)S(1)} %get-tuple-element.46.head_ref, f32[256,512]{1,0:T(8,128)S(1)} %slice.13.refs_0_, f32[256,512]{1,0:T(8,128)} %collective-permute-done.4.refs_1_, ...), custom_call_target="tpu_custom_call" | custom-call | flops 4000000000 | bytes 5000000 | tf_op jit(solution)/shard_map/solve_across/pallas_call | solution.py:210
  85.7 2.6 %collective-permute-done.14.top_other_ref = f32[2,256,256]{2,1,0:T(8,128)S(1)} collective-permute-done((f32[2,256,256]{2,1,0:T(8,128)S(1)}, f32[2,256,256]{2,1,0:T(8,128)S(1)}, u32[]{:S(2)}, u32[]{:S(2)}) %collective-permute-start.14) | collective-permute-done | bytes 524320 | tf_op jit(solution)/shard_map/ppermute | solution.py:301
  88.3 13.9 %update.1 = f32[1024,512]{1,0:T(8,128)} custom-call(s32[2]{0:T(128)S(1)} %copy-done.3, f32[3,256,256]{2,1,0:T(8,128)S(1)} %get-tuple-element.45.inverse_ref, f32[768,768]{1,0:T(8,128)S(1)} %get-tuple-element.46.head_ref, f32[2,256,256]{2,1,0:T(8,128)S(1)} %pad_maximum_fusion.top_ref, f32[2,256,256]{2,1,0:T(8,128)S(1)} %collective-permute-done.14.top_other_ref, ...), custom_call_target="tpu_custom_call" | custom-call | flops 10000000000 | bytes 10000000 | tf_op jit(solution)/shard_map/update/pallas_call | solution.py:280
  (40 shorter events, 8.0 us)
Async XLA Ops:
  1.0 14.8 %collective-permute-start.3 = (f32[256,256]{1,0:T(8,128)S(1)}, f32[256,256]{1,0:T(8,128)S(1)}, u32[]{:S(2)}, u32[]{:S(2)}) collective-permute-start(f32[256,256]{1,0:T(8,128)S(1)} %slice.12), channel_id=1, source_target_pairs={{18,19}} | collective-permute-start | bytes 786440 | tf_op jit(solution)/shard_map/ppermute | solution.py:301
  1.7 21.4 %collective-permute-start.2 = (f32[256,256]{1,0:T(8,128)S(1)}, f32[256,256]{1,0:T(8,128)S(1)}, u32[]{:S(2)}, u32[]{:S(2)}) collective-permute-start(f32[256,256]{1,0:T(8,128)S(1)} %slice.12), channel_id=1, source_target_pairs={{0,6},{1,7},{10,8},{9,15},{16,22},{18,17},{24,30},{25,31},{26,24}} | collective-permute-start | bytes 786440 | tf_op jit(solution)/shard_map/ppermute | solution.py:301
  8.6 14.5 %collective-permute-start.1 = (f32[256,256]{1,0:T(8,128)S(1)}, f32[256,256]{1,0:T(8,128)S(1)}, u32[]{:S(2)}, u32[]{:S(2)}) collective-permute-start(f32[256,256]{1,0:T(8,128)S(1)} %slice.12), channel_id=1, source_target_pairs={{0,4},{1,5},{10,14},{9,13},{16,20},{18,23},{24,28},{25,29},{26,30}} | collective-permute-start | bytes 786440 | tf_op jit(solution)/shard_map/ppermute | solution.py:301
  9.9 15.5 %collective-permute-start = (f32[256,256]{1,0:T(8,128)S(1)}, f32[256,256]{1,0:T(8,128)S(1)}, u32[]{:S(2)}, u32[]{:S(2)}) collective-permute-start(f32[256,256]{1,0:T(8,128)S(1)} %slice.12), channel_id=1, source_target_pairs={{0,2},{1,3},{10,12},{9,11},{16,18},{18,21},{24,26},{25,27},{26,28}} | collective-permute-start | bytes 786440 | tf_op jit(solution)/shard_map/ppermute | solution.py:301
  12.3 15.3 %collective-permute-start.5 = (f32[256,512]{1,0:T(8,128)S(1)}, f32[256,512]{1,0:T(8,128)S(1)}, u32[]{:S(2)}, u32[]{:S(2)}) collective-permute-start(f32[256,512]{1,0:T(8,128)S(1)} %slice.13.refs_0_), channel_id=1, source_target_pairs={{0,16},{1,17},{2,18},{3,19},{4,20},{5,21},{6,22},{7,23},{8,24},{9,... | collective-permute-start | bytes 1572872 | tf_op jit(solution)/shard_map/ppermute | solution.py:301
  15.8 14.9 %collective-permute-start.4 = (f32[256,512]{1,0:T(8,128)S(1)}, f32[256,512]{1,0:T(8,128)}, u32[]{:S(2)}, u32[]{:S(2)}) collective-permute-start(f32[256,512]{1,0:T(8,128)S(1)} %slice.13.refs_0_), channel_id=1, source_target_pairs={{0,8},{1,9},{2,10},{3,11},{4,12},{5,13},{6,14},{7,15},{8,0},{9,1},... | collective-permute-start | bytes 1572872 | tf_op jit(solution)/shard_map/ppermute | solution.py:301
  25.5 25.8 %copy-start.6 = (f32[256,256]{1,0:T(8,128)}, f32[256,256]{1,0:T(8,128)S(1)}, u32[]{:S(2)}) copy-start(f32[256,256]{1,0:T(8,128)S(1)} %get-tuple-element.34.refs_0_) | copy-start | bytes 786436
  25.5 33.1 %copy-start.1 = (f32[1024,512]{1,0:T(8,128)S(1)}, f32[1024,512]{1,0:T(8,128)}, u32[]{:S(2)}) copy-start(f32[1024,512]{1,0:T(8,128)} %refs_5_) | copy-start | bytes 6291460
  30.7 27.9 %collective-permute-start.13 = (f32[768,256]{1,0:T(8,128)}, f32[768,256]{1,0:T(8,128)}, u32[]{:S(2)}, u32[]{:S(2)}) collective-permute-start(f32[768,256]{1,0:T(8,128)} %slice.14), channel_id=1, source_target_pairs={{0,4},{1,5},{2,6},{8,12},{9,13},{10,14},{16,20},{17,21},{18,22},{2... | collective-permute-start | bytes 2359304 | tf_op jit(solution)/shard_map/ppermute | solution.py:301
  32.9 10.1 %collective-permute-start.8 = (f32[256,256]{1,0:T(8,128)S(1)}, f32[256,256]{1,0:T(8,128)}, u32[]{:S(2)}, u32[]{:S(2)}) collective-permute-start(f32[256,256]{1,0:T(8,128)S(1)} %get-tuple-element.34.refs_0_), channel_id=1, source_target_pairs={{0,24},{1,25},{2,26},{3,27},{4,28},{5,29},{6,30},{7,31},{8,16},{9,... | collective-permute-start | bytes 786440 | tf_op jit(solution)/shard_map/ppermute | solution.py:301
  37.7 8.4 %collective-permute-start.7 = (f32[256,256]{1,0:T(8,128)S(1)}, f32[256,256]{1,0:T(8,128)}, u32[]{:S(2)}, u32[]{:S(2)}) collective-permute-start(f32[256,256]{1,0:T(8,128)S(1)} %get-tuple-element.34.refs_0_), channel_id=1, source_target_pairs={{0,16},{1,17},{2,18},{3,19},{4,20},{5,21},{6,22},{7,23},{8,24},{9,... | collective-permute-start | bytes 786440 | tf_op jit(solution)/shard_map/ppermute | solution.py:301
  39.9 8.4 %collective-permute-start.6 = (f32[256,256]{1,0:T(8,128)S(1)}, f32[256,256]{1,0:T(8,128)}, u32[]{:S(2)}, u32[]{:S(2)}) collective-permute-start(f32[256,256]{1,0:T(8,128)S(1)} %get-tuple-element.34.refs_0_), channel_id=1, source_target_pairs={{0,8},{1,9},{2,10},{3,11},{4,12},{5,13},{6,14},{7,15},{8,0},{9,1},... | collective-permute-start | bytes 786440 | tf_op jit(solution)/shard_map/ppermute | solution.py:301
  48.2 2.0 %collective-permute-start.9 = (f32[256,256]{1,0:T(8,128)S(1)}, f32[256,256]{1,0:T(8,128)}, u32[]{:S(2)}, u32[]{:S(2)}) collective-permute-start(f32[256,256]{1,0:T(8,128)S(1)} %get-tuple-element.34.refs_0_), channel_id=1, source_target_pairs={{0,1},{1,0},{2,3},{3,2},{4,5},{5,4},{6,7},{7,6},{8,9},{9,8},{10,11... | collective-permute-start | bytes 786440 | tf_op jit(solution)/shard_map/ppermute | solution.py:301
  48.3 2.2 %collective-permute-start.10 = (f32[256,256]{1,0:T(8,128)}, f32[256,256]{1,0:T(8,128)}, u32[]{:S(2)}, u32[]{:S(2)}) collective-permute-start(f32[256,256]{1,0:T(8,128)} %collective-permute-done.6.refs_1_), channel_id=1, source_target_pairs={{0,1},{1,0},{2,3},{3,2},{4,5},{5,4},{6,7},{7,6},{8,9},{9,8},{10,11... | collective-permute-start | bytes 786440 | tf_op jit(solution)/shard_map/ppermute | solution.py:301
  48.8 2.1 %collective-permute-start.11 = (f32[256,256]{1,0:T(8,128)}, f32[256,256]{1,0:T(8,128)}, u32[]{:S(2)}, u32[]{:S(2)}) collective-permute-start(f32[256,256]{1,0:T(8,128)} %collective-permute-done.7.refs_2_), channel_id=1, source_target_pairs={{0,1},{1,0},{2,3},{3,2},{4,5},{5,4},{6,7},{7,6},{8,9},{9,8},{10,11... | collective-permute-start | bytes 786440 | tf_op jit(solution)/shard_map/ppermute | solution.py:301
  48.8 2.5 %collective-permute-start.12 = (f32[256,256]{1,0:T(8,128)}, f32[256,256]{1,0:T(8,128)}, u32[]{:S(2)}, u32[]{:S(2)}) collective-permute-start(f32[256,256]{1,0:T(8,128)} %collective-permute-done.8.refs_3_), channel_id=1, source_target_pairs={{0,1},{1,0},{2,3},{3,2},{4,5},{5,4},{6,7},{7,6},{8,9},{9,8},{10,11... | collective-permute-start | bytes 786440 | tf_op jit(solution)/shard_map/ppermute | solution.py:301
  58.6 6.7 %copy-start.2 = (f32[128,128]{1,0:T(8,128)S(1)}, f32[128,128]{1,0:T(8,128)}, u32[]{:S(2)}) copy-start(f32[128,128]{1,0:T(8,128)} %get-tuple-element.38.refs_0_) | copy-start | bytes 196612
  58.6 6.7 %copy-start.3 = (s32[2]{0:T(128)S(1)}, s32[2]{0:T(128)}, u32[]{:S(2)}) copy-start(s32[2]{0:T(128)} %pad_add_fusion.place_ref) | copy-start | bytes 28
  58.6 21.9 %copy-start.5 = (f32[256,512]{1,0:T(8,128)S(1)}, f32[256,512]{1,0:T(8,128)}, u32[]{:S(2)}) copy-start(f32[256,512]{1,0:T(8,128)} %copy-done.4) | copy-start | bytes 1572868
  58.7 21.9 %collective-permute-start.17 = (f32[256,512]{1,0:T(8,128)S(1)}, f32[256,512]{1,0:T(8,128)S(1)}, u32[]{:S(2)}, u32[]{:S(2)}) collective-permute-start(f32[256,512]{1,0:T(8,128)S(1)} %slice.15), channel_id=1, source_target_pairs={{0,24},{1,25},{2,26},{3,27},{4,28},{5,29},{6,30},{7,31},{8,16},{9,... | collective-permute-start | bytes 1572872 | tf_op jit(solution)/shard_map/ppermute | solution.py:301
  63.1 22.0 %collective-permute-start.16 = (f32[768,256]{1,0:T(8,128)S(1)}, f32[768,256]{1,0:T(8,128)S(1)}, u32[]{:S(2)}, u32[]{:S(2)}) collective-permute-start(f32[768,256]{1,0:T(8,128)S(1)} %broadcast_select_fusion.refs_0_), channel_id=1, source_target_pairs={{0,2},{1,3},{2,0},{8,10},{9,11},{10,8},{16,18},{17,19},{18,16},{24... | collective-permute-start | bytes 2359304 | tf_op jit(solution)/shard_map/ppermute | solution.py:301
  65.2 23.1 %collective-permute-start.15 = (f32[768,256]{1,0:T(8,128)S(1)}, f32[768,256]{1,0:T(8,128)S(1)}, u32[]{:S(2)}, u32[]{:S(2)}) collective-permute-start(f32[768,256]{1,0:T(8,128)S(1)} %broadcast_select_fusion.refs_0_), channel_id=1, source_target_pairs={{0,1},{1,0},{2,3},{3,2},{4,5},{5,4},{6,7},{7,6},{8,9},{9,8},{10,11... | collective-permute-start | bytes 2359304 | tf_op jit(solution)/shard_map/ppermute | solution.py:301
  85.1 3.2 %collective-permute-start.18 = (f32[768,256]{1,0:T(8,128)S(1)}, f32[768,256]{1,0:T(8,128)S(1)}, u32[]{:S(2)}, u32[]{:S(2)}) collective-permute-start(f32[768,256]{1,0:T(8,128)S(1)} %collective-permute-done.16.refs_2_), channel_id=1, source_target_pairs={{0,1},{1,0},{2,3},{3,2},{4,5},{5,4},{6,7},{7,6},{8,9},{9,8},{10,11... | collective-permute-start | bytes 2359304 | tf_op jit(solution)/shard_map/ppermute | solution.py:301
  85.6 2.7 %collective-permute-start.14 = (f32[2,256,256]{2,1,0:T(8,128)S(1)}, f32[2,256,256]{2,1,0:T(8,128)S(1)}, u32[]{:S(2)}, u32[]{:S(2)}) collective-permute-start(f32[2,256,256]{2,1,0:T(8,128)S(1)} %pad_maximum_fusion.top_ref), channel_id=1, source_target_pairs={{0,1},{1,0},{2,3},{3,2},{4,5},{5,4},{6,7},{7,6},{8,9},{9,8},{10,11... | collective-permute-start | bytes 1572872 | tf_op jit(solution)/shard_map/ppermute | solution.py:301
  (2 other events, 7.5 us)

commit v5 on v4

--- a/solution.py
+++ b/solution.py
@@ -179,16 +179,18 @@
         ],
         in_specs=[pl.BlockSpec(memory_space=pltpu.SMEM)] + [pl.BlockSpec(memory_space=pltpu.VMEM)] * len(blocks),
         out_specs=[pl.BlockSpec(memory_space=pltpu.VMEM)] * 2,
-        cost_estimate=pl.CostEstimate(flops=1_000, bytes_accessed=1_000, transcendentals=0),
+        cost_estimate=pl.CostEstimate(flops=15_000_000_000 if begin else 1_000, bytes_accessed=1_000, transcendentals=0),
         compiler_params=pltpu.CompilerParams(vmem_limit_bytes=(14 if begin else 56) * MIB),
         name="factor_head",
     )(place, *blocks)
 
 
-def across_kernel(place_ref, inverse_ref, head_ref, *refs):
-    heads, across = refs[:-1], refs[-1]
+def across_kernel(begin, end, place_ref, inverse_ref, head_ref, *refs):
+    heads, across = refs[: len(refs) - 1 - (begin > 0)], refs[-1]
     inverse, lower = head_blocks(inverse_ref, head_ref)
-    for j in range(PANELS):
+    if begin:
+        across[: begin * NB] = refs[-2][...]
+    for j in range(begin, end):
         raw = heads[0][...]
         for d in range(1, len(heads)):
             raw = jnp.where((place_ref[0] ^ j) == d, heads[d][...], raw)
@@ -205,17 +207,17 @@
     return inverse, lower
 
 
-def solve_across(place, inverse, head, heads):
+def solve_across(begin, end, place, inverse, head, heads, *given):
     whole = pl.BlockSpec(memory_space=pltpu.VMEM)
     return pl.pallas_call(
-        across_kernel,
-        out_shape=jax.ShapeDtypeStruct((HEAD, heads[0].shape[1]), jnp.float32),
-        in_specs=[pl.BlockSpec(memory_space=pltpu.SMEM)] + [whole] * (2 + len(heads)),
+        functools.partial(across_kernel, begin, end),
+        out_shape=jax.ShapeDtypeStruct((end * NB, heads[0].shape[1]), jnp.float32),
+        in_specs=[pl.BlockSpec(memory_space=pltpu.SMEM)] + [whole] * (2 + len(heads) + len(given)),
         out_specs=whole,
         cost_estimate=pl.CostEstimate(flops=4_000_000_000, bytes_accessed=5_000_000, transcendentals=0),
         compiler_params=pltpu.CompilerParams(vmem_limit_bytes=(20 if len(heads) <= 4 else 56) * MIB),
         name="solve_across",
-    )(place, inverse, head, *heads)
+    )(place, inverse, head, *heads, *given)
 
 
 def update_kernel(grid_rows, place_ref, inverse_ref, head_ref, top_ref, top_other_ref, *refs):
@@ -366,9 +368,10 @@
     swapped = send(held, pairs)
     held_other, top_other = swap_cores(held), swap_cores(top)
     inverse, head = factor_head(1, HEAD // HALF, place, early, head)
-    across = solve_across(place, inverse, head, heads)
+    across = solve_across(0, 1, place, inverse, head, heads)
     swapped, across = lax.optimization_barrier((swapped, across))
     swapped_other = swap_cores(swapped)
+    across = solve_across(1, PANELS, place, inverse, head, heads, across)
     sent = [held, held_other, swapped, swapped_other]
     return update(grid_rows, place, inverse, head, top, top_other, sent, across, matrix)
 

time: 103 us -> 99.4 us (0.965)
  waiting for transfers between devices: 17.6 us -> 14.8 us
    ppermute x19, waiting for transfers between devices: 17.6 us -> 14.8 us  [send(): return lax.ppermute(x, ('row', 'col'), flat)]
    select_n x1, other arithmetic: 1.25 us -> 0.11 us  [body(): held = jnp.where(plane // distance % 2 == 1, got, held)]
    pallas_call x1 -> x2, Pallas kernels: 4.47 us -> 4.53 us  [solve_across(): pl.pallas_call(functools.partial(across_kernel, begin, end), out_shape=ja...]
  transfers between devices with their start and end apart: 19 -> 19, of which waited for: 11 -> 9; matrix products, arithmetic and copies ran while one was open for 5% -> 4% of each run, Pallas kernels for 26% -> 27%
where the time goes in v5:
time: 99.4 us; the launch traced here: 98.9 us
  Pallas kernels  41.2 us (41%)
  starting transfers between devices  36.7 us (37%)
  waiting for transfers between devices  14.8 us (15%)
  local copies, waits for them, and re-layouts  3.99 us (4%)
  other arithmetic  1.93 us (2%)
    ppermute x19, starting transfers between devices, send(): return lax.ppermute(x, ('row', 'col'), flat)  36.7 us
    pallas_call x2, Pallas kernels, factor_head(): pl.pallas_call(functools.partial(head_kernel, begin, end), out_shape=[jax...  22.6 us
    ppermute x19, waiting for transfers between devices, send(): return lax.ppermute(x, ('row', 'col'), flat)  14.8 us
    pallas_call x1, Pallas kernels, update(): pl.pallas_call(functools.partial(update_kernel, grid_rows), out_shape=jax...  14.1 us
    pallas_call x2, Pallas kernels, solve_across(): pl.pallas_call(functools.partial(across_kernel, begin, end), out_shape=ja...  4.53 us
  transfers between devices with their start and end apart: 19, of which 9 were waited for; matrix products, arithmetic and copies ran while one was open for 4% of the time, Pallas kernels for 27%

profile of v5, /device:TPU:0, one launch (start us, length us, event | category | flops | bytes accessed | tf_op | source)
XLA Modules:
  0.0 98.9 jit_solution(14601005679452625064)
XLA Ops:
  1.7 7.0 %collective-permute-start.2 = (f32[256,256]{1,0:T(8,128)S(1)}, f32[256,256]{1,0:T(8,128)S(1)}, u32[]{:S(2)}, u32[]{:S(2)}) collective-permute-start(f32[256,256]{1,0:T(8,128)S(1)} %slice.12), channel_id=1, source_target_pairs={{0,6},{1,7},{10,8},{9,15},{16,22},{18,17},{24,30},{25,31},{26,24}} | collective-permute-start | bytes 786440 | tf_op jit(solution)/shard_map/ppermute | solution.py:303
  8.6 1.3 %collective-permute-start.1 = (f32[256,256]{1,0:T(8,128)S(1)}, f32[256,256]{1,0:T(8,128)S(1)}, u32[]{:S(2)}, u32[]{:S(2)}) collective-permute-start(f32[256,256]{1,0:T(8,128)S(1)} %slice.12), channel_id=1, source_target_pairs={{0,4},{1,5},{10,14},{9,13},{16,20},{18,23},{24,28},{25,29},{26,30}} | collective-permute-start | bytes 786440 | tf_op jit(solution)/shard_map/ppermute | solution.py:303
  9.9 2.0 %collective-permute-start = (f32[256,256]{1,0:T(8,128)S(1)}, f32[256,256]{1,0:T(8,128)}, u32[]{:S(2)}, u32[]{:S(2)}) collective-permute-start(f32[256,256]{1,0:T(8,128)S(1)} %slice.12), channel_id=1, source_target_pairs={{0,2},{1,3},{10,12},{9,11},{16,18},{18,21},{24,26},{25,27},{26,28}} | collective-permute-start | bytes 786440 | tf_op jit(solution)/shard_map/ppermute | solution.py:303
  12.0 1.1 %slice.13.refs_0_ = f32[256,512]{1,0:T(8,128)S(1)} slice(f32[1024,512]{1,0:T(8,128)} %refs_5_), slice={[0:256], [0:512]} | slice | bytes 1048576 | tf_op jit(solution)/shard_map/slice | solution.py:336
  13.0 3.4 %collective-permute-start.5 = (f32[256,512]{1,0:T(8,128)S(1)}, f32[256,512]{1,0:T(8,128)S(1)}, u32[]{:S(2)}, u32[]{:S(2)}) collective-permute-start(f32[256,512]{1,0:T(8,128)S(1)} %slice.13.refs_0_), channel_id=1, source_target_pairs={{0,16},{1,17},{2,18},{3,19},{4,20},{5,21},{6,22},{7,23},{8,24},{9,... | collective-permute-start | bytes 1572872 | tf_op jit(solution)/shard_map/ppermute | solution.py:303
  16.5 4.6 %collective-permute-start.4 = (f32[256,512]{1,0:T(8,128)S(1)}, f32[256,512]{1,0:T(8,128)S(1)}, u32[]{:S(2)}, u32[]{:S(2)}) collective-permute-start(f32[256,512]{1,0:T(8,128)S(1)} %slice.13.refs_0_), channel_id=1, source_target_pairs={{0,8},{1,9},{2,10},{3,11},{4,12},{5,13},{6,14},{7,15},{8,0},{9,1},... | collective-permute-start | bytes 1572872 | tf_op jit(solution)/shard_map/ppermute | solution.py:303
  21.1 1.2 %slice.14 = f32[768,256]{1,0:T(8,128)S(1)} slice(f32[1024,512]{1,0:T(8,128)} %refs_5_), slice={[256:1024], [0:256]} | slice | bytes 1572864 | tf_op jit(solution)/shard_map/slice | solution.py:345
  23.7 1.7 %collective-permute-done = f32[256,256]{1,0:T(8,128)} collective-permute-done((f32[256,256]{1,0:T(8,128)S(1)}, f32[256,256]{1,0:T(8,128)}, u32[]{:S(2)}, u32[]{:S(2)}) %collective-permute-start) | collective-permute-done | bytes 262176 | tf_op jit(solution)/shard_map/ppermute | solution.py:303
  25.4 1.1 %select_bitcast_fusion.1 = (f32[1,256,256]{2,1,0:T(8,128)S(1)}, f32[1,256,256]{2,1,0:T(8,128)S(1)}, f32[256,256]{1,0:T(8,128)S(1)}) fusion(f32[256,256]{1,0:T(8,128)S(1)} %collective-permute-done.2, f32[256,256]{1,0:T(8,128)} %copy-done.5, f32[256,256]{1,0:T(8,128)} %collective-permute-done, f32[256,256]{1,0:T(8,128)S(1)} %slice.12, pred[]{:T(512)S(6)} %eq.56, ...), kind=kLoop, calls=%fused_computation.3 | loop fusion | flops 655360 | bytes 2097159 | tf_op jit(solution)/shard_map/stack | solution.py:343
  26.5 1.8 %collective-permute-done.5.refs_2_ = f32[256,512]{1,0:T(8,128)S(1)} collective-permute-done((f32[256,512]{1,0:T(8,128)S(1)}, f32[256,512]{1,0:T(8,128)S(1)}, u32[]{:S(2)}, u32[]{:S(2)}) %collective-permute-start.5) | collective-permute-done | bytes 524320 | tf_op jit(solution)/shard_map/ppermute | solution.py:303
  28.3 3.0 %collective-permute-done.4.refs_1_ = f32[256,512]{1,0:T(8,128)S(1)} collective-permute-done((f32[256,512]{1,0:T(8,128)S(1)}, f32[256,512]{1,0:T(8,128)S(1)}, u32[]{:S(2)}, u32[]{:S(2)}) %collective-permute-start.4) | collective-permute-done | bytes 524320 | tf_op jit(solution)/shard_map/ppermute | solution.py:303
  31.3 2.2 %collective-permute-start.13 = (f32[768,256]{1,0:T(8,128)S(1)}, f32[768,256]{1,0:T(8,128)}, u32[]{:S(2)}, u32[]{:S(2)}) collective-permute-start(f32[768,256]{1,0:T(8,128)S(1)} %slice.14), channel_id=1, source_target_pairs={{0,4},{1,5},{2,6},{8,12},{9,13},{10,14},{16,20},{17,21},{18,22},{2... | collective-permute-start | bytes 2359304 | tf_op jit(solution)/shard_map/ppermute | solution.py:303
  33.4 3.8 %collective-permute-start.8 = (f32[256,256]{1,0:T(8,128)S(1)}, f32[256,256]{1,0:T(8,128)S(1)}, u32[]{:S(2)}, u32[]{:S(2)}) collective-permute-start(f32[256,256]{1,0:T(8,128)S(1)} %get-tuple-element.34.refs_0_), channel_id=1, source_target_pairs={{0,24},{1,25},{2,26},{3,27},{4,28},{5,29},{6,30},{7,31},{8,16},{9,... | collective-permute-start | bytes 786440 | tf_op jit(solution)/shard_map/ppermute | solution.py:303
  37.2 3.2 %collective-permute-start.7 = (f32[256,256]{1,0:T(8,128)S(1)}, f32[256,256]{1,0:T(8,128)}, u32[]{:S(2)}, u32[]{:S(2)}) collective-permute-start(f32[256,256]{1,0:T(8,128)S(1)} %get-tuple-element.34.refs_0_), channel_id=1, source_target_pairs={{0,16},{1,17},{2,18},{3,19},{4,20},{5,21},{6,22},{7,23},{8,24},{9,... | collective-permute-start | bytes 786440 | tf_op jit(solution)/shard_map/ppermute | solution.py:303
  40.5 1.9 %collective-permute-start.6 = (f32[256,256]{1,0:T(8,128)S(1)}, f32[256,256]{1,0:T(8,128)}, u32[]{:S(2)}, u32[]{:S(2)}) collective-permute-start(f32[256,256]{1,0:T(8,128)S(1)} %get-tuple-element.34.refs_0_), channel_id=1, source_target_pairs={{0,8},{1,9},{2,10},{3,11},{4,12},{5,13},{6,14},{7,15},{8,0},{9,1},... | collective-permute-start | bytes 786440 | tf_op jit(solution)/shard_map/ppermute | solution.py:303
  42.8 3.1 %collective-permute-done.7.refs_2_ = f32[256,256]{1,0:T(8,128)} collective-permute-done((f32[256,256]{1,0:T(8,128)S(1)}, f32[256,256]{1,0:T(8,128)}, u32[]{:S(2)}, u32[]{:S(2)}) %collective-permute-start.7) | collective-permute-done | bytes 262176 | tf_op jit(solution)/shard_map/ppermute | solution.py:303
  45.9 2.9 %collective-permute-done.6.refs_1_ = f32[256,256]{1,0:T(8,128)} collective-permute-done((f32[256,256]{1,0:T(8,128)S(1)}, f32[256,256]{1,0:T(8,128)}, u32[]{:S(2)}, u32[]{:S(2)}) %collective-permute-start.6) | collective-permute-done | bytes 262176 | tf_op jit(solution)/shard_map/ppermute | solution.py:303
  51.9 7.3 %factor_head.2 = (f32[128,128]{1,0:T(8,128)}, f32[768,768]{1,0:T(8,128)}) custom-call(s32[2]{0:T(128)} %pad_add_fusion.place_ref, f32[256,256]{1,0:T(8,128)} %copy-done.4, f32[256,256]{1,0:T(8,128)} %collective-permute-done.6.refs_1_, f32[256,256]{1,0:T(8,128)} %collective-permute-done.7.refs_2_, f32[256,256]{1,0:T(8,128)} %copy-done.6, ...), custom_call_target="tpu_custom_call" | custom-call | flops 1000 | bytes 1000 | tf_op jit(solution)/shard_map/factor_head/pallas_call | solution.py:174
  59.3 2.1 %collective-permute-start.16 = (f32[768,256]{1,0:T(8,128)S(1)}, f32[768,256]{1,0:T(8,128)S(1)}, u32[]{:S(2)}, u32[]{:S(2)}) collective-permute-start(f32[768,256]{1,0:T(8,128)S(1)} %broadcast_select_fusion.refs_0_), channel_id=1, source_target_pairs={{0,2},{1,3},{2,0},{8,10},{9,11},{10,8},{16,18},{17,19},{18,16},{24... | collective-permute-start | bytes 2359304 | tf_op jit(solution)/shard_map/ppermute | solution.py:303
  61.5 2.9 %collective-permute-start.17 = (f32[256,512]{1,0:T(8,128)S(1)}, f32[256,512]{1,0:T(8,128)S(1)}, u32[]{:S(2)}, u32[]{:S(2)}) collective-permute-start(f32[256,512]{1,0:T(8,128)S(1)} %slice.15), channel_id=1, source_target_pairs={{0,24},{1,25},{2,26},{3,27},{4,28},{5,29},{6,30},{7,31},{8,16},{9,... | collective-permute-start | bytes 1572872 | tf_op jit(solution)/shard_map/ppermute | solution.py:303
  64.4 15.3 %factor_head.3 = (f32[3,256,256]{2,1,0:T(8,128)S(1)}, f32[768,768]{1,0:T(8,128)S(1)}) custom-call(s32[2]{0:T(128)S(1)} %copy-done.1, f32[128,128]{1,0:T(8,128)S(1)} %copy-done.3, f32[768,768]{1,0:T(8,128)S(1)} %copy-done.2), custom_call_target="tpu_custom_call" | custom-call | flops 15000000512 | bytes 1000 | tf_op jit(solution)/shard_map/factor_head/pallas_call | solution.py:174
  79.7 1.2 %solve_across.2.refs_4_ = f32[256,512]{1,0:T(8,128)S(1)} custom-call(s32[2]{0:T(128)S(1)} %copy-done.1, f32[3,256,256]{2,1,0:T(8,128)S(1)} %get-tuple-element.45.inverse_ref, f32[768,768]{1,0:T(8,128)S(1)} %get-tuple-element.46.head_ref, f32[256,512]{1,0:T(8,128)S(1)} %slice.13.refs_0_, f32[256,512]{1,0:T(8,128)S(1)} %collective-permute-done.4.refs_1_, ...), custom_call_target="tpu_custom_call" | custom-call | flops 4000000000 | bytes 5000000 | tf_op jit(solution)/shard_map/solve_across/pallas_call | solution.py:212
  81.5 3.3 %solve_across.3.refs_4_ = f32[768,512]{1,0:T(8,128)S(1)} custom-call(s32[2]{0:T(128)S(1)} %copy-done.1, f32[3,256,256]{2,1,0:T(8,128)S(1)} %get-tuple-element.45.inverse_ref, f32[768,768]{1,0:T(8,128)S(1)} %get-tuple-element.46.head_ref, f32[256,512]{1,0:T(8,128)S(1)} %slice.13.refs_0_, f32[256,512]{1,0:T(8,128)S(1)} %collective-permute-done.4.refs_1_, ...), custom_call_target="tpu_custom_call" | custom-call | flops 4000000000 | bytes 5000000 | tf_op jit(solution)/shard_map/solve_across/pallas_call | solution.py:212
  84.8 14.1 %update.1 = f32[1024,512]{1,0:T(8,128)} custom-call(s32[2]{0:T(128)S(1)} %copy-done.1, f32[3,256,256]{2,1,0:T(8,128)S(1)} %get-tuple-element.45.inverse_ref, f32[768,768]{1,0:T(8,128)S(1)} %get-tuple-element.46.head_ref, f32[2,256,256]{2,1,0:T(8,128)S(1)} %pad_maximum_fusion.top_ref, f32[2,256,256]{2,1,0:T(8,128)S(1)} %collective-permute-done.14.top_other_ref, ...), custom_call_target="tpu_custom_call" | custom-call | flops 10000000000 | bytes 10000000 | tf_op jit(solution)/shard_map/update/pallas_call | solution.py:282
  (41 shorter events, 7.3 us)
Async XLA Ops:
  1.0 15.5 %collective-permute-start.3 = (f32[256,256]{1,0:T(8,128)S(1)}, f32[256,256]{1,0:T(8,128)S(1)}, u32[]{:S(2)}, u32[]{:S(2)}) collective-permute-start(f32[256,256]{1,0:T(8,128)S(1)} %slice.12), channel_id=1, source_target_pairs={{18,19}} | collective-permute-start | bytes 786440 | tf_op jit(solution)/shard_map/ppermute | solution.py:303
  1.7 21.4 %collective-permute-start.2 = (f32[256,256]{1,0:T(8,128)S(1)}, f32[256,256]{1,0:T(8,128)S(1)}, u32[]{:S(2)}, u32[]{:S(2)}) collective-permute-start(f32[256,256]{1,0:T(8,128)S(1)} %slice.12), channel_id=1, source_target_pairs={{0,6},{1,7},{10,8},{9,15},{16,22},{18,17},{24,30},{25,31},{26,24}} | collective-permute-start | bytes 786440 | tf_op jit(solution)/shard_map/ppermute | solution.py:303
  8.6 14.4 %collective-permute-start.1 = (f32[256,256]{1,0:T(8,128)S(1)}, f32[256,256]{1,0:T(8,128)S(1)}, u32[]{:S(2)}, u32[]{:S(2)}) collective-permute-start(f32[256,256]{1,0:T(8,128)S(1)} %slice.12), channel_id=1, source_target_pairs={{0,4},{1,5},{10,14},{9,13},{16,20},{18,23},{24,28},{25,29},{26,30}} | collective-permute-start | bytes 786440 | tf_op jit(solution)/shard_map/ppermute | solution.py:303
  9.9 15.5 %collective-permute-start = (f32[256,256]{1,0:T(8,128)S(1)}, f32[256,256]{1,0:T(8,128)}, u32[]{:S(2)}, u32[]{:S(2)}) collective-permute-start(f32[256,256]{1,0:T(8,128)S(1)} %slice.12), channel_id=1, source_target_pairs={{0,2},{1,3},{10,12},{9,11},{16,18},{18,21},{24,26},{25,27},{26,28}} | collective-permute-start | bytes 786440 | tf_op jit(solution)/shard_map/ppermute | solution.py:303
  13.0 15.3 %collective-permute-start.5 = (f32[256,512]{1,0:T(8,128)S(1)}, f32[256,512]{1,0:T(8,128)S(1)}, u32[]{:S(2)}, u32[]{:S(2)}) collective-permute-start(f32[256,512]{1,0:T(8,128)S(1)} %slice.13.refs_0_), channel_id=1, source_target_pairs={{0,16},{1,17},{2,18},{3,19},{4,20},{5,21},{6,22},{7,23},{8,24},{9,... | collective-permute-start | bytes 1572872 | tf_op jit(solution)/shard_map/ppermute | solution.py:303
  16.5 14.8 %collective-permute-start.4 = (f32[256,512]{1,0:T(8,128)S(1)}, f32[256,512]{1,0:T(8,128)S(1)}, u32[]{:S(2)}, u32[]{:S(2)}) collective-permute-start(f32[256,512]{1,0:T(8,128)S(1)} %slice.13.refs_0_), channel_id=1, source_target_pairs={{0,8},{1,9},{2,10},{3,11},{4,12},{5,13},{6,14},{7,15},{8,0},{9,1},... | collective-permute-start | bytes 1572872 | tf_op jit(solution)/shard_map/ppermute | solution.py:303
  26.5 25.3 %copy-start.4 = (f32[256,256]{1,0:T(8,128)}, f32[256,256]{1,0:T(8,128)S(1)}, u32[]{:S(2)}) copy-start(f32[256,256]{1,0:T(8,128)S(1)} %get-tuple-element.34.refs_0_) | copy-start | bytes 786436
  31.3 27.9 %collective-permute-start.13 = (f32[768,256]{1,0:T(8,128)S(1)}, f32[768,256]{1,0:T(8,128)}, u32[]{:S(2)}, u32[]{:S(2)}) collective-permute-start(f32[768,256]{1,0:T(8,128)S(1)} %slice.14), channel_id=1, source_target_pairs={{0,4},{1,5},{2,6},{8,12},{9,13},{10,14},{16,20},{17,21},{18,22},{2... | collective-permute-start | bytes 2359304 | tf_op jit(solution)/shard_map/ppermute | solution.py:303
  33.4 9.4 %collective-permute-start.8 = (f32[256,256]{1,0:T(8,128)S(1)}, f32[256,256]{1,0:T(8,128)S(1)}, u32[]{:S(2)}, u32[]{:S(2)}) collective-permute-start(f32[256,256]{1,0:T(8,128)S(1)} %get-tuple-element.34.refs_0_), channel_id=1, source_target_pairs={{0,24},{1,25},{2,26},{3,27},{4,28},{5,29},{6,30},{7,31},{8,16},{9,... | collective-permute-start | bytes 786440 | tf_op jit(solution)/shard_map/ppermute | solution.py:303
  37.2 8.7 %collective-permute-start.7 = (f32[256,256]{1,0:T(8,128)S(1)}, f32[256,256]{1,0:T(8,128)}, u32[]{:S(2)}, u32[]{:S(2)}) collective-permute-start(f32[256,256]{1,0:T(8,128)S(1)} %get-tuple-element.34.refs_0_), channel_id=1, source_target_pairs={{0,16},{1,17},{2,18},{3,19},{4,20},{5,21},{6,22},{7,23},{8,24},{9,... | collective-permute-start | bytes 786440 | tf_op jit(solution)/shard_map/ppermute | solution.py:303
  40.5 8.4 %collective-permute-start.6 = (f32[256,256]{1,0:T(8,128)S(1)}, f32[256,256]{1,0:T(8,128)}, u32[]{:S(2)}, u32[]{:S(2)}) collective-permute-start(f32[256,256]{1,0:T(8,128)S(1)} %get-tuple-element.34.refs_0_), channel_id=1, source_target_pairs={{0,8},{1,9},{2,10},{3,11},{4,12},{5,13},{6,14},{7,15},{8,0},{9,1},... | collective-permute-start | bytes 786440 | tf_op jit(solution)/shard_map/ppermute | solution.py:303
  42.8 9.0 %copy-start.6 = (f32[256,256]{1,0:T(8,128)}, f32[256,256]{1,0:T(8,128)S(1)}, u32[]{:S(2)}) copy-start(f32[256,256]{1,0:T(8,128)S(1)} %collective-permute-done.8.refs_3_) | copy-start | bytes 786436
  48.8 2.0 %collective-permute-start.9 = (f32[256,256]{1,0:T(8,128)S(1)}, f32[256,256]{1,0:T(8,128)}, u32[]{:S(2)}, u32[]{:S(2)}) collective-permute-start(f32[256,256]{1,0:T(8,128)S(1)} %get-tuple-element.34.refs_0_), channel_id=1, source_target_pairs={{0,1},{1,0},{2,3},{3,2},{4,5},{5,4},{6,7},{7,6},{8,9},{9,8},{10,11... | collective-permute-start | bytes 786440 | tf_op jit(solution)/shard_map/ppermute | solution.py:303
  48.8 2.3 %collective-permute-start.10 = (f32[256,256]{1,0:T(8,128)}, f32[256,256]{1,0:T(8,128)}, u32[]{:S(2)}, u32[]{:S(2)}) collective-permute-start(f32[256,256]{1,0:T(8,128)} %collective-permute-done.6.refs_1_), channel_id=1, source_target_pairs={{0,1},{1,0},{2,3},{3,2},{4,5},{5,4},{6,7},{7,6},{8,9},{9,8},{10,11... | collective-permute-start | bytes 786440 | tf_op jit(solution)/shard_map/ppermute | solution.py:303
  49.3 2.5 %collective-permute-start.11 = (f32[256,256]{1,0:T(8,128)}, f32[256,256]{1,0:T(8,128)}, u32[]{:S(2)}, u32[]{:S(2)}) collective-permute-start(f32[256,256]{1,0:T(8,128)} %collective-permute-done.7.refs_2_), channel_id=1, source_target_pairs={{0,1},{1,0},{2,3},{3,2},{4,5},{5,4},{6,7},{7,6},{8,9},{9,8},{10,11... | collective-permute-start | bytes 786440 | tf_op jit(solution)/shard_map/ppermute | solution.py:303
  49.4 2.5 %collective-permute-start.12 = (f32[256,256]{1,0:T(8,128)S(1)}, f32[256,256]{1,0:T(8,128)}, u32[]{:S(2)}, u32[]{:S(2)}) collective-permute-start(f32[256,256]{1,0:T(8,128)S(1)} %collective-permute-done.8.refs_3_), channel_id=1, source_target_pairs={{0,1},{1,0},{2,3},{3,2},{4,5},{5,4},{6,7},{7,6},{8,9},{9,8},{10,11... | collective-permute-start | bytes 786440 | tf_op jit(solution)/shard_map/ppermute | solution.py:303
  49.9 11.6 %copy-start = (f32[1024,512]{1,0:T(8,128)S(1)}, f32[1024,512]{1,0:T(8,128)}, u32[]{:S(2)}) copy-start(f32[1024,512]{1,0:T(8,128)} %refs_5_) | copy-start | bytes 6291460
  59.2 5.2 %copy-start.2 = (f32[768,768]{1,0:T(8,128)S(1)}, f32[768,768]{1,0:T(8,128)}, u32[]{:S(2)}) copy-start(f32[768,768]{1,0:T(8,128)} %get-tuple-element.44.refs_1_) | copy-start | bytes 7077892
  59.2 5.2 %copy-start.3 = (f32[128,128]{1,0:T(8,128)S(1)}, f32[128,128]{1,0:T(8,128)}, u32[]{:S(2)}) copy-start(f32[128,128]{1,0:T(8,128)} %get-tuple-element.38.refs_0_) | copy-start | bytes 196612
  59.3 21.6 %collective-permute-start.16 = (f32[768,256]{1,0:T(8,128)S(1)}, f32[768,256]{1,0:T(8,128)S(1)}, u32[]{:S(2)}, u32[]{:S(2)}) collective-permute-start(f32[768,256]{1,0:T(8,128)S(1)} %broadcast_select_fusion.refs_0_), channel_id=1, source_target_pairs={{0,2},{1,3},{2,0},{8,10},{9,11},{10,8},{16,18},{17,19},{18,16},{24... | collective-permute-start | bytes 2359304 | tf_op jit(solution)/shard_map/ppermute | solution.py:303
  61.4 23.4 %collective-permute-start.15 = (f32[768,256]{1,0:T(8,128)S(1)}, f32[768,256]{1,0:T(8,128)S(1)}, u32[]{:S(2)}, u32[]{:S(2)}) collective-permute-start(f32[768,256]{1,0:T(8,128)S(1)} %broadcast_select_fusion.refs_0_), channel_id=1, source_target_pairs={{0,1},{1,0},{2,3},{3,2},{4,5},{5,4},{6,7},{7,6},{8,9},{9,8},{10,11... | collective-permute-start | bytes 2359304 | tf_op jit(solution)/shard_map/ppermute | solution.py:303
  61.5 18.2 %collective-permute-start.17 = (f32[256,512]{1,0:T(8,128)S(1)}, f32[256,512]{1,0:T(8,128)S(1)}, u32[]{:S(2)}, u32[]{:S(2)}) collective-permute-start(f32[256,512]{1,0:T(8,128)S(1)} %slice.15), channel_id=1, source_target_pairs={{0,24},{1,25},{2,26},{3,27},{4,28},{5,29},{6,30},{7,31},{8,16},{9,... | collective-permute-start | bytes 1572872 | tf_op jit(solution)/shard_map/ppermute | solution.py:303
  80.9 3.9 %collective-permute-start.18 = (f32[768,256]{1,0:T(8,128)S(1)}, f32[768,256]{1,0:T(8,128)S(1)}, u32[]{:S(2)}, u32[]{:S(2)}) collective-permute-start(f32[768,256]{1,0:T(8,128)S(1)} %collective-permute-done.16.refs_2_), channel_id=1, source_target_pairs={{0,1},{1,0},{2,3},{3,2},{4,5},{5,4},{6,7},{7,6},{8,9},{9,8},{10,11... | collective-permute-start | bytes 2359304 | tf_op jit(solution)/shard_map/ppermute | solution.py:303
  81.2 3.6 %collective-permute-start.14 = (f32[2,256,256]{2,1,0:T(8,128)S(1)}, f32[2,256,256]{2,1,0:T(8,128)S(1)}, u32[]{:S(2)}, u32[]{:S(2)}) collective-permute-start(f32[2,256,256]{2,1,0:T(8,128)S(1)} %pad_maximum_fusion.top_ref), channel_id=1, source_target_pairs={{0,1},{1,0},{2,3},{3,2},{4,5},{5,4},{6,7},{7,6},{8,9},{9,8},{10,11... | collective-permute-start | bytes 1572872 | tf_op jit(solution)/shard_map/ppermute | solution.py:303
  (2 other events, 5.9 us)

commit v6 on v5

--- a/solution.py
+++ b/solution.py
@@ -180,7 +180,7 @@
         in_specs=[pl.BlockSpec(memory_space=pltpu.SMEM)] + [pl.BlockSpec(memory_space=pltpu.VMEM)] * len(blocks),
         out_specs=[pl.BlockSpec(memory_space=pltpu.VMEM)] * 2,
         cost_estimate=pl.CostEstimate(flops=15_000_000_000 if begin else 1_000, bytes_accessed=1_000, transcendentals=0),
-        compiler_params=pltpu.CompilerParams(vmem_limit_bytes=(14 if begin else 56) * MIB),
+        compiler_params=pltpu.CompilerParams(vmem_limit_bytes=(14 if begin else 48) * MIB),
         name="factor_head",
     )(place, *blocks)
 
@@ -334,13 +334,13 @@
             native = native | ((my_row == i) & (my_col == j))
     carried = jnp.where(native, corner, carried)
     heads = along_rows(matrix[:NB], 0, EARLY)
-    carried, heads, place = lax.optimization_barrier((carried, heads, place))
+    carried, heads[:2], place = lax.optimization_barrier((carried, heads[:2], place))
     found = along_rows(carried, 0, grid_rows)
     top_mine, top_last = corner, corner
     for d in range(1, planes):
         top_mine = jnp.where(plane == d, passed[d - 1], top_mine)
         top_last = jnp.where((plane - 1) % planes == d, passed[d - 1], top_last)
-    found, top = lax.optimization_barrier((found, jnp.stack([top_mine, top_last])))
+    found, top, heads = lax.optimization_barrier((found, jnp.stack([top_mine, top_last]), heads))
     mirrored = [swap_cores(x) for x in found]
     strip, _ = lax.optimization_barrier((matrix[NB:, :NB], carried))
 

time: 99.4 us -> 97.7 us (0.983)
  waiting for transfers between devices: 14.8 us -> 12.1 us
  Pallas kernels: 41.2 us -> 38.8 us
  starting transfers between devices: 36.7 us -> 38.6 us
  local copies, waits for them, and re-layouts: 3.99 us -> 5.79 us
    ppermute x19, waiting for transfers between devices: 14.8 us -> 12.1 us  [send(): return lax.ppermute(x, ('row', 'col'), flat)]
    pallas_call x2, Pallas kernels: 22.6 us -> 20.2 us  [factor_head(): pl.pallas_call(functools.partial(head_kernel, begin, end), out_shape=[jax...]
    ppermute x19, starting transfers between devices: 36.7 us -> 38.6 us  [send(): return lax.ppermute(x, ('row', 'col'), flat)]
    select_n x1, other arithmetic: 0.11 us -> 1.25 us  [body(): held = jnp.where(plane // distance % 2 == 1, got, held)]
    another operation x2, other arithmetic: 1.16 us -> 0.13 us  [body(): jnp.stack([top_mine, top_last])]
  transfers between devices with their start and end apart: 19 -> 19, of which waited for: 9 -> 9; matrix products, arithmetic and copies ran while one was open for 4% -> 3% of each run, Pallas kernels for 27% -> 25%
where the time goes in v6:
time: 97.7 us; the launch traced here: 97.1 us
  Pallas kernels  38.8 us (40%)
  starting transfers between devices  38.6 us (40%)
  waiting for transfers between devices  12.1 us (12%)
  local copies, waits for them, and re-layouts  5.79 us (6%)
  other arithmetic  1.46 us (1%)
    ppermute x19, starting transfers between devices, send(): return lax.ppermute(x, ('row', 'col'), flat)  38.6 us
    pallas_call x2, Pallas kernels, factor_head(): pl.pallas_call(functools.partial(head_kernel, begin, end), out_shape=[jax...  20.2 us
    pallas_call x1, Pallas kernels, update(): pl.pallas_call(functools.partial(update_kernel, grid_rows), out_shape=jax...  14.1 us
    ppermute x19, waiting for transfers between devices, send(): return lax.ppermute(x, ('row', 'col'), flat)  12.1 us
    pallas_call x2, Pallas kernels, solve_across(): pl.pallas_call(functools.partial(across_kernel, begin, end), out_shape=ja...  4.53 us
    slice x1, local copies, waits for them, and re-layouts, body(): strip, _ = lax.optimization_barrier((matrix[NB:, :NB], carried))  2.07 us
  transfers between devices with their start and end apart: 19, of which 9 were waited for; matrix products, arithmetic and copies ran while one was open for 3% of the time, Pallas kernels for 25%

profile of v6, /device:TPU:0, one launch (start us, length us, event | category | flops | bytes accessed | tf_op | source)
XLA Modules:
  0.0 97.1 jit_solution(14810700673723215488)
XLA Ops:
  0.0 1.0 slice.12
  1.7 7.0 %collective-permute-start.2 = (f32[256,256]{1,0:T(8,128)S(1)}, f32[256,256]{1,0:T(8,128)S(1)}, u32[]{:S(2)}, u32[]{:S(2)}) collective-permute-start(f32[256,256]{1,0:T(8,128)S(1)} %slice.12), channel_id=1, source_target_pairs={{0,6},{1,7},{10,8},{9,15},{16,22},{18,17},{24,30},{25,31},{26,24}} | collective-permute-start | bytes 786440 | tf_op jit(solution)/shard_map/ppermute | solution.py:303
  8.6 1.3 %collective-permute-start.1 = (f32[256,256]{1,0:T(8,128)S(1)}, f32[256,256]{1,0:T(8,128)S(1)}, u32[]{:S(2)}, u32[]{:S(2)}) collective-permute-start(f32[256,256]{1,0:T(8,128)S(1)} %slice.12), channel_id=1, source_target_pairs={{0,4},{1,5},{10,14},{9,13},{16,20},{18,23},{24,28},{25,29},{26,30}} | collective-permute-start | bytes 786440 | tf_op jit(solution)/shard_map/ppermute | solution.py:303
  9.9 1.3 %collective-permute-start = (f32[256,256]{1,0:T(8,128)S(1)}, f32[256,256]{1,0:T(8,128)S(1)}, u32[]{:S(2)}, u32[]{:S(2)}) collective-permute-start(f32[256,256]{1,0:T(8,128)S(1)} %slice.12), channel_id=1, source_target_pairs={{0,2},{1,3},{10,12},{9,11},{16,18},{18,21},{24,26},{25,27},{26,28}} | collective-permute-start | bytes 786440 | tf_op jit(solution)/shard_map/ppermute | solution.py:303
  11.3 1.1 %slice.13.refs_0_ = f32[256,512]{1,0:T(8,128)S(1)} slice(f32[1024,512]{1,0:T(8,128)} %refs_5_), slice={[0:256], [0:512]} | slice | bytes 1048576 | tf_op jit(solution)/shard_map/slice | solution.py:336
  12.3 1.9 %collective-permute-start.4 = (f32[256,512]{1,0:T(8,128)S(1)}, f32[256,512]{1,0:T(8,128)S(1)}, u32[]{:S(2)}, u32[]{:S(2)}) collective-permute-start(f32[256,512]{1,0:T(8,128)S(1)} %slice.13.refs_0_), channel_id=1, source_target_pairs={{0,8},{1,9},{2,10},{3,11},{4,12},{5,13},{6,14},{7,15},{8,0},{9,1},... | collective-permute-start | bytes 1572872 | tf_op jit(solution)/shard_map/ppermute | solution.py:303
  14.3 2.1 %slice.14 = f32[768,256]{1,0:T(8,128)} slice(f32[1024,512]{1,0:T(8,128)} %refs_5_), slice={[256:1024], [0:256]} | slice | bytes 1572864 | tf_op jit(solution)/shard_map/slice | solution.py:345
  16.5 6.1 %collective-permute-start.8 = (f32[256,512]{1,0:T(8,128)S(1)}, f32[256,512]{1,0:T(8,128)S(1)}, u32[]{:S(2)}, u32[]{:S(2)}) collective-permute-start(f32[256,512]{1,0:T(8,128)S(1)} %slice.13.refs_0_), channel_id=1, source_target_pairs={{0,16},{1,17},{2,18},{3,19},{4,20},{5,21},{6,22},{7,23},{8,24},{9,... | collective-permute-start | bytes 1572872 | tf_op jit(solution)/shard_map/ppermute | solution.py:303
  22.6 2.8 %collective-permute-done = f32[256,256]{1,0:T(8,128)S(1)} collective-permute-done((f32[256,256]{1,0:T(8,128)S(1)}, f32[256,256]{1,0:T(8,128)S(1)}, u32[]{:S(2)}, u32[]{:S(2)}) %collective-permute-start) | collective-permute-done | bytes 262176 | tf_op jit(solution)/shard_map/ppermute | solution.py:303
  25.5 2.1 %collective-permute-done.4.refs_1_ = f32[256,512]{1,0:T(8,128)S(1)} collective-permute-done((f32[256,512]{1,0:T(8,128)S(1)}, f32[256,512]{1,0:T(8,128)S(1)}, u32[]{:S(2)}, u32[]{:S(2)}) %collective-permute-start.4) | collective-permute-done | bytes 524320 | tf_op jit(solution)/shard_map/ppermute | solution.py:303
  28.5 2.2 %collective-permute-start.13 = (f32[768,256]{1,0:T(8,128)}, f32[768,256]{1,0:T(8,128)}, u32[]{:S(2)}, u32[]{:S(2)}) collective-permute-start(f32[768,256]{1,0:T(8,128)} %slice.14), channel_id=1, source_target_pairs={{0,4},{1,5},{2,6},{8,12},{9,13},{10,14},{16,20},{17,21},{18,22},{2... | collective-permute-start | bytes 2359304 | tf_op jit(solution)/shard_map/ppermute | solution.py:303
  30.6 6.2 %collective-permute-start.7 = (f32[256,256]{1,0:T(8,128)S(1)}, f32[256,256]{1,0:T(8,128)S(1)}, u32[]{:S(2)}, u32[]{:S(2)}) collective-permute-start(f32[256,256]{1,0:T(8,128)S(1)} %get-tuple-element.38.refs_0_), channel_id=1, source_target_pairs={{0,24},{1,25},{2,26},{3,27},{4,28},{5,29},{6,30},{7,31},{8,16},{9,... | collective-permute-start | bytes 786440 | tf_op jit(solution)/shard_map/ppermute | solution.py:303
  36.9 1.9 %collective-permute-start.6 = (f32[256,256]{1,0:T(8,128)S(1)}, f32[256,256]{1,0:T(8,128)S(1)}, u32[]{:S(2)}, u32[]{:S(2)}) collective-permute-start(f32[256,256]{1,0:T(8,128)S(1)} %get-tuple-element.38.refs_0_), channel_id=1, source_target_pairs={{0,16},{1,17},{2,18},{3,19},{4,20},{5,21},{6,22},{7,23},{8,24},{9,... | collective-permute-start | bytes 786440 | tf_op jit(solution)/shard_map/ppermute | solution.py:303
  38.8 1.9 %collective-permute-start.5 = (f32[256,256]{1,0:T(8,128)S(1)}, f32[256,256]{1,0:T(8,128)S(1)}, u32[]{:S(2)}, u32[]{:S(2)}) collective-permute-start(f32[256,256]{1,0:T(8,128)S(1)} %get-tuple-element.38.refs_0_), channel_id=1, source_target_pairs={{0,8},{1,9},{2,10},{3,11},{4,12},{5,13},{6,14},{7,15},{8,0},{9,1},... | collective-permute-start | bytes 786440 | tf_op jit(solution)/shard_map/ppermute | solution.py:303
  42.4 2.7 %collective-permute-done.6.refs_2_ = f32[256,256]{1,0:T(8,128)S(1)} collective-permute-done((f32[256,256]{1,0:T(8,128)S(1)}, f32[256,256]{1,0:T(8,128)S(1)}, u32[]{:S(2)}, u32[]{:S(2)}) %collective-permute-start.6) | collective-permute-done | bytes 262176 | tf_op jit(solution)/shard_map/ppermute | solution.py:303
  45.1 1.9 %collective-permute-done.5.refs_1_ = f32[256,256]{1,0:T(8,128)S(1)} collective-permute-done((f32[256,256]{1,0:T(8,128)S(1)}, f32[256,256]{1,0:T(8,128)S(1)}, u32[]{:S(2)}, u32[]{:S(2)}) %collective-permute-start.5) | collective-permute-done | bytes 262176 | tf_op jit(solution)/shard_map/ppermute | solution.py:303
  49.7 4.9 %factor_head.2 = (f32[128,128]{1,0:T(8,128)S(1)}, f32[768,768]{1,0:T(8,128)S(1)}) custom-call(s32[2]{0:T(128)S(1)} %pad_add_fusion.place_ref, f32[256,256]{1,0:T(8,128)S(1)} %get-tuple-element.38.refs_0_, f32[256,256]{1,0:T(8,128)S(1)} %collective-permute-done.5.refs_1_, f32[256,256]{1,0:T(8,128)S(1)} %collective-permute-done.6.refs_2_, ...), custom_call_target="tpu_custom_call" | custom-call | flops 1000 | bytes 1000 | tf_op jit(solution)/shard_map/factor_head/pallas_call | solution.py:174
  54.7 1.2 %broadcast_select_fusion.refs_0_ = f32[768,256]{1,0:T(8,128)S(1)} fusion(f32[768,256]{1,0:T(8,128)} %collective-permute-done.13, f32[768,256]{1,0:T(8,128)} %slice.14, pred[]{:T(512)S(6)} %eq.60), kind=kLoop, calls=%fused_computation.1 | loop fusion | flops 196608 | bytes 2359297 | tf_op jit(solution)/shard_map/jit(_where)/select_n | solution.py:360
  55.9 3.5 %collective-permute-start.16 = (f32[768,256]{1,0:T(8,128)S(1)}, f32[768,256]{1,0:T(8,128)S(1)}, u32[]{:S(2)}, u32[]{:S(2)}) collective-permute-start(f32[768,256]{1,0:T(8,128)S(1)} %broadcast_select_fusion.refs_0_), channel_id=1, source_target_pairs={{0,2},{1,3},{2,0},{8,10},{9,11},{10,8},{16,18},{17,19},{18,16},{24... | collective-permute-start | bytes 2359304 | tf_op jit(solution)/shard_map/ppermute | solution.py:303
  59.6 2.9 %collective-permute-start.17 = (f32[256,512]{1,0:T(8,128)S(1)}, f32[256,512]{1,0:T(8,128)S(1)}, u32[]{:S(2)}, u32[]{:S(2)}) collective-permute-start(f32[256,512]{1,0:T(8,128)S(1)} %slice.15), channel_id=1, source_target_pairs={{0,24},{1,25},{2,26},{3,27},{4,28},{5,29},{6,30},{7,31},{8,16},{9,... | collective-permute-start | bytes 1572872 | tf_op jit(solution)/shard_map/ppermute | solution.py:303
  62.5 15.3 %factor_head.3 = (f32[3,256,256]{2,1,0:T(8,128)S(1)}, f32[768,768]{1,0:T(8,128)S(1)}) custom-call(s32[2]{0:T(128)S(1)} %pad_add_fusion.place_ref, f32[128,128]{1,0:T(8,128)S(1)} %get-tuple-element.42.refs_0_, f32[768,768]{1,0:T(8,128)S(1)} %get-tuple-element.48.refs_1_), custom_call_target="tpu_custom_call" | custom-call | flops 15000000512 | bytes 1000 | tf_op jit(solution)/shard_map/factor_head/pallas_call | solution.py:174
  77.8 1.2 %solve_across.2.refs_4_ = f32[256,512]{1,0:T(8,128)S(1)} custom-call(s32[2]{0:T(128)S(1)} %pad_add_fusion.place_ref, f32[3,256,256]{2,1,0:T(8,128)S(1)} %get-tuple-element.49.inverse_ref, f32[768,768]{1,0:T(8,128)S(1)} %get-tuple-element.50.head_ref, f32[256,512]{1,0:T(8,128)S(1)} %slice.13.refs_0_, f32[256,512]{1,0:T(8,128)S(1)} %copy-done.2, ...), custom_call_target="tpu_custom_call" | custom-call | flops 4000000000 | bytes 5000000 | tf_op jit(solution)/shard_map/solve_across/pallas_call | solution.py:212
  79.6 3.3 %solve_across.3.refs_4_ = f32[768,512]{1,0:T(8,128)S(1)} custom-call(s32[2]{0:T(128)S(1)} %pad_add_fusion.place_ref, f32[3,256,256]{2,1,0:T(8,128)S(1)} %get-tuple-element.49.inverse_ref, f32[768,768]{1,0:T(8,128)S(1)} %get-tuple-element.50.head_ref, f32[256,512]{1,0:T(8,128)S(1)} %slice.13.refs_0_, f32[256,512]{1,0:T(8,128)S(1)} %copy-done.2, ...), custom_call_target="tpu_custom_call" | custom-call | flops 4000000000 | bytes 5000000 | tf_op jit(solution)/shard_map/solve_across/pallas_call | solution.py:212
  83.0 14.1 %update.1 = f32[1024,512]{1,0:T(8,128)} custom-call(s32[2]{0:T(128)S(1)} %pad_add_fusion.place_ref, f32[3,256,256]{2,1,0:T(8,128)S(1)} %get-tuple-element.49.inverse_ref, f32[768,768]{1,0:T(8,128)S(1)} %get-tuple-element.50.head_ref, f32[2,256,256]{2,1,0:T(8,128)S(1)} %pad_maximum_fusion.top_ref, f32[2,256,256]{2,1,0:T(8,128)S(1)} %collective-permute-done.14.top_other_ref, ...), custom_call_target="tpu_custom_call" | custom-call | flops 10000000000 | bytes 10000000 | tf_op jit(solution)/shard_map/update/pallas_call | solution.py:282
  (37 shorter events, 6.7 us)
Async XLA Ops:
  1.0 15.5 %collective-permute-start.3 = (f32[256,256]{1,0:T(8,128)S(1)}, f32[256,256]{1,0:T(8,128)S(1)}, u32[]{:S(2)}, u32[]{:S(2)}) collective-permute-start(f32[256,256]{1,0:T(8,128)S(1)} %slice.12), channel_id=1, source_target_pairs={{18,19}} | collective-permute-start | bytes 786440 | tf_op jit(solution)/shard_map/ppermute | solution.py:303
  1.7 20.9 %collective-permute-start.2 = (f32[256,256]{1,0:T(8,128)S(1)}, f32[256,256]{1,0:T(8,128)S(1)}, u32[]{:S(2)}, u32[]{:S(2)}) collective-permute-start(f32[256,256]{1,0:T(8,128)S(1)} %slice.12), channel_id=1, source_target_pairs={{0,6},{1,7},{10,8},{9,15},{16,22},{18,17},{24,30},{25,31},{26,24}} | collective-permute-start | bytes 786440 | tf_op jit(solution)/shard_map/ppermute | solution.py:303
  8.6 14.0 %collective-permute-start.1 = (f32[256,256]{1,0:T(8,128)S(1)}, f32[256,256]{1,0:T(8,128)S(1)}, u32[]{:S(2)}, u32[]{:S(2)}) collective-permute-start(f32[256,256]{1,0:T(8,128)S(1)} %slice.12), channel_id=1, source_target_pairs={{0,4},{1,5},{10,14},{9,13},{16,20},{18,23},{24,28},{25,29},{26,30}} | collective-permute-start | bytes 786440 | tf_op jit(solution)/shard_map/ppermute | solution.py:303
  9.9 15.5 %collective-permute-start = (f32[256,256]{1,0:T(8,128)S(1)}, f32[256,256]{1,0:T(8,128)S(1)}, u32[]{:S(2)}, u32[]{:S(2)}) collective-permute-start(f32[256,256]{1,0:T(8,128)S(1)} %slice.12), channel_id=1, source_target_pairs={{0,2},{1,3},{10,12},{9,11},{16,18},{18,21},{24,26},{25,27},{26,28}} | collective-permute-start | bytes 786440 | tf_op jit(solution)/shard_map/ppermute | solution.py:303
  12.3 15.3 %collective-permute-start.4 = (f32[256,512]{1,0:T(8,128)S(1)}, f32[256,512]{1,0:T(8,128)S(1)}, u32[]{:S(2)}, u32[]{:S(2)}) collective-permute-start(f32[256,512]{1,0:T(8,128)S(1)} %slice.13.refs_0_), channel_id=1, source_target_pairs={{0,8},{1,9},{2,10},{3,11},{4,12},{5,13},{6,14},{7,15},{8,0},{9,1},... | collective-permute-start | bytes 1572872 | tf_op jit(solution)/shard_map/ppermute | solution.py:303
  16.5 24.3 %collective-permute-start.8 = (f32[256,512]{1,0:T(8,128)S(1)}, f32[256,512]{1,0:T(8,128)S(1)}, u32[]{:S(2)}, u32[]{:S(2)}) collective-permute-start(f32[256,512]{1,0:T(8,128)S(1)} %slice.13.refs_0_), channel_id=1, source_target_pairs={{0,16},{1,17},{2,18},{3,19},{4,20},{5,21},{6,22},{7,23},{8,24},{9,... | collective-permute-start | bytes 1572872 | tf_op jit(solution)/shard_map/ppermute | solution.py:303
  27.6 0.8 copy-start.1
  28.5 26.2 %collective-permute-start.13 = (f32[768,256]{1,0:T(8,128)}, f32[768,256]{1,0:T(8,128)}, u32[]{:S(2)}, u32[]{:S(2)}) collective-permute-start(f32[768,256]{1,0:T(8,128)} %slice.14), channel_id=1, source_target_pairs={{0,4},{1,5},{2,6},{8,12},{9,13},{10,14},{16,20},{17,21},{18,22},{2... | collective-permute-start | bytes 2359304 | tf_op jit(solution)/shard_map/ppermute | solution.py:303
  30.6 11.8 %collective-permute-start.7 = (f32[256,256]{1,0:T(8,128)S(1)}, f32[256,256]{1,0:T(8,128)S(1)}, u32[]{:S(2)}, u32[]{:S(2)}) collective-permute-start(f32[256,256]{1,0:T(8,128)S(1)} %get-tuple-element.38.refs_0_), channel_id=1, source_target_pairs={{0,24},{1,25},{2,26},{3,27},{4,28},{5,29},{6,30},{7,31},{8,16},{9,... | collective-permute-start | bytes 786440 | tf_op jit(solution)/shard_map/ppermute | solution.py:303
  36.9 8.3 %collective-permute-start.6 = (f32[256,256]{1,0:T(8,128)S(1)}, f32[256,256]{1,0:T(8,128)S(1)}, u32[]{:S(2)}, u32[]{:S(2)}) collective-permute-start(f32[256,256]{1,0:T(8,128)S(1)} %get-tuple-element.38.refs_0_), channel_id=1, source_target_pairs={{0,16},{1,17},{2,18},{3,19},{4,20},{5,21},{6,22},{7,23},{8,24},{9,... | collective-permute-start | bytes 786440 | tf_op jit(solution)/shard_map/ppermute | solution.py:303
  38.8 8.3 %collective-permute-start.5 = (f32[256,256]{1,0:T(8,128)S(1)}, f32[256,256]{1,0:T(8,128)S(1)}, u32[]{:S(2)}, u32[]{:S(2)}) collective-permute-start(f32[256,256]{1,0:T(8,128)S(1)} %get-tuple-element.38.refs_0_), channel_id=1, source_target_pairs={{0,8},{1,9},{2,10},{3,11},{4,12},{5,13},{6,14},{7,15},{8,0},{9,1},... | collective-permute-start | bytes 786440 | tf_op jit(solution)/shard_map/ppermute | solution.py:303
  40.8 0.8 copy-start.3
  47.1 1.5 %collective-permute-start.9 = (f32[256,256]{1,0:T(8,128)S(1)}, f32[256,256]{1,0:T(8,128)S(1)}, u32[]{:S(2)}, u32[]{:S(2)}) collective-permute-start(f32[256,256]{1,0:T(8,128)S(1)} %get-tuple-element.38.refs_0_), channel_id=1, source_target_pairs={{0,1},{1,0},{2,3},{3,2},{4,5},{5,4},{6,7},{7,6},{8,9},{9,8},{10,11... | collective-permute-start | bytes 786440 | tf_op jit(solution)/shard_map/ppermute | solution.py:303
  47.1 1.9 %collective-permute-start.10 = (f32[256,256]{1,0:T(8,128)S(1)}, f32[256,256]{1,0:T(8,128)S(1)}, u32[]{:S(2)}, u32[]{:S(2)}) collective-permute-start(f32[256,256]{1,0:T(8,128)S(1)} %collective-permute-done.5.refs_1_), channel_id=1, source_target_pairs={{0,1},{1,0},{2,3},{3,2},{4,5},{5,4},{6,7},{7,6},{8,9},{9,8},{10,11... | collective-permute-start | bytes 786440 | tf_op jit(solution)/shard_map/ppermute | solution.py:303
  47.6 1.8 %collective-permute-start.11 = (f32[256,256]{1,0:T(8,128)S(1)}, f32[256,256]{1,0:T(8,128)S(1)}, u32[]{:S(2)}, u32[]{:S(2)}) collective-permute-start(f32[256,256]{1,0:T(8,128)S(1)} %collective-permute-done.6.refs_2_), channel_id=1, source_target_pairs={{0,1},{1,0},{2,3},{3,2},{4,5},{5,4},{6,7},{7,6},{8,9},{9,8},{10,11... | collective-permute-start | bytes 786440 | tf_op jit(solution)/shard_map/ppermute | solution.py:303
  47.6 2.1 %collective-permute-start.12 = (f32[256,256]{1,0:T(8,128)S(1)}, f32[256,256]{1,0:T(8,128)S(1)}, u32[]{:S(2)}, u32[]{:S(2)}) collective-permute-start(f32[256,256]{1,0:T(8,128)S(1)} %collective-permute-done.7.refs_3_), channel_id=1, source_target_pairs={{0,1},{1,0},{2,3},{3,2},{4,5},{5,4},{6,7},{7,6},{8,9},{9,8},{10,11... | collective-permute-start | bytes 786440 | tf_op jit(solution)/shard_map/ppermute | solution.py:303
  48.1 11.4 %copy-start = (f32[1024,512]{1,0:T(8,128)S(1)}, f32[1024,512]{1,0:T(8,128)}, u32[]{:S(2)}) copy-start(f32[1024,512]{1,0:T(8,128)} %refs_5_) | copy-start | bytes 6291460
  55.9 23.1 %collective-permute-start.16 = (f32[768,256]{1,0:T(8,128)S(1)}, f32[768,256]{1,0:T(8,128)S(1)}, u32[]{:S(2)}, u32[]{:S(2)}) collective-permute-start(f32[768,256]{1,0:T(8,128)S(1)} %broadcast_select_fusion.refs_0_), channel_id=1, source_target_pairs={{0,2},{1,3},{2,0},{8,10},{9,11},{10,8},{16,18},{17,19},{18,16},{24... | collective-permute-start | bytes 2359304 | tf_op jit(solution)/shard_map/ppermute | solution.py:303
  59.5 23.5 %collective-permute-start.15 = (f32[768,256]{1,0:T(8,128)S(1)}, f32[768,256]{1,0:T(8,128)S(1)}, u32[]{:S(2)}, u32[]{:S(2)}) collective-permute-start(f32[768,256]{1,0:T(8,128)S(1)} %broadcast_select_fusion.refs_0_), channel_id=1, source_target_pairs={{0,1},{1,0},{2,3},{3,2},{4,5},{5,4},{6,7},{7,6},{8,9},{9,8},{10,11... | collective-permute-start | bytes 2359304 | tf_op jit(solution)/shard_map/ppermute | solution.py:303
  59.6 18.2 %collective-permute-start.17 = (f32[256,512]{1,0:T(8,128)S(1)}, f32[256,512]{1,0:T(8,128)S(1)}, u32[]{:S(2)}, u32[]{:S(2)}) collective-permute-start(f32[256,512]{1,0:T(8,128)S(1)} %slice.15), channel_id=1, source_target_pairs={{0,24},{1,25},{2,26},{3,27},{4,28},{5,29},{6,30},{7,31},{8,16},{9,... | collective-permute-start | bytes 1572872 | tf_op jit(solution)/shard_map/ppermute | solution.py:303
  62.5 15.3 %copy-start.2 = (f32[256,512]{1,0:T(8,128)S(1)}, f32[256,512]{1,0:T(8,128)}, u32[]{:S(2)}) copy-start(f32[256,512]{1,0:T(8,128)} %copy-done.1) | copy-start | bytes 1572868
  62.5 15.3 %copy-start.4 = (f32[256,512]{1,0:T(8,128)S(1)}, f32[256,512]{1,0:T(8,128)}, u32[]{:S(2)}) copy-start(f32[256,512]{1,0:T(8,128)} %copy-done.3) | copy-start | bytes 1572868
  79.1 3.9 %collective-permute-start.18 = (f32[768,256]{1,0:T(8,128)S(1)}, f32[768,256]{1,0:T(8,128)S(1)}, u32[]{:S(2)}, u32[]{:S(2)}) collective-permute-start(f32[768,256]{1,0:T(8,128)S(1)} %collective-permute-done.16.refs_2_), channel_id=1, source_target_pairs={{0,1},{1,0},{2,3},{3,2},{4,5},{5,4},{6,7},{7,6},{8,9},{9,8},{10,11... | collective-permute-start | bytes 2359304 | tf_op jit(solution)/shard_map/ppermute | solution.py:303
  79.3 3.6 %collective-permute-start.14 = (f32[2,256,256]{2,1,0:T(8,128)S(1)}, f32[2,256,256]{2,1,0:T(8,128)S(1)}, u32[]{:S(2)}, u32[]{:S(2)}) collective-permute-start(f32[2,256,256]{2,1,0:T(8,128)S(1)} %pad_maximum_fusion.top_ref), channel_id=1, source_target_pairs={{0,1},{1,0},{2,3},{3,2},{4,5},{5,4},{6,7},{7,6},{8,9},{9,8},{10,11... | collective-permute-start | bytes 1572872 | tf_op jit(solution)/shard_map/ppermute | solution.py:303

commit v7 on v6

--- a/solution.py
+++ b/solution.py
@@ -278,6 +278,8 @@
 def update(grid_rows, place, inverse, head, top, top_other, sent, across, matrix):
     whole = pl.BlockSpec(memory_space=pltpu.VMEM)
     depth = 2 * NB if matrix.shape[0] % (2 * NB) == 0 else NB
+    if matrix.shape[1] <= 2 * NB:
+        depth = matrix.shape[0]
     strip = pl.BlockSpec((depth, matrix.shape[1]), lambda step: (step, 0))
     return pl.pallas_call(
         functools.partial(update_kernel, grid_rows),

time: 97.7 us -> 97.9 us (level)
  no operation moved by 1% of the time
where the time goes in v7:
time: 97.9 us; the launch traced here: 97.3 us
  Pallas kernels  39 us (40%)
  starting transfers between devices  38.6 us (39%)
  waiting for transfers between devices  12.1 us (12%)
  local copies, waits for them, and re-layouts  5.79 us (6%)
  other arithmetic  1.46 us (1%)
    ppermute x19, starting transfers between devices, send(): return lax.ppermute(x, ('row', 'col'), flat)  38.6 us
    pallas_call x2, Pallas kernels, factor_head(): pl.pallas_call(functools.partial(head_kernel, begin, end), out_shape=[jax...  20.2 us
    pallas_call x1, Pallas kernels, update(): pl.pallas_call(functools.partial(update_kernel, grid_rows), out_shape=jax...  14.3 us
    ppermute x19, waiting for transfers between devices, send(): return lax.ppermute(x, ('row', 'col'), flat)  12.1 us
    pallas_call x2, Pallas kernels, solve_across(): pl.pallas_call(functools.partial(across_kernel, begin, end), out_shape=ja...  4.53 us
    slice x1, local copies, waits for them, and re-layouts, body(): strip, _ = lax.optimization_barrier((matrix[NB:, :NB], carried))  2.07 us
  transfers between devices with their start and end apart: 19, of which 9 were waited for; matrix products, arithmetic and copies ran while one was open for 3% of the time, Pallas kernels for 25%

profile of v7, /device:TPU:0, one launch (start us, length us, event | category | flops | bytes accessed | tf_op | source)
XLA Modules:
  0.0 97.3 jit_solution(329779137375333309)
XLA Ops:
  0.0 1.0 slice.12
  1.7 7.0 %collective-permute-start.2 = (f32[256,256]{1,0:T(8,128)S(1)}, f32[256,256]{1,0:T(8,128)S(1)}, u32[]{:S(2)}, u32[]{:S(2)}) collective-permute-start(f32[256,256]{1,0:T(8,128)S(1)} %slice.12), channel_id=1, source_target_pairs={{0,6},{1,7},{10,8},{9,15},{16,22},{18,17},{24,30},{25,31},{26,24}} | collective-permute-start | bytes 786440 | tf_op jit(solution)/shard_map/ppermute | solution.py:305
  8.6 1.3 %collective-permute-start.1 = (f32[256,256]{1,0:T(8,128)S(1)}, f32[256,256]{1,0:T(8,128)S(1)}, u32[]{:S(2)}, u32[]{:S(2)}) collective-permute-start(f32[256,256]{1,0:T(8,128)S(1)} %slice.12), channel_id=1, source_target_pairs={{0,4},{1,5},{10,14},{9,13},{16,20},{18,23},{24,28},{25,29},{26,30}} | collective-permute-start | bytes 786440 | tf_op jit(solution)/shard_map/ppermute | solution.py:305
  9.9 1.3 %collective-permute-start = (f32[256,256]{1,0:T(8,128)S(1)}, f32[256,256]{1,0:T(8,128)S(1)}, u32[]{:S(2)}, u32[]{:S(2)}) collective-permute-start(f32[256,256]{1,0:T(8,128)S(1)} %slice.12), channel_id=1, source_target_pairs={{0,2},{1,3},{10,12},{9,11},{16,18},{18,21},{24,26},{25,27},{26,28}} | collective-permute-start | bytes 786440 | tf_op jit(solution)/shard_map/ppermute | solution.py:305
  11.3 1.1 %slice.13.refs_0_ = f32[256,512]{1,0:T(8,128)S(1)} slice(f32[1024,512]{1,0:T(8,128)} %refs_5_), slice={[0:256], [0:512]} | slice | bytes 1048576 | tf_op jit(solution)/shard_map/slice | solution.py:338
  12.3 1.9 %collective-permute-start.4 = (f32[256,512]{1,0:T(8,128)S(1)}, f32[256,512]{1,0:T(8,128)S(1)}, u32[]{:S(2)}, u32[]{:S(2)}) collective-permute-start(f32[256,512]{1,0:T(8,128)S(1)} %slice.13.refs_0_), channel_id=1, source_target_pairs={{0,8},{1,9},{2,10},{3,11},{4,12},{5,13},{6,14},{7,15},{8,0},{9,1},... | collective-permute-start | bytes 1572872 | tf_op jit(solution)/shard_map/ppermute | solution.py:305
  14.3 2.1 %slice.14 = f32[768,256]{1,0:T(8,128)} slice(f32[1024,512]{1,0:T(8,128)} %refs_5_), slice={[256:1024], [0:256]} | slice | bytes 1572864 | tf_op jit(solution)/shard_map/slice | solution.py:347
  16.5 6.1 %collective-permute-start.8 = (f32[256,512]{1,0:T(8,128)S(1)}, f32[256,512]{1,0:T(8,128)S(1)}, u32[]{:S(2)}, u32[]{:S(2)}) collective-permute-start(f32[256,512]{1,0:T(8,128)S(1)} %slice.13.refs_0_), channel_id=1, source_target_pairs={{0,16},{1,17},{2,18},{3,19},{4,20},{5,21},{6,22},{7,23},{8,24},{9,... | collective-permute-start | bytes 1572872 | tf_op jit(solution)/shard_map/ppermute | solution.py:305
  22.6 2.8 %collective-permute-done = f32[256,256]{1,0:T(8,128)S(1)} collective-permute-done((f32[256,256]{1,0:T(8,128)S(1)}, f32[256,256]{1,0:T(8,128)S(1)}, u32[]{:S(2)}, u32[]{:S(2)}) %collective-permute-start) | collective-permute-done | bytes 262176 | tf_op jit(solution)/shard_map/ppermute | solution.py:305
  25.5 2.1 %collective-permute-done.4.refs_1_ = f32[256,512]{1,0:T(8,128)S(1)} collective-permute-done((f32[256,512]{1,0:T(8,128)S(1)}, f32[256,512]{1,0:T(8,128)S(1)}, u32[]{:S(2)}, u32[]{:S(2)}) %collective-permute-start.4) | collective-permute-done | bytes 524320 | tf_op jit(solution)/shard_map/ppermute | solution.py:305
  28.5 2.2 %collective-permute-start.13 = (f32[768,256]{1,0:T(8,128)}, f32[768,256]{1,0:T(8,128)}, u32[]{:S(2)}, u32[]{:S(2)}) collective-permute-start(f32[768,256]{1,0:T(8,128)} %slice.14), channel_id=1, source_target_pairs={{0,4},{1,5},{2,6},{8,12},{9,13},{10,14},{16,20},{17,21},{18,22},{2... | collective-permute-start | bytes 2359304 | tf_op jit(solution)/shard_map/ppermute | solution.py:305
  30.6 6.2 %collective-permute-start.7 = (f32[256,256]{1,0:T(8,128)S(1)}, f32[256,256]{1,0:T(8,128)S(1)}, u32[]{:S(2)}, u32[]{:S(2)}) collective-permute-start(f32[256,256]{1,0:T(8,128)S(1)} %get-tuple-element.38.refs_0_), channel_id=1, source_target_pairs={{0,24},{1,25},{2,26},{3,27},{4,28},{5,29},{6,30},{7,31},{8,16},{9,... | collective-permute-start | bytes 786440 | tf_op jit(solution)/shard_map/ppermute | solution.py:305
  36.9 1.9 %collective-permute-start.6 = (f32[256,256]{1,0:T(8,128)S(1)}, f32[256,256]{1,0:T(8,128)S(1)}, u32[]{:S(2)}, u32[]{:S(2)}) collective-permute-start(f32[256,256]{1,0:T(8,128)S(1)} %get-tuple-element.38.refs_0_), channel_id=1, source_target_pairs={{0,16},{1,17},{2,18},{3,19},{4,20},{5,21},{6,22},{7,23},{8,24},{9,... | collective-permute-start | bytes 786440 | tf_op jit(solution)/shard_map/ppermute | solution.py:305
  38.8 1.9 %collective-permute-start.5 = (f32[256,256]{1,0:T(8,128)S(1)}, f32[256,256]{1,0:T(8,128)S(1)}, u32[]{:S(2)}, u32[]{:S(2)}) collective-permute-start(f32[256,256]{1,0:T(8,128)S(1)} %get-tuple-element.38.refs_0_), channel_id=1, source_target_pairs={{0,8},{1,9},{2,10},{3,11},{4,12},{5,13},{6,14},{7,15},{8,0},{9,1},... | collective-permute-start | bytes 786440 | tf_op jit(solution)/shard_map/ppermute | solution.py:305
  42.4 2.7 %collective-permute-done.6.refs_2_ = f32[256,256]{1,0:T(8,128)S(1)} collective-permute-done((f32[256,256]{1,0:T(8,128)S(1)}, f32[256,256]{1,0:T(8,128)S(1)}, u32[]{:S(2)}, u32[]{:S(2)}) %collective-permute-start.6) | collective-permute-done | bytes 262176 | tf_op jit(solution)/shard_map/ppermute | solution.py:305
  45.1 1.9 %collective-permute-done.5.refs_1_ = f32[256,256]{1,0:T(8,128)S(1)} collective-permute-done((f32[256,256]{1,0:T(8,128)S(1)}, f32[256,256]{1,0:T(8,128)S(1)}, u32[]{:S(2)}, u32[]{:S(2)}) %collective-permute-start.5) | collective-permute-done | bytes 262176 | tf_op jit(solution)/shard_map/ppermute | solution.py:305
  49.7 4.9 %factor_head.2 = (f32[128,128]{1,0:T(8,128)S(1)}, f32[768,768]{1,0:T(8,128)S(1)}) custom-call(s32[2]{0:T(128)S(1)} %pad_add_fusion.place_ref, f32[256,256]{1,0:T(8,128)S(1)} %get-tuple-element.38.refs_0_, f32[256,256]{1,0:T(8,128)S(1)} %collective-permute-done.5.refs_1_, f32[256,256]{1,0:T(8,128)S(1)} %collective-permute-done.6.refs_2_, ...), custom_call_target="tpu_custom_call" | custom-call | flops 1000 | bytes 1000 | tf_op jit(solution)/shard_map/factor_head/pallas_call | solution.py:174
  54.7 1.2 %broadcast_select_fusion.refs_0_ = f32[768,256]{1,0:T(8,128)S(1)} fusion(f32[768,256]{1,0:T(8,128)} %collective-permute-done.13, f32[768,256]{1,0:T(8,128)} %slice.14, pred[]{:T(512)S(6)} %eq.60), kind=kLoop, calls=%fused_computation.1 | loop fusion | flops 196608 | bytes 2359297 | tf_op jit(solution)/shard_map/jit(_where)/select_n | solution.py:362
  55.9 3.5 %collective-permute-start.16 = (f32[768,256]{1,0:T(8,128)S(1)}, f32[768,256]{1,0:T(8,128)S(1)}, u32[]{:S(2)}, u32[]{:S(2)}) collective-permute-start(f32[768,256]{1,0:T(8,128)S(1)} %broadcast_select_fusion.refs_0_), channel_id=1, source_target_pairs={{0,2},{1,3},{2,0},{8,10},{9,11},{10,8},{16,18},{17,19},{18,16},{24... | collective-permute-start | bytes 2359304 | tf_op jit(solution)/shard_map/ppermute | solution.py:305
  59.6 2.9 %collective-permute-start.17 = (f32[256,512]{1,0:T(8,128)S(1)}, f32[256,512]{1,0:T(8,128)S(1)}, u32[]{:S(2)}, u32[]{:S(2)}) collective-permute-start(f32[256,512]{1,0:T(8,128)S(1)} %slice.15), channel_id=1, source_target_pairs={{0,24},{1,25},{2,26},{3,27},{4,28},{5,29},{6,30},{7,31},{8,16},{9,... | collective-permute-start | bytes 1572872 | tf_op jit(solution)/shard_map/ppermute | solution.py:305
  62.5 15.3 %factor_head.3 = (f32[3,256,256]{2,1,0:T(8,128)S(1)}, f32[768,768]{1,0:T(8,128)S(1)}) custom-call(s32[2]{0:T(128)S(1)} %pad_add_fusion.place_ref, f32[128,128]{1,0:T(8,128)S(1)} %get-tuple-element.42.refs_0_, f32[768,768]{1,0:T(8,128)S(1)} %get-tuple-element.48.refs_1_), custom_call_target="tpu_custom_call" | custom-call | flops 15000000512 | bytes 1000 | tf_op jit(solution)/shard_map/factor_head/pallas_call | solution.py:174
  77.8 1.2 %solve_across.2.refs_4_ = f32[256,512]{1,0:T(8,128)S(1)} custom-call(s32[2]{0:T(128)S(1)} %pad_add_fusion.place_ref, f32[3,256,256]{2,1,0:T(8,128)S(1)} %get-tuple-element.49.inverse_ref, f32[768,768]{1,0:T(8,128)S(1)} %get-tuple-element.50.head_ref, f32[256,512]{1,0:T(8,128)S(1)} %slice.13.refs_0_, f32[256,512]{1,0:T(8,128)S(1)} %copy-done.2, ...), custom_call_target="tpu_custom_call" | custom-call | flops 4000000000 | bytes 5000000 | tf_op jit(solution)/shard_map/solve_across/pallas_call | solution.py:212
  79.6 3.3 %solve_across.3.refs_4_ = f32[768,512]{1,0:T(8,128)S(1)} custom-call(s32[2]{0:T(128)S(1)} %pad_add_fusion.place_ref, f32[3,256,256]{2,1,0:T(8,128)S(1)} %get-tuple-element.49.inverse_ref, f32[768,768]{1,0:T(8,128)S(1)} %get-tuple-element.50.head_ref, f32[256,512]{1,0:T(8,128)S(1)} %slice.13.refs_0_, f32[256,512]{1,0:T(8,128)S(1)} %copy-done.2, ...), custom_call_target="tpu_custom_call" | custom-call | flops 4000000000 | bytes 5000000 | tf_op jit(solution)/shard_map/solve_across/pallas_call | solution.py:212
  83.0 14.3 %update.1 = f32[1024,512]{1,0:T(8,128)} custom-call(s32[2]{0:T(128)S(1)} %pad_add_fusion.place_ref, f32[3,256,256]{2,1,0:T(8,128)S(1)} %get-tuple-element.49.inverse_ref, f32[768,768]{1,0:T(8,128)S(1)} %get-tuple-element.50.head_ref, f32[2,256,256]{2,1,0:T(8,128)S(1)} %pad_maximum_fusion.top_ref, f32[2,256,256]{2,1,0:T(8,128)S(1)} %collective-permute-done.14.top_other_ref, ...), custom_call_target="tpu_custom_call" | custom-call | flops 10000000000 | bytes 10000000 | tf_op jit(solution)/shard_map/update/pallas_call | solution.py:284
  (37 shorter events, 6.7 us)
Async XLA Ops:
  1.0 15.5 %collective-permute-start.3 = (f32[256,256]{1,0:T(8,128)S(1)}, f32[256,256]{1,0:T(8,128)S(1)}, u32[]{:S(2)}, u32[]{:S(2)}) collective-permute-start(f32[256,256]{1,0:T(8,128)S(1)} %slice.12), channel_id=1, source_target_pairs={{18,19}} | collective-permute-start | bytes 786440 | tf_op jit(solution)/shard_map/ppermute | solution.py:305
  1.7 20.9 %collective-permute-start.2 = (f32[256,256]{1,0:T(8,128)S(1)}, f32[256,256]{1,0:T(8,128)S(1)}, u32[]{:S(2)}, u32[]{:S(2)}) collective-permute-start(f32[256,256]{1,0:T(8,128)S(1)} %slice.12), channel_id=1, source_target_pairs={{0,6},{1,7},{10,8},{9,15},{16,22},{18,17},{24,30},{25,31},{26,24}} | collective-permute-start | bytes 786440 | tf_op jit(solution)/shard_map/ppermute | solution.py:305
  8.6 14.0 %collective-permute-start.1 = (f32[256,256]{1,0:T(8,128)S(1)}, f32[256,256]{1,0:T(8,128)S(1)}, u32[]{:S(2)}, u32[]{:S(2)}) collective-permute-start(f32[256,256]{1,0:T(8,128)S(1)} %slice.12), channel_id=1, source_target_pairs={{0,4},{1,5},{10,14},{9,13},{16,20},{18,23},{24,28},{25,29},{26,30}} | collective-permute-start | bytes 786440 | tf_op jit(solution)/shard_map/ppermute | solution.py:305
  9.9 15.5 %collective-permute-start = (f32[256,256]{1,0:T(8,128)S(1)}, f32[256,256]{1,0:T(8,128)S(1)}, u32[]{:S(2)}, u32[]{:S(2)}) collective-permute-start(f32[256,256]{1,0:T(8,128)S(1)} %slice.12), channel_id=1, source_target_pairs={{0,2},{1,3},{10,12},{9,11},{16,18},{18,21},{24,26},{25,27},{26,28}} | collective-permute-start | bytes 786440 | tf_op jit(solution)/shard_map/ppermute | solution.py:305
  12.3 15.3 %collective-permute-start.4 = (f32[256,512]{1,0:T(8,128)S(1)}, f32[256,512]{1,0:T(8,128)S(1)}, u32[]{:S(2)}, u32[]{:S(2)}) collective-permute-start(f32[256,512]{1,0:T(8,128)S(1)} %slice.13.refs_0_), channel_id=1, source_target_pairs={{0,8},{1,9},{2,10},{3,11},{4,12},{5,13},{6,14},{7,15},{8,0},{9,1},... | collective-permute-start | bytes 1572872 | tf_op jit(solution)/shard_map/ppermute | solution.py:305
  16.5 24.3 %collective-permute-start.8 = (f32[256,512]{1,0:T(8,128)S(1)}, f32[256,512]{1,0:T(8,128)S(1)}, u32[]{:S(2)}, u32[]{:S(2)}) collective-permute-start(f32[256,512]{1,0:T(8,128)S(1)} %slice.13.refs_0_), channel_id=1, source_target_pairs={{0,16},{1,17},{2,18},{3,19},{4,20},{5,21},{6,22},{7,23},{8,24},{9,... | collective-permute-start | bytes 1572872 | tf_op jit(solution)/shard_map/ppermute | solution.py:305
  27.6 0.8 copy-start.1
  28.5 26.2 %collective-permute-start.13 = (f32[768,256]{1,0:T(8,128)}, f32[768,256]{1,0:T(8,128)}, u32[]{:S(2)}, u32[]{:S(2)}) collective-permute-start(f32[768,256]{1,0:T(8,128)} %slice.14), channel_id=1, source_target_pairs={{0,4},{1,5},{2,6},{8,12},{9,13},{10,14},{16,20},{17,21},{18,22},{2... | collective-permute-start | bytes 2359304 | tf_op jit(solution)/shard_map/ppermute | solution.py:305
  30.6 11.8 %collective-permute-start.7 = (f32[256,256]{1,0:T(8,128)S(1)}, f32[256,256]{1,0:T(8,128)S(1)}, u32[]{:S(2)}, u32[]{:S(2)}) collective-permute-start(f32[256,256]{1,0:T(8,128)S(1)} %get-tuple-element.38.refs_0_), channel_id=1, source_target_pairs={{0,24},{1,25},{2,26},{3,27},{4,28},{5,29},{6,30},{7,31},{8,16},{9,... | collective-permute-start | bytes 786440 | tf_op jit(solution)/shard_map/ppermute | solution.py:305
  36.9 8.3 %collective-permute-start.6 = (f32[256,256]{1,0:T(8,128)S(1)}, f32[256,256]{1,0:T(8,128)S(1)}, u32[]{:S(2)}, u32[]{:S(2)}) collective-permute-start(f32[256,256]{1,0:T(8,128)S(1)} %get-tuple-element.38.refs_0_), channel_id=1, source_target_pairs={{0,16},{1,17},{2,18},{3,19},{4,20},{5,21},{6,22},{7,23},{8,24},{9,... | collective-permute-start | bytes 786440 | tf_op jit(solution)/shard_map/ppermute | solution.py:305
  38.8 8.3 %collective-permute-start.5 = (f32[256,256]{1,0:T(8,128)S(1)}, f32[256,256]{1,0:T(8,128)S(1)}, u32[]{:S(2)}, u32[]{:S(2)}) collective-permute-start(f32[256,256]{1,0:T(8,128)S(1)} %get-tuple-element.38.refs_0_), channel_id=1, source_target_pairs={{0,8},{1,9},{2,10},{3,11},{4,12},{5,13},{6,14},{7,15},{8,0},{9,1},... | collective-permute-start | bytes 786440 | tf_op jit(solution)/shard_map/ppermute | solution.py:305
  40.8 0.8 copy-start.3
  47.1 1.5 %collective-permute-start.9 = (f32[256,256]{1,0:T(8,128)S(1)}, f32[256,256]{1,0:T(8,128)S(1)}, u32[]{:S(2)}, u32[]{:S(2)}) collective-permute-start(f32[256,256]{1,0:T(8,128)S(1)} %get-tuple-element.38.refs_0_), channel_id=1, source_target_pairs={{0,1},{1,0},{2,3},{3,2},{4,5},{5,4},{6,7},{7,6},{8,9},{9,8},{10,11... | collective-permute-start | bytes 786440 | tf_op jit(solution)/shard_map/ppermute | solution.py:305
  47.1 1.9 %collective-permute-start.10 = (f32[256,256]{1,0:T(8,128)S(1)}, f32[256,256]{1,0:T(8,128)S(1)}, u32[]{:S(2)}, u32[]{:S(2)}) collective-permute-start(f32[256,256]{1,0:T(8,128)S(1)} %collective-permute-done.5.refs_1_), channel_id=1, source_target_pairs={{0,1},{1,0},{2,3},{3,2},{4,5},{5,4},{6,7},{7,6},{8,9},{9,8},{10,11... | collective-permute-start | bytes 786440 | tf_op jit(solution)/shard_map/ppermute | solution.py:305
  47.6 1.8 %collective-permute-start.11 = (f32[256,256]{1,0:T(8,128)S(1)}, f32[256,256]{1,0:T(8,128)S(1)}, u32[]{:S(2)}, u32[]{:S(2)}) collective-permute-start(f32[256,256]{1,0:T(8,128)S(1)} %collective-permute-done.6.refs_2_), channel_id=1, source_target_pairs={{0,1},{1,0},{2,3},{3,2},{4,5},{5,4},{6,7},{7,6},{8,9},{9,8},{10,11... | collective-permute-start | bytes 786440 | tf_op jit(solution)/shard_map/ppermute | solution.py:305
  47.6 2.1 %collective-permute-start.12 = (f32[256,256]{1,0:T(8,128)S(1)}, f32[256,256]{1,0:T(8,128)S(1)}, u32[]{:S(2)}, u32[]{:S(2)}) collective-permute-start(f32[256,256]{1,0:T(8,128)S(1)} %collective-permute-done.7.refs_3_), channel_id=1, source_target_pairs={{0,1},{1,0},{2,3},{3,2},{4,5},{5,4},{6,7},{7,6},{8,9},{9,8},{10,11... | collective-permute-start | bytes 786440 | tf_op jit(solution)/shard_map/ppermute | solution.py:305
  48.1 11.4 %copy-start = (f32[1024,512]{1,0:T(8,128)S(1)}, f32[1024,512]{1,0:T(8,128)}, u32[]{:S(2)}) copy-start(f32[1024,512]{1,0:T(8,128)} %refs_5_) | copy-start | bytes 6291460
  55.9 23.1 %collective-permute-start.16 = (f32[768,256]{1,0:T(8,128)S(1)}, f32[768,256]{1,0:T(8,128)S(1)}, u32[]{:S(2)}, u32[]{:S(2)}) collective-permute-start(f32[768,256]{1,0:T(8,128)S(1)} %broadcast_select_fusion.refs_0_), channel_id=1, source_target_pairs={{0,2},{1,3},{2,0},{8,10},{9,11},{10,8},{16,18},{17,19},{18,16},{24... | collective-permute-start | bytes 2359304 | tf_op jit(solution)/shard_map/ppermute | solution.py:305
  59.5 23.5 %collective-permute-start.15 = (f32[768,256]{1,0:T(8,128)S(1)}, f32[768,256]{1,0:T(8,128)S(1)}, u32[]{:S(2)}, u32[]{:S(2)}) collective-permute-start(f32[768,256]{1,0:T(8,128)S(1)} %broadcast_select_fusion.refs_0_), channel_id=1, source_target_pairs={{0,1},{1,0},{2,3},{3,2},{4,5},{5,4},{6,7},{7,6},{8,9},{9,8},{10,11... | collective-permute-start | bytes 2359304 | tf_op jit(solution)/shard_map/ppermute | solution.py:305
  59.6 18.2 %collective-permute-start.17 = (f32[256,512]{1,0:T(8,128)S(1)}, f32[256,512]{1,0:T(8,128)S(1)}, u32[]{:S(2)}, u32[]{:S(2)}) collective-permute-start(f32[256,512]{1,0:T(8,128)S(1)} %slice.15), channel_id=1, source_target_pairs={{0,24},{1,25},{2,26},{3,27},{4,28},{5,29},{6,30},{7,31},{8,16},{9,... | collective-permute-start | bytes 1572872 | tf_op jit(solution)/shard_map/ppermute | solution.py:305
  62.5 15.3 %copy-start.2 = (f32[256,512]{1,0:T(8,128)S(1)}, f32[256,512]{1,0:T(8,128)}, u32[]{:S(2)}) copy-start(f32[256,512]{1,0:T(8,128)} %copy-done.1) | copy-start | bytes 1572868
  62.5 15.3 %copy-start.4 = (f32[256,512]{1,0:T(8,128)S(1)}, f32[256,512]{1,0:T(8,128)}, u32[]{:S(2)}) copy-start(f32[256,512]{1,0:T(8,128)} %copy-done.3) | copy-start | bytes 1572868
  79.1 3.9 %collective-permute-start.18 = (f32[768,256]{1,0:T(8,128)S(1)}, f32[768,256]{1,0:T(8,128)S(1)}, u32[]{:S(2)}, u32[]{:S(2)}) collective-permute-start(f32[768,256]{1,0:T(8,128)S(1)} %collective-permute-done.16.refs_2_), channel_id=1, source_target_pairs={{0,1},{1,0},{2,3},{3,2},{4,5},{5,4},{6,7},{7,6},{8,9},{9,8},{10,11... | collective-permute-start | bytes 2359304 | tf_op jit(solution)/shard_map/ppermute | solution.py:305
  79.3 3.6 %collective-permute-start.14 = (f32[2,256,256]{2,1,0:T(8,128)S(1)}, f32[2,256,256]{2,1,0:T(8,128)S(1)}, u32[]{:S(2)}, u32[]{:S(2)}) collective-permute-start(f32[2,256,256]{2,1,0:T(8,128)S(1)} %pad_maximum_fusion.top_ref), channel_id=1, source_target_pairs={{0,1},{1,0},{2,3},{3,2},{4,5},{5,4},{6,7},{7,6},{8,9},{9,8},{10,11... | collective-permute-start | bytes 1572872 | tf_op jit(solution)/shard_map/ppermute | solution.py:305
